TPU v7x, 128 devices: a whole 4x4x4 slice. The times are simulated.
128 devices in a mesh: dp: 16 (over y, z_hi, core), tensor: 8 (over z_lo, x).
Axes of the slice: x: 4, y: 4, z: 4 (z_hi: 2, z_lo: 2; z = z_hi * 2 + z_lo), core: 2. Of those that a mesh axis runs over, the one named last changes fastest.
Arguments:
- tokens: bfloat16 [16384, 2048], P(('dp', 'tensor')), may hold values from -6 to 6
- segment: int32 [16384], P('dp'), may hold values from -1024 to 2, as said below
- ln_gain: bfloat16 [2048], replicated, may hold values from 0.099609375 to 1.8984375
- ln_bias: bfloat16 [2048], replicated, may hold values from -3 to 3
- w_qkv: bfloat16 [2048, 3, 2048], P(None, None, 'tensor'), may hold values from -0.125 to 0.125
- b_qkv: bfloat16 [3, 2048], P(None, 'tensor'), may hold values from -3 to 3
- w_out: bfloat16 [2048, 2048], P('tensor'), may hold values from -0.5 to 0.5
- b_out: bfloat16 [2048], replicated, may hold values from -1.75 to 1.75
- w_up: bfloat16 [2048, 8192], P(None, 'tensor'), may hold values from -0.125 to 0.125
- b_up: bfloat16 [8192], P('tensor'), may hold values from -3 to 3
- w_down: bfloat16 [8192, 2048], P('tensor'), may hold values from -0.0625 to 0.0625
- b_down: bfloat16 [2048], replicated, may hold values from -1.75 to 1.75
- cotangent: bfloat16 [16384, 2048], P(('dp', 'tensor')), may hold values from -6 to 6
Outputs:
- output: bfloat16 [16384, 2048], P(('dp', 'tensor'))
- input_grad: bfloat16 [16384, 2048], P(('dp', 'tensor'))
- grad_ln_gain: float32 [2048], replicated
- grad_ln_bias: float32 [2048], replicated
- grad_w_qkv: float32 [2048, 3, 2048], P(None, None, 'tensor')
- grad_b_qkv: float32 [3, 2048], P(None, 'tensor')
- grad_w_out: float32 [2048, 2048], P('tensor')
- grad_b_out: float32 [2048], replicated
- grad_w_up: float32 [2048, 8192], P(None, 'tensor')
- grad_b_up: float32 [8192], P('tensor')
- grad_w_down: float32 [8192, 2048], P('tensor')
- grad_b_down: float32 [2048], replicated
Inputs may be any that keep to these rules, and one draw needn't show every extreme that they name: `segment`: within each group the slots of each device that hold tokens come first and the rest of its 128 slots are padding, with distinct negative ids, the slot at index k of the group having id -(k + 1); the last slot of every group is padding; the tokens of a group form three whole sequences with ids 0, 1, 2 in order, the first lying within the group's first device and the last within its last device.
All inputs are finite; a program needn't handle non-finite values.
Results may differ from a plain program's by a relative error of at most 0.012.
The roundings to bfloat16 on the way count: a program that leaves them out, or rounds other values in their place, can miss the bound.
Values may be sent and summed in bfloat16 or wider, within the bound.
A program may use at most 192 MiB of HBM per device.

v0:
```python
import jax
import jax.numpy as jnp
from jax import lax
from jax.sharding import PartitionSpec as P

HEAD_DIM = 64
ROT = 32


EPSILON = 1e-05


def positions_of(segment):
    is_valid = segment >= 0
    valid_rank = jnp.cumsum(is_valid.astype(jnp.int32)) - 1
    seen = lax.cummax(jnp.where(is_valid, segment, -1), axis=0)
    before = jnp.concatenate([jnp.full((1,), -1, jnp.int32), seen[:-1]])
    starts = is_valid & (segment > before)
    start_rank = lax.cummax(jnp.where(starts, valid_rank, -1), axis=0)
    return jnp.where(is_valid, valid_rank - start_rank, 0)


def rotary_tables(position):
    exponent = jnp.arange(ROT // 2, dtype=jnp.float32) * (2.0 / ROT)
    inverse = jnp.power(10000.0, -exponent)
    angle = position.astype(jnp.float32)[:, None] * inverse[None, :]
    return (jnp.cos(angle)[:, None, :], jnp.sin(angle)[:, None, :])


def rotate(vectors, cosine_table, sine_table):
    half_rot = ROT // 2
    first_part = vectors[..., :half_rot]
    second_part = vectors[..., half_rot:ROT]
    return jnp.concatenate(
        [
            first_part * cosine_table - second_part * sine_table,
            second_part * cosine_table + first_part * sine_table,
            vectors[..., ROT:],
        ],
        axis=-1,
    )


def unrotate(grads_in, cosine_table, sine_table):
    half_rot = ROT // 2
    first_part = grads_in[..., :half_rot]
    second_part = grads_in[..., half_rot:ROT]
    return jnp.concatenate(
        [
            first_part * cosine_table + second_part * sine_table,
            second_part * cosine_table - first_part * sine_table,
            grads_in[..., ROT:],
        ],
        axis=-1,
    )


def block_scores(queries, key_rows, segment, begin_row, end_row):
    scale = HEAD_DIM ** (-0.5)
    scores = (
        jnp.einsum(
            "ihd,jhd->hij",
            queries[begin_row:end_row],
            key_rows[:end_row],
            preferred_element_type=jnp.float32,
        )
        * scale
    )
    position = jnp.arange(end_row, dtype=jnp.int32)
    allowed = (segment[begin_row:end_row, None] == segment[None, :end_row]) & (
        position[begin_row:end_row, None] >= position[None, :]
    )
    return (scores, allowed[None])


def attend_forward(queries, key_rows, value_rows, segment):
    group_rows = queries.shape[0]
    block_rows = min(512, group_rows)
    out_blocks = []
    lse_blocks = []
    for begin_row in range(0, group_rows, block_rows):
        end_row = begin_row + block_rows
        scores, allowed = block_scores(queries, key_rows, segment, begin_row, end_row)
        scores = jnp.where(allowed, scores, -1e30)
        row_max = jnp.max(scores, axis=2, keepdims=True)
        exponent = jnp.exp(scores - row_max)
        row_total = jnp.sum(exponent, axis=2, keepdims=True)
        probs = (exponent / row_total).astype(jnp.bfloat16)
        out_blocks.append(
            jnp.einsum(
                "hij,jhd->ihd", probs, value_rows[:end_row], preferred_element_type=jnp.float32
            )
        )
        lse_blocks.append(row_max + jnp.log(row_total))
    return (jnp.concatenate(out_blocks, axis=0), jnp.concatenate(lse_blocks, axis=1))


def attend_backward(queries, key_rows, value_rows, segment, lse_all, grad_heads):
    group_rows = queries.shape[0]
    block_rows = min(512, group_rows)
    scale = HEAD_DIM ** (-0.5)
    grad_keys = jnp.zeros(key_rows.shape, jnp.float32)
    grad_values = jnp.zeros(value_rows.shape, jnp.float32)
    query_blocks = []
    for begin_row in range(0, group_rows, block_rows):
        end_row = begin_row + block_rows
        scores, allowed = block_scores(queries, key_rows, segment, begin_row, end_row)
        probs_exact = jnp.where(allowed, jnp.exp(scores - lse_all[:, begin_row:end_row]), 0.0)
        grad_block = grad_heads[begin_row:end_row]
        grad_probs = jnp.einsum(
            "ihd,jhd->hij", grad_block, value_rows[:end_row], preferred_element_type=jnp.float32
        )
        delta = jnp.sum(probs_exact * grad_probs, axis=2, keepdims=True)
        grad_scores = (probs_exact * (grad_probs - delta)).astype(jnp.bfloat16)
        query_blocks.append(
            jnp.einsum(
                "hij,jhd->ihd", grad_scores, key_rows[:end_row], preferred_element_type=jnp.float32
            )
            * scale
        )
        grad_keys = grad_keys.at[:end_row].add(
            jnp.einsum(
                "hij,ihd->jhd",
                grad_scores,
                queries[begin_row:end_row],
                preferred_element_type=jnp.float32,
            )
            * scale
        )
        grad_values = grad_values.at[:end_row].add(
            jnp.einsum(
                "hij,ihd->jhd",
                probs_exact.astype(jnp.bfloat16),
                grad_block,
                preferred_element_type=jnp.float32,
            )
        )
    return (jnp.concatenate(query_blocks, axis=0), grad_keys, grad_values)


def gelu_tanh(values_in):
    return jax.nn.gelu(values_in, approximate=True)


def on_device(
    tokens,
    segment,
    ln_gain,
    ln_bias,
    w_qkv,
    b_qkv,
    w_out,
    b_out,
    w_up,
    b_up,
    w_down,
    b_down,
    cotangent,
):
    inputs = tokens.astype(jnp.float32)
    centered = inputs - jnp.mean(inputs, axis=1, keepdims=True)
    rstd_rows = lax.rsqrt(jnp.mean(centered * centered, axis=1, keepdims=True) + EPSILON)
    unit_rows = centered * rstd_rows
    gain_float = ln_gain.astype(jnp.float32)
    normed = (unit_rows * gain_float + ln_bias.astype(jnp.float32)).astype(jnp.bfloat16)
    gathered = lax.all_gather(normed, "tensor", axis=0, tiled=True)
    group_rows = gathered.shape[0]
    local_width = w_qkv.shape[2]
    local_heads = local_width // HEAD_DIM
    cosine_table, sine_table = rotary_tables(positions_of(segment))
    qkv_pre = jnp.einsum(
        "td,dcf->tcf", gathered, w_qkv, preferred_element_type=jnp.float32
    ) + b_qkv.astype(jnp.float32)
    shaped = qkv_pre.reshape(group_rows, 3, local_heads, HEAD_DIM)
    queries = rotate(shaped[:, 0], cosine_table, sine_table).astype(jnp.bfloat16)
    key_rows = rotate(shaped[:, 1], cosine_table, sine_table).astype(jnp.bfloat16)
    value_rows = shaped[:, 2].astype(jnp.bfloat16)
    up_pre = jnp.dot(gathered, w_up, preferred_element_type=jnp.float32) + b_up.astype(jnp.float32)
    activated = gelu_tanh(up_pre).astype(jnp.bfloat16)
    attended, lse_all = attend_forward(queries, key_rows, value_rows, segment)
    heads_out = attended.reshape(group_rows, local_width).astype(jnp.bfloat16)
    branches = lax.psum_scatter(
        jnp.dot(heads_out, w_out, preferred_element_type=jnp.float32)
        + jnp.dot(activated, w_down, preferred_element_type=jnp.float32),
        "tensor",
        scatter_dimension=0,
        tiled=True,
    )
    output = (inputs + branches + b_out.astype(jnp.float32) + b_down.astype(jnp.float32)).astype(
        jnp.bfloat16
    )
    grad_rows = lax.all_gather(cotangent, "tensor", axis=0, tiled=True)
    bias_total = jnp.sum(grad_rows, axis=0, dtype=jnp.float32)
    grad_w_out = jnp.einsum("tf,td->fd", heads_out, grad_rows, preferred_element_type=jnp.float32)
    grad_w_down = jnp.einsum("tf,td->fd", activated, grad_rows, preferred_element_type=jnp.float32)
    grad_heads = jnp.einsum(
        "td,fd->tf", grad_rows, w_out, preferred_element_type=jnp.float32
    ).astype(jnp.bfloat16)
    grad_act = jnp.einsum("td,fd->tf", grad_rows, w_down, preferred_element_type=jnp.float32)
    gelu_pullback = jax.vjp(gelu_tanh, up_pre)[1]
    grad_up = gelu_pullback(grad_act)[0].astype(jnp.bfloat16)
    grad_w_up = jnp.einsum("td,tf->df", gathered, grad_up, preferred_element_type=jnp.float32)
    grad_b_up = jnp.sum(grad_up, axis=0, dtype=jnp.float32)
    grad_queries, grad_keys, grad_values = attend_backward(
        queries,
        key_rows,
        value_rows,
        segment,
        lse_all,
        grad_heads.reshape(group_rows, local_heads, HEAD_DIM),
    )
    grad_qkv = (
        jnp.stack(
            [
                unrotate(grad_queries, cosine_table, sine_table),
                unrotate(grad_keys, cosine_table, sine_table),
                grad_values,
            ],
            axis=1,
        )
        .reshape(group_rows, 3, local_width)
        .astype(jnp.bfloat16)
    )
    grad_w_qkv = jnp.einsum("td,tcf->dcf", gathered, grad_qkv, preferred_element_type=jnp.float32)
    grad_b_qkv = jnp.sum(grad_qkv, axis=0, dtype=jnp.float32)
    grad_normed = lax.psum_scatter(
        jnp.einsum("tf,df->td", grad_up, w_up, preferred_element_type=jnp.float32)
        + jnp.einsum("tcf,dcf->td", grad_qkv, w_qkv, preferred_element_type=jnp.float32),
        "tensor",
        scatter_dimension=0,
        tiled=True,
    )
    scaled = grad_normed * gain_float
    mean_plain = jnp.mean(scaled, axis=1, keepdims=True)
    mean_unit = jnp.mean(scaled * unit_rows, axis=1, keepdims=True)
    input_grad = (
        cotangent.astype(jnp.float32) + rstd_rows * (scaled - mean_plain - unit_rows * mean_unit)
    ).astype(jnp.bfloat16)
    gain_part = jnp.sum(grad_normed * unit_rows, axis=0)
    shift_part = jnp.sum(grad_normed, axis=0)
    grad_ln_gain, grad_ln_bias = lax.psum((gain_part, shift_part), ("dp", "tensor"))
    grad_w_out, grad_w_down, bias_total, grad_w_up, grad_b_up, grad_w_qkv, grad_b_qkv = lax.psum(
        (grad_w_out, grad_w_down, bias_total, grad_w_up, grad_b_up, grad_w_qkv, grad_b_qkv), "dp"
    )
    return (
        output,
        input_grad,
        grad_ln_gain,
        grad_ln_bias,
        grad_w_qkv,
        grad_b_qkv,
        grad_w_out,
        bias_total,
        grad_w_up,
        grad_b_up,
        grad_w_down,
        bias_total,
    )


def solution(mesh):
    placed = (
        P(("dp", "tensor"), None),
        P("dp"),
        P(),
        P(),
        P(None, None, "tensor"),
        P(None, "tensor"),
        P("tensor", None),
        P(),
        P(None, "tensor"),
        P("tensor"),
        P("tensor", None),
        P(),
        P(("dp", "tensor"), None),
    )
    return jax.shard_map(
        on_device,
        mesh=mesh,
        in_specs=placed,
        out_specs=(
            P(("dp", "tensor"), None),
            P(("dp", "tensor"), None),
            P(),
            P(),
            P(None, None, "tensor"),
            P(None, "tensor"),
            P("tensor", None),
            P(),
            P(None, "tensor"),
            P("tensor"),
            P("tensor", None),
            P(),
        ),
        check_vma=False,
    )
```

profile of v0, /device:TPU:1, one launch (start us, length us, event | category | flops | bytes accessed | tf_op | source)
XLA Modules:
  0.0 968.4 jit_solution(329537424231629454)
XLA Ops:
  24.7 40.8 %all-gather.5.cloned.1.call-done = bf16[1024,2048]{1,0:T(8,128)(2,1)} async-done(((bf16[128,2048]{1,0:T(8,128)(2,1)}), bf16[1024,2048]{1,0:T(8,128)(2,1)}) %all-gather.5.cloned.1.call-update) | async-done | bytes 4194320 | tf_op jit(solution)/shard_map/all_gather | solution.py:192
  65.5 3.8 convolution_convert_fusion
  70.1 49.0 %all-gather.3.cloned.1.call-done = bf16[1024,2048]{1,0:T(8,128)(2,1)} async-done(((bf16[128,2048]{1,0:T(8,128)(2,1)}), bf16[1024,2048]{1,0:T(8,128)(2,1)}) %all-gather.3.cloned.1.call-update) | async-done | bytes 4194320 | tf_op jit(solution)/shard_map/all_gather | solution.py:166
  119.2 5.4 fusion.24
  137.0 3.2 multiply_reduce_fusion
  147.9 6.0 fusion.97
  153.9 9.5 convert_reduce_fusion.1
  163.4 6.9 fusion.98
  181.6 8.3 bitcast_add_fusion
  191.3 3.5 fusion.52
  194.8 5.6 fusion.53
  201.5 4.9 fusion.93
  206.5 4.7 convolution_add_fusion
  211.3 4.9 fusion.99
  216.3 5.7 fusion.9
  222.0 6.8 fusion.100
  228.8 7.4 fusion.92
  237.2 2.9 convert_reduce_fusion
  240.1 151.6 %all-reduce.3 = (f32[3,256]{1,0:T(4,128)}, f32[2048]{0:T(1024)S(1)}, f32[1024]{0:T(1024)}) all-reduce(f32[3,256]{1,0:T(4,128)S(1)} %convert_reduce_fusion.2, f32[2048]{0:T(1024)S(1)} %convert_reduce_fusion, f32[1024]{0:T(1024)S(1)} %copy-done.36), channel_id=1, replica_groups=mesh['dp'=16,'tensor'=8] {'dp'}, use_global_device_ids=true, to_apply=%region_24.25 | all-reduce | flops 3840 | bytes 30720 | tf_op jit(solution)/shard_map/psum | solution.py:242
  393.4 545.7 %all-reduce.2 = (f32[2048]{0:T(1024)}, f32[2048]{0:T(1024)}) all-reduce(f32[2048]{0:T(1024)S(1)} %get-tuple-element.76, f32[2048]{0:T(1024)S(1)} %get-tuple-element.79), channel_id=1, replica_groups=mesh['dp'=16,'tensor'=8] {'dp','tensor'}, use_global_device_ids=true, to_apply=%region_19.20 | all-reduce | flops 4096 | bytes 32768 | tf_op jit(solution)/shard_map/psum | solution.py:241
  939.2 3.2 fusion.60
  943.0 6.6 copy.56
  951.8 4.3 copy.58
  957.4 3.9 copy.59
  (181 shorter events, 59.1 us)
Async XLA Ops:
  7.2 112.0 %copy-start = (bf16[2048,3,256]{2,0,1:T(8,128)(2,1)S(1)}, bf16[2048,3,256]{2,0,1:T(8,128)(2,1)}, u32[]{:S(2)}) copy-start(bf16[2048,3,256]{2,0,1:T(8,128)(2,1)} %param.29) | copy-start | bytes 9437188
  7.2 58.3 %all-gather.5.cloned.1.call-start = ((), (), s32[]{:S(2)}) async-start(), calls=%async_computation.4 | async-start | bytes 4718592 | tf_op jit(solution)/shard_map/all_gather | solution.py:192
  7.9 111.2 %all-gather.3.cloned.1.call-start = ((), (), s32[]{:S(2)}) async-start(), calls=%async_computation.2 | async-start | bytes 4718592 | tf_op jit(solution)/shard_map/all_gather | solution.py:166
  14.9 376.8 %reduce-scatter.5.cloned.1.call-start = ((), (), s32[]{:S(2)}) async-start(), calls=%async_computation.5 | async-start | bytes 9437184 | tf_op jit(solution)/shard_map/reduce_scatter | solution.py:226
  124.9 12.1 %copy-start.10 = (bf16[1024,3,4,64]{0,3,2,1:T(8,128)(2,1)}, bf16[1024,3,4,64]{0,3,2,1:T(8,128)(2,1)S(1)}, u32[]{:S(2)}) copy-start(bf16[1024,3,4,64]{0,3,2,1:T(8,128)(2,1)S(1)} %bitcast_convert_fusion) | copy-start | bytes 4718596
  134.0 36.3 %copy-start.2 = (f32[4,512,1024]{2,1,0:T(8,128)}, f32[4,512,1024]{2,1,0:T(8,128)S(1)}, u32[]{:S(2)}) copy-start(f32[4,512,1024]{2,1,0:T(8,128)S(1)} %get-tuple-element.114) | copy-start | bytes 25165828
  147.9 6.0 copy-start.8
  147.9 6.0 copy-start.34
  147.9 6.0 copy-start.38
  163.4 6.9 copy-start.44
  190.0 749.2 %reduce-scatter.3.cloned.1.call-start = ((), (), s32[]{:S(2)}) async-start(), calls=%async_computation.3 | async-start | bytes 9437184 | tf_op jit(solution)/shard_map/reduce_scatter | solution.py:182
  194.8 6.7 copy-start.42
  211.3 731.1 %all-reduce.7.cloned.1.call-start = ((), (), s32[]{:S(2)}) async-start(), calls=%async_computation.6 | async-start | bytes 50331648 | tf_op jit(solution)/shard_map/psum | solution.py:242
  222.0 6.9 copy-start.9
  222.0 6.9 copy-start.43
  236.9 154.8 %copy-start.4 = (bf16[128,2048]{1,0:T(8,128)(2,1)S(1)}, bf16[128,2048]{1,0:T(8,128)(2,1)}, u32[]{:S(2)}) copy-start(bf16[128,2048]{1,0:T(8,128)(2,1)} %param.25) | copy-start | bytes 1572868
  236.9 154.8 %copy-start.22 = (f32[2048]{0:T(1024)S(1)}, f32[2048]{0:T(1024)}, u32[]{:S(2)}) copy-start(f32[2048]{0:T(1024)} %copy-done.21) | copy-start | bytes 24580
  236.9 154.8 %copy-start.29 = (f32[128]{0:T(128)S(1)}, f32[128]{0:T(128)}, u32[]{:S(2)}) copy-start(f32[128]{0:T(128)} %copy-done.28) | copy-start | bytes 1540
  236.9 154.8 %copy-start.31 = (f32[128]{0:T(128)S(1)}, f32[128]{0:T(128)}, u32[]{:S(2)}) copy-start(f32[128]{0:T(128)} %copy-done.30) | copy-start | bytes 1540
  236.9 702.2 %copy-start.16 = (bf16[128,2048]{1,0:T(8,128)(2,1)S(1)}, bf16[128,2048]{1,0:T(8,128)(2,1)}, u32[]{:S(2)}) copy-start(bf16[128,2048]{1,0:T(8,128)(2,1)} %param.37) | copy-start | bytes 1572868
  391.7 557.9 %copy-start.27 = (f32[2048]{0:T(1024)}, f32[2048]{0:T(1024)S(1)}, u32[]{:S(2)}) copy-start(f32[2048]{0:T(1024)S(1)} %get-tuple-element.154) | copy-start | bytes 24580
  943.0 6.6 copy-start.15
  943.0 8.9 copy-start.7
  949.6 6.6 slice-start
  (29 other events, 104.6 us)
Sparse Core Ops, SparseCore 0:
  9.7 55.8 all-gather.4
  67.7 51.3 all-gather.2
  190.0 91.7 reduce-scatter.4
  284.7 91.4 reduce-scatter.2
  379.4 536.5 all-reduce.6
where the time goes:
time: 973 us; the launch traced here: 968 us
  blocking collectives  697 us (72%)
  matrix products  98.3 us (10%)
  waiting for transfers between devices  90.6 us (9%)
  other arithmetic  34.6 us (4%)
  local copies, waits for them, and re-layouts  32.8 us (3%)
  between operations  14.6 us (2%)
    psum x1, blocking collectives, on_device(): lax.psum((gain_part, shift_part), ('dp', 'tensor'))  546 us
    psum x1, blocking collectives, on_device(): lax.psum((grad_w_out, grad_w_down, bias_total, grad_w_up, grad_b_up, grad...  152 us
    all_gather x1, waiting for transfers between devices, on_device(): gathered = lax.all_gather(normed, 'tensor', axis=0, tiled=True)  49 us
    all_gather x1, waiting for transfers between devices, on_device(): grad_rows = lax.all_gather(cotangent, 'tensor', axis=0, tiled=True)  40.8 us
    unnamed x101, local copies, waits for them, and re-layouts  23.5 us
  transfers between devices with their start and end apart: 5, of which 2 were waited for; matrix products, arithmetic and copies ran while one was open for 7% of the time, Pallas kernels for 0%

commit v1 on v0

--- a/solution.py
+++ b/solution.py
@@ -1,13 +1,228 @@
 import jax
 import jax.numpy as jnp
 from jax import lax
+from jax.experimental import pallas as pl
+from jax.experimental.pallas import tpu as pltpu
 from jax.sharding import PartitionSpec as P
 
 HEAD_DIM = 64
 ROT = 32
-
-
 EPSILON = 1e-05
+MESH = pl.DeviceIdType.MESH
+BF = jnp.bfloat16
+F32 = jnp.float32
+NP = 24
+DP_STAGES = 8
+
+
+def neighbours():
+    dp = lax.axis_index("dp")
+    tensor = lax.axis_index("tensor")
+    y, zh, core = dp // 4, (dp // 2) % 2, dp % 2
+    zl, x = tensor // 4, tensor % 4
+    yl, yr, yo = (y + 3) % 4, (y + 1) % 4, (y + 2) % 4
+    xl, xr, xo = (x + 3) % 4, (x + 1) % 4, (x + 2) % 4
+    where = dict(y=y, core=core, zl=zl, x=x, yl=yl, yr=yr, yo=yo, xl=xl, xr=xr, xo=xo)
+    where["dev_yl"] = (yl * 4 + zh * 2 + core, tensor)
+    where["dev_yr"] = (yr * 4 + zh * 2 + core, tensor)
+    where["dev_zh"] = (y * 4 + (1 - zh) * 2 + core, tensor)
+    where["dev_core"] = (y * 4 + zh * 2 + 1 - core, tensor)
+    where["dev_xl"] = (dp, zl * 4 + xl)
+    where["dev_xr"] = (dp, zl * 4 + xr)
+    where["dev_zl"] = (dp, (1 - zl) * 4 + x)
+    return where
+
+
+def greet(devices):
+    barrier = pltpu.get_barrier_semaphore()
+    for device in devices:
+        pl.semaphore_signal(barrier, inc=1, device_id=device, device_id_type=MESH)
+    pl.semaphore_wait(barrier, len(devices))
+
+
+def rcopy(src, dst, send, recv, device):
+    return pltpu.make_async_remote_copy(
+        src_ref=src, dst_ref=dst, send_sem=send, recv_sem=recv, device_id=device, device_id_type=MESH
+    )
+
+
+def rows_at(index, size, count=None):
+    return pl.ds(pl.multiple_of(index * size, size), size if count is None else count)
+
+
+class GradSum:
+    def scratch():
+        return [
+            pltpu.VMEM((2, 1024, 256), BF),
+            pltpu.VMEM((4, 512, 256), BF),
+            pltpu.VMEM((4, 512, 256), BF),
+            pltpu.VMEM((4, 2, 64, 256), BF),
+            pltpu.VMEM((4, 2, 128, 256), BF),
+            pltpu.VMEM((4, 128, 256), BF),
+            pltpu.VMEM((4, 128, 256), BF),
+            pltpu.VMEM((4, 128, 256), BF),
+            pltpu.SemaphoreType.DMA((11, 4)),
+            pltpu.SemaphoreType.DMA((11, 4)),
+            pltpu.SemaphoreType.DMA((4,)),
+        ]
+
+    def __init__(self, at, out, scratch):
+        self.at, self.out = at, out
+        (self.own, self.other, self.half, self.r1, self.r2, self.zs, self.zr, self.full,
+         self.send, self.recv, self.local) = scratch
+
+    def core_copy(self, p):
+        s, at = p % 4, self.at
+        return rcopy(self.own.at[p % 2, rows_at(1 - at["core"], 512)], self.other.at[s],
+                     self.send.at[0, s], self.recv.at[0, s], at["dev_core"])
+
+    def first_copies(self, p):
+        s, at = p % 4, self.at
+        top = self.half.at[s, rows_at(at["yo"], 128, 64)]
+        low = self.half.at[s, pl.ds(pl.multiple_of(at["yo"] * 128 + 64, 64), 64)]
+        return (rcopy(top, self.r1.at[s, 0], self.send.at[1, s], self.recv.at[1, s], at["dev_yr"]),
+                rcopy(low, self.r1.at[s, 1], self.send.at[2, s], self.recv.at[2, s], at["dev_yl"]))
+
+    def second_copies(self, p):
+        s, at = p % 4, self.at
+        return (rcopy(self.half.at[s, rows_at(at["yr"], 128)], self.r2.at[s, 0],
+                      self.send.at[3, s], self.recv.at[3, s], at["dev_yr"]),
+                rcopy(self.half.at[s, rows_at(at["yl"], 128)], self.r2.at[s, 1],
+                      self.send.at[4, s], self.recv.at[4, s], at["dev_yl"]))
+
+    def z_copy(self, p):
+        s = p % 4
+        return rcopy(self.zs.at[s], self.zr.at[s], self.send.at[5, s], self.recv.at[5, s],
+                     self.at["dev_zh"])
+
+    def back_first(self, p):
+        s, at = p % 4, self.at
+        mine = self.out.at[p, rows_at(at["core"] * 4 + at["y"], 128)]
+        return (rcopy(self.full.at[s], mine, self.send.at[6, s], self.recv.at[6, s], at["dev_yr"]),
+                rcopy(self.full.at[s], mine, self.send.at[7, s], self.recv.at[7, s], at["dev_yl"]),
+                pltpu.make_async_copy(self.full.at[s], mine, self.local.at[s]))
+
+    def back_second(self, p):
+        s, at = p % 4, self.at
+        top = self.out.at[p, rows_at(at["core"] * 4 + at["yl"], 128, 64)]
+        low = self.out.at[p, pl.ds(pl.multiple_of((at["core"] * 4 + at["yr"]) * 128 + 64, 64), 64)]
+        return (rcopy(top, top, self.send.at[9, s], self.recv.at[9, s], at["dev_yr"]),
+                rcopy(low, low, self.send.at[10, s], self.recv.at[10, s], at["dev_yl"]))
+
+    def back_core(self, p):
+        s, at = p % 4, self.at
+        mine = self.out.at[p, rows_at(at["core"], 512)]
+        return rcopy(mine, mine, self.send.at[8, s], self.recv.at[8, s], at["dev_core"])
+
+    def send_piece(self, p):
+        self.core_copy(p).start()
+
+    def add_core(self, p):
+        s = p % 4
+        self.core_copy(p).wait()
+
+        @pl.loop(0, 4)
+        def _(j):
+            rows = rows_at(j, 128)
+            mine = self.own[p % 2, pl.ds(pl.multiple_of(self.at["core"] * 512 + j * 128, 128), 128)]
+            self.half[s, rows] = (mine.astype(F32) + self.other[s, rows].astype(F32)).astype(BF)
+
+        for copy in self.first_copies(p):
+            copy.start()
+
+    def add_first(self, p):
+        s, at = p % 4, self.at
+        for copy in self.first_copies(p):
+            copy.wait()
+        top = rows_at(at["yr"], 128, 64)
+        low = pl.ds(pl.multiple_of(at["yl"] * 128 + 64, 64), 64)
+        self.half[s, top] = (self.half[s, top].astype(F32) + self.r1[s, 0].astype(F32)).astype(BF)
+        self.half[s, low] = (self.half[s, low].astype(F32) + self.r1[s, 1].astype(F32)).astype(BF)
+        for copy in self.second_copies(p):
+            copy.start()
+
+    def add_second(self, p):
+        s = p % 4
+        for copy in self.second_copies(p):
+            copy.wait()
+        mine = self.half[s, rows_at(self.at["y"], 128)].astype(F32)
+        self.zs[s] = (mine + self.r2[s, 0].astype(F32) + self.r2[s, 1].astype(F32)).astype(BF)
+        self.z_copy(p).start()
+
+    def add_z(self, p):
+        s = p % 4
+        self.z_copy(p).wait()
+        self.full[s] = (self.zs[s].astype(F32) + self.zr[s].astype(F32)).astype(BF)
+        for copy in self.back_first(p):
+            copy.start()
+
+    def forward_y(self, p):
+        for copy in self.back_first(p):
+            copy.wait()
+        for copy in self.back_second(p):
+            copy.start()
+
+    def forward_core(self, p):
+        for copy in self.back_second(p):
+            copy.wait()
+        self.back_core(p).start()
+
+    def finish(self, p):
+        self.back_core(p).wait()
+
+    def steps(self, t, begin=0):
+        for lag, step in enumerate((self.add_core, self.add_first, self.add_second, self.add_z,
+                                    self.forward_y, self.forward_core, self.finish), 1):
+            p = t - lag
+            pl.when((p >= 0) & (p < NP))(lambda step=step, p=p: step(p))
+
+
+def sum_kernel(pieces, out, copied, *scratch):
+    at = neighbours()
+    greet([at["dev_yl"], at["dev_yr"], at["dev_zh"], at["dev_core"]])
+    engine = GradSum(at, out, scratch)
+
+    @pl.loop(0, NP + DP_STAGES - 1)
+    def _(t):
+        engine.steps(t)
+
+        @pl.when(t < NP)
+        def _():
+            copy = pltpu.make_async_copy(pieces.at[t], engine.own.at[t % 2], copied)
+            copy.start()
+            copy.wait()
+            engine.send_piece(t)
+
+
+def sum_pieces(pieces):
+    return pl.pallas_call(
+        sum_kernel,
+        out_shape=jax.ShapeDtypeStruct((NP, 1024, 256), BF),
+        in_specs=[pl.BlockSpec(memory_space=pl.ANY)],
+        out_specs=pl.BlockSpec(memory_space=pl.ANY),
+        scratch_shapes=[pltpu.SemaphoreType.DMA] + GradSum.scratch(),
+        compiler_params=pltpu.CompilerParams(
+            collective_id=0, has_side_effects=True, vmem_limit_bytes=32 << 20),
+        cost_estimate=pl.CostEstimate(flops=0, bytes_accessed=2 * NP * 1024 * 512, transcendentals=0),
+    )(pieces)
+
+
+def to_pieces(grad_w_down, grad_w_out, grad_w_up, grad_w_qkv):
+    parts = [
+        grad_w_down.astype(BF).reshape(1024, 8, 256).transpose(1, 0, 2),
+        grad_w_out.astype(BF).reshape(256, 8, 256).transpose(1, 0, 2).reshape(2, 1024, 256),
+        grad_w_up.astype(BF).reshape(2, 1024, 4, 256).transpose(2, 0, 1, 3).reshape(8, 1024, 256),
+        grad_w_qkv.astype(BF).reshape(2, 1024, 3, 256).transpose(2, 0, 1, 3).reshape(6, 1024, 256),
+    ]
+    return jnp.concatenate(parts, axis=0)
+
+
+def from_pieces(total):
+    down = total[:8].transpose(1, 0, 2).reshape(1024, 2048).astype(F32)
+    out = total[8:10].reshape(8, 256, 256).transpose(1, 0, 2).reshape(256, 2048).astype(F32)
+    up = total[10:18].reshape(4, 2048, 256).transpose(1, 0, 2).reshape(2048, 1024).astype(F32)
+    qkv = total[18:].reshape(3, 2048, 256).transpose(1, 0, 2).astype(F32)
+    return down, out, up, qkv
 
 
 def positions_of(segment):
@@ -239,8 +454,9 @@
     gain_part = jnp.sum(grad_normed * unit_rows, axis=0)
     shift_part = jnp.sum(grad_normed, axis=0)
     grad_ln_gain, grad_ln_bias = lax.psum((gain_part, shift_part), ("dp", "tensor"))
-    grad_w_out, grad_w_down, bias_total, grad_w_up, grad_b_up, grad_w_qkv, grad_b_qkv = lax.psum(
-        (grad_w_out, grad_w_down, bias_total, grad_w_up, grad_b_up, grad_w_qkv, grad_b_qkv), "dp"
+    bias_total, grad_b_up, grad_b_qkv = lax.psum((bias_total, grad_b_up, grad_b_qkv), "dp")
+    grad_w_down, grad_w_out, grad_w_up, grad_w_qkv = from_pieces(
+        sum_pieces(to_pieces(grad_w_down, grad_w_out, grad_w_up, grad_w_qkv))
     )
     return (
         output,

time: 973 us -> 672 us (0.69)
  blocking collectives: 697 us -> 129 us
  Pallas kernels: 0 us -> 209 us
  local copies, waits for them, and re-layouts: 32.8 us -> 73.1 us
  other arithmetic: 34.6 us -> 52.2 us
    psum x1, blocking collectives: 546 us -> 67.6 us  [on_device(): lax.psum((gain_part, shift_part), ('dp', 'tensor'))]
    pallas_call x0 -> x1, Pallas kernels: none -> 209 us  [sum_pieces(): pl.pallas_call(sum_kernel, out_shape=jax.ShapeDtypeStruct((NP, 1024, 256)...]
    psum x1, blocking collectives: 152 us -> 61 us  [on_device(): lax.psum((bias_total, grad_b_up, grad_b_qkv), 'dp')]
    convert_element_type x0 -> x4, local copies, waits for them, and re-layouts: none -> 21.8 us  [the longest x1 9.12 us: from_pieces(): down = total[:8].transpose(1, 0, 2).reshape(1024, 2048).astype(F32)]
    reshape x0 -> x4, local copies, waits for them, and re-layouts: none -> 19.4 us  [the longest x2 12.9 us: to_pieces(): grad_w_up.astype(BF).reshape(2, 1024, 4, 256).transpose(2, 0, 1, 3)]
    convert_element_type x0 -> x2, other arithmetic: none -> 10.5 us  [the longest x1 7.31 us: from_pieces(): down = total[:8].transpose(1, 0, 2).reshape(1024, 2048).astype(F32)]
    unnamed x101 -> x96, local copies, waits for them, and re-layouts: 23.5 us -> 22.6 us
  transfers between devices with their start and end apart: 5 -> 4, of which waited for: 2 -> 2; matrix products, arithmetic and copies ran while one was open for 7% -> 20% of each run, Pallas kernels for 0% -> 31%
where the time goes in v1:
time: 672 us; the launch traced here: 666 us
  Pallas kernels  209 us (31%)
  blocking collectives  129 us (19%)
  matrix products  98.2 us (15%)
  waiting for transfers between devices  90.5 us (13%)
  local copies, waits for them, and re-layouts  73.1 us (11%)
  other arithmetic  52.2 us (8%)
  between operations  14.6 us (2%)
    pallas_call x1, Pallas kernels, sum_pieces(): pl.pallas_call(sum_kernel, out_shape=jax.ShapeDtypeStruct((NP, 1024, 256)...  209 us
    psum x1, blocking collectives, on_device(): lax.psum((gain_part, shift_part), ('dp', 'tensor'))  67.6 us
    psum x1, blocking collectives, on_device(): lax.psum((bias_total, grad_b_up, grad_b_qkv), 'dp')  61 us
    all_gather x1, waiting for transfers between devices, on_device(): gathered = lax.all_gather(normed, 'tensor', axis=0, tiled=True)  49 us
    all_gather x1, waiting for transfers between devices, on_device(): grad_rows = lax.all_gather(cotangent, 'tensor', axis=0, tiled=True)  40.8 us
    unnamed x96, local copies, waits for them, and re-layouts  22.6 us
  transfers between devices with their start and end apart: 4, of which 2 were waited for; matrix products, arithmetic and copies ran while one was open for 20% of the time, Pallas kernels for 31%

profile of v1, /device:TPU:1, one launch (start us, length us, event | category | flops | bytes accessed | tf_op | source)
XLA Modules:
  0.0 666.4 jit_solution(5151226631781474168)
XLA Ops:
  24.7 40.8 %all-gather.5.cloned.1.call-done = bf16[1024,2048]{1,0:T(8,128)(2,1)} async-done(((bf16[128,2048]{1,0:T(8,128)(2,1)}), bf16[1024,2048]{1,0:T(8,128)(2,1)}) %all-gather.5.cloned.1.call-update) | async-done | bytes 4194320 | tf_op jit(solution)/shard_map/all_gather | solution.py:407
  70.1 49.0 %all-gather.3.cloned.1.call-done = bf16[1024,2048]{1,0:T(8,128)(2,1)} async-done(((bf16[128,2048]{1,0:T(8,128)(2,1)}), bf16[1024,2048]{1,0:T(8,128)(2,1)}) %all-gather.3.cloned.1.call-update) | async-done | bytes 4194320 | tf_op jit(solution)/shard_map/all_gather | solution.py:381
  119.1 5.4 fusion.27
  148.5 6.0 fusion.99
  154.5 10.6 %convert_reduce_fusion.1 = (f32[1024]{0:T(1024)}, bf16[1024,1024]{1,0:T(8,128)(2,1)S(1)}) fusion(f32[1024,1024]{1,0:T(8,128)} %fusion.99, f32[1024]{0:T(1024)S(1)} %copy-done.35, bf16[1024,2048]{1,0:T(8,128)(2,1)S(1)} %copy-done.9, bf16[1024,2048]{1,0:T(8,128)(2,1)} %param.35), kind=kOutput, calls=%fused_computation.28 | convolution fusion | flops 4319083520 | bytes 14688256 | tf_op jit(solution)/shard_map/td,fd->tf/dot_general | solution.py:414
  165.0 7.2 %fusion.100 = f32[1024,2048]{1,0:T(8,128)} fusion(bf16[1024,1024]{1,0:T(8,128)(2,1)S(1)} %get-tuple-element.98, bf16[2048,1024]{1,0:T(8,128)(2,1)S(1)} %copy-done.38), kind=kOutput, calls=%fused_computation.173 | convolution fusion | flops 4294967296 | bytes 14680064 | tf_op jit(solution)/shard_map/tf,df->td/dot_general | solution.py:442
  183.5 8.3 %bitcast_add_fusion = f32[1024,2048]{1,0:T(8,128)} fusion(f32[1024,2048]{1,0:T(8,128)} %fusion.100, bf16[2048,3,256]{2,0,1:T(8,128)(2,1)S(1)} %copy-done, bf16[1024,1,256]{2,0,1:T(8,128)(2,1)} %copy.45, bf16[1024,1,256]{2,0,1:T(8,128)(2,1)} %copy.44, bf16[1024,1,256]{2,0,1:T(8,128)(2,1)} %copy.43), kind=kOutput, calls=%fused_computation.2 | convolution fusion | flops 3224895488 | bytes 21495808 | tf_op jit(solution)/shard_map/tcf,dcf->td/dot_general | solution.py:443
  196.7 5.8 fusion.56
  203.4 5.0 fusion.95
  208.4 4.6 convolution_add_fusion
  214.7 8.4 %convolution_convert_fusion = bf16[2048,1024]{1,0:T(8,128)(2,1)} fusion(bf16[1024,2048]{1,0:T(8,128)(2,1)} %all-gather.3.cloned.1.call-done, bf16[1024,1024]{1,0:T(8,128)(2,1)S(1)} %copy-done.46), kind=kOutput, calls=%fused_computation.39 | convolution fusion | flops 4297064448 | bytes 10485760 | tf_op jit(solution)/shard_map/td,tf->df/dot_general | solution.py:417
  223.0 7.9 %reshape.447 = bf16[2,1024,4,256]{3,2,1,0:T(4,128)(2,1)} reshape(bf16[2048,1024]{1,0:T(8,128)(2,1)} %convolution_convert_fusion) | data formatting | bytes 8388608 | tf_op jit(solution)/shard_map/reshape | solution.py:214
  230.9 5.1 copy.49
  237.2 6.8 %convolution_convert_fusion.1 = bf16[1024,2048]{1,0:T(8,128)(2,1)} fusion(bf16[1024,2048]{1,0:T(8,128)(2,1)S(1)} %copy-done.10, f32[1024,1024]{1,0:T(8,128)S(1)} %copy-done.44, f32[1024]{0:T(1024)S(1)} %copy-done.36), kind=kOutput, calls=%fused_computation.40 | convolution fusion | flops 4307550208 | bytes 12587008 | tf_op jit(solution)/shard_map/tf,td->fd/dot_general | solution.py:410
  244.0 6.6 copy.46
  250.6 6.4 copy.47
  264.8 5.9 pad_maximum_fusion.pieces
  270.7 208.9 %shard_map.230 = bf16[24,1024,256]{2,1,0:T(8,128)(2,1)S(1)} custom-call(bf16[24,1024,256]{2,1,0:T(8,128)(2,1)} %pad_maximum_fusion.pieces), custom_call_target="tpu_custom_call" | custom-call | bytes 25165824 | tf_op jit(solution)/shard_map/pallas_call | solution.py:198
  479.7 4.5 copy-done.2
  487.1 61.0 %all-reduce.3 = (f32[3,256]{1,0:T(4,128)}, f32[2048]{0:T(1024)S(1)}, f32[1024]{0:T(1024)}) all-reduce(f32[3,256]{1,0:T(4,128)S(1)} %convert_reduce_fusion.2, f32[2048]{0:T(1024)S(1)} %convert_reduce_fusion, f32[1024]{0:T(1024)S(1)} %copy-done.37), channel_id=1, replica_groups=mesh['dp'=16,'tensor'=8] {'dp'}, use_global_device_ids=true, to_apply=%region_23.24 | all-reduce | flops 3840 | bytes 30720 | tf_op jit(solution)/shard_map/psum | solution.py:457
  549.8 7.3 %convert_bitcast_fusion.1 = (f32[1024,8,256]{2,0,1:T(8,128)}, bf16[8,1024,256]{2,1,0:T(8,128)(2,1)}) fusion(bf16[24,1024,256]{2,1,0:T(8,128)(2,1)} %copy-done.2), kind=kLoop, calls=%fused_computation.3 | loop fusion | flops 2097152 | bytes 20971520 | tf_op jit(solution)/shard_map/convert_element_type | solution.py:221
  557.1 9.1 %copy.53 = f32[1024,8,256]{0,2,1:T(8,128)} copy(f32[1024,8,256]{2,0,1:T(8,128)} %get-tuple-element.99) | data formatting | bytes 16777216 | tf_op jit(solution)/shard_map/convert_element_type | solution.py:221
  566.3 9.1 %copy.54 = f32[1024,2048]{1,0:T(8,128)} copy(f32[1024,2048]{0,1:T(8,128)} %bitcast.145) | data formatting | bytes 16777216
  587.9 67.6 %all-reduce.2 = (f32[2048]{0:T(1024)}, f32[2048]{0:T(1024)}) all-reduce(f32[2048]{0:T(1024)S(1)} %get-tuple-element.88, f32[2048]{0:T(1024)S(1)} %get-tuple-element.91), channel_id=1, replica_groups=mesh['dp'=16,'tensor'=8] {'dp','tensor'}, use_global_device_ids=true, to_apply=%region_19.20 | all-reduce | flops 4096 | bytes 32768 | tf_op jit(solution)/shard_map/psum | solution.py:456
  (189 shorter events, 94.5 us)
Async XLA Ops:
  7.2 112.0 %copy-start = (bf16[2048,3,256]{2,0,1:T(8,128)(2,1)S(1)}, bf16[2048,3,256]{2,0,1:T(8,128)(2,1)}, u32[]{:S(2)}) copy-start(bf16[2048,3,256]{2,0,1:T(8,128)(2,1)} %param.29) | copy-start | bytes 9437188
  7.2 58.3 %all-gather.5.cloned.1.call-start = ((), (), s32[]{:S(2)}) async-start(), calls=%async_computation.4 | async-start | bytes 4718592 | tf_op jit(solution)/shard_map/all_gather | solution.py:407
  7.9 111.2 %all-gather.3.cloned.1.call-start = ((), (), s32[]{:S(2)}) async-start(), calls=%async_computation.2 | async-start | bytes 4718592 | tf_op jit(solution)/shard_map/all_gather | solution.py:381
  14.9 571.2 %reduce-scatter.5.cloned.1.call-start = ((), (), s32[]{:S(2)}) async-start(), calls=%async_computation.5 | async-start | bytes 9437184 | tf_op jit(solution)/shard_map/reduce_scatter | solution.py:441
  124.8 12.7 %copy-start.12 = (bf16[1024,3,4,64]{0,3,2,1:T(8,128)(2,1)}, bf16[1024,3,4,64]{0,3,2,1:T(8,128)(2,1)S(1)}, u32[]{:S(2)}) copy-start(bf16[1024,3,4,64]{0,3,2,1:T(8,128)(2,1)S(1)} %bitcast_convert_fusion) | copy-start | bytes 4718596
  134.8 37.4 %copy-start.3 = (f32[4,512,1024]{2,1,0:T(8,128)}, f32[4,512,1024]{2,1,0:T(8,128)S(1)}, u32[]{:S(2)}) copy-start(f32[4,512,1024]{2,1,0:T(8,128)S(1)} %get-tuple-element.124) | copy-start | bytes 25165828
  148.5 6.0 copy-start.9
  148.5 6.0 copy-start.35
  165.0 7.2 %copy-start.45 = (bf16[1024,1024]{1,0:T(8,128)(2,1)}, bf16[1024,1024]{1,0:T(8,128)(2,1)S(1)}, u32[]{:S(2)}) copy-start(bf16[1024,1024]{1,0:T(8,128)(2,1)S(1)} %get-tuple-element.98) | copy-start | bytes 6291460
  165.0 7.2 %copy-start.18 = (bf16[512,256]{0,1:T(8,128)(2,1)S(1)}, bf16[512,256]{0,1:T(8,128)(2,1)}, u32[]{:S(2)}) copy-start(bf16[512,256]{0,1:T(8,128)(2,1)} %get-tuple-element.114) | copy-start | bytes 786436
  165.0 7.2 %copy-start.42 = (f32[512,4,64]{0,2,1:T(8,128)S(1)}, f32[512,4,64]{0,2,1:T(8,128)}, u32[]{:S(2)}) copy-start(f32[512,4,64]{0,2,1:T(8,128)} %fusion.47) | copy-start | bytes 1572868
  172.2 4.9 copy-start.21
  191.8 4.9 copy-start.8
  191.8 4.9 copy-start.25
  191.8 4.9 copy-start.27
  191.8 463.7 %reduce-scatter.3.cloned.1.call-start = ((), (), s32[]{:S(2)}) async-start(), calls=%async_computation.3 | async-start | bytes 9437184 | tf_op jit(solution)/shard_map/reduce_scatter | solution.py:397
  196.7 5.9 copy-start.36
  196.7 5.9 copy-start.39
  196.7 6.7 %copy-start.43 = (f32[1024,1024]{1,0:T(8,128)S(1)}, f32[1024,1024]{1,0:T(8,128)}, u32[]{:S(2)}) copy-start(f32[1024,1024]{1,0:T(8,128)} %fusion.99) | copy-start | bytes 12582916
  203.4 5.0 copy-start.19
  230.9 5.1 copy-start.10
  230.9 6.3 copy-start.44
  548.0 111.0 %copy-start.28 = (f32[2048]{0:T(1024)}, f32[2048]{0:T(1024)S(1)}, u32[]{:S(2)}) copy-start(f32[2048]{0:T(1024)S(1)} %get-tuple-element.156) | copy-start | bytes 24580
  582.8 76.8 %copy-start.1 = (bf16[2048,3,256]{2,0,1:T(8,128)(2,1)S(1)}, bf16[2048,3,256]{2,0,1:T(8,128)(2,1)}, u32[]{:S(2)}) copy-start(bf16[2048,3,256]{2,0,1:T(8,128)(2,1)} %param.29) | copy-start | bytes 9437188
  (28 other events, 79.7 us)
Sparse Core Ops, SparseCore 0:
  9.7 55.8 all-gather.4
  67.8 51.3 all-gather.2
  191.9 91.4 reduce-scatter.4
  285.7 91.4 reduce-scatter.2

commit v2 on v1

v2 whole, which is shorter than its diff:
```python
import jax
import jax.numpy as jnp
from jax import lax
from jax.experimental import pallas as pl
from jax.experimental.pallas import tpu as pltpu
from jax.sharding import PartitionSpec as P

HEAD_DIM = 64
ROT = 32
EPSILON = 1e-05
MESH = pl.DeviceIdType.MESH
BF = jnp.bfloat16
F32 = jnp.float32
NP = 24
VMEM_LIMIT = 64 << 20


def neighbours():
    dp = lax.axis_index("dp")
    tensor = lax.axis_index("tensor")
    y, zh, core = dp // 4, (dp // 2) % 2, dp % 2
    zl, x = tensor // 4, tensor % 4
    yl, yr, yo = (y + 3) % 4, (y + 1) % 4, (y + 2) % 4
    xl, xr, xo = (x + 3) % 4, (x + 1) % 4, (x + 2) % 4
    where = dict(y=y, core=core, zl=zl, x=x, yl=yl, yr=yr, yo=yo, xl=xl, xr=xr, xo=xo)
    where["dev_yl"] = (yl * 4 + zh * 2 + core, tensor)
    where["dev_yr"] = (yr * 4 + zh * 2 + core, tensor)
    where["dev_zh"] = (y * 4 + (1 - zh) * 2 + core, tensor)
    where["dev_core"] = (y * 4 + zh * 2 + 1 - core, tensor)
    where["dev_xl"] = (dp, zl * 4 + xl)
    where["dev_xr"] = (dp, zl * 4 + xr)
    where["dev_zl"] = (dp, (1 - zl) * 4 + x)
    return where


def greet(devices):
    barrier = pltpu.get_barrier_semaphore()
    for device in devices:
        pl.semaphore_signal(barrier, inc=1, device_id=device, device_id_type=MESH)
    pl.semaphore_wait(barrier, len(devices))


def rcopy(src, dst, send, recv, device):
    return pltpu.make_async_remote_copy(
        src_ref=src, dst_ref=dst, send_sem=send, recv_sem=recv, device_id=device, device_id_type=MESH
    )


def rows_at(index, size, count=None):
    return pl.ds(pl.multiple_of(index * size, size), size if count is None else count)


class GradSum:
    def scratch():
        return [
            pltpu.VMEM((2, 1024, 256), BF),
            pltpu.VMEM((4, 512, 256), BF),
            pltpu.VMEM((4, 512, 256), BF),
            pltpu.VMEM((4, 2, 64, 256), BF),
            pltpu.VMEM((4, 2, 128, 256), BF),
            pltpu.VMEM((4, 128, 256), BF),
            pltpu.VMEM((4, 128, 256), BF),
            pltpu.VMEM((4, 128, 256), BF),
            pltpu.SemaphoreType.DMA((11, 4)),
            pltpu.SemaphoreType.DMA((11, 4)),
            pltpu.SemaphoreType.DMA((4,)),
        ]

    def __init__(self, at, out, scratch):
        self.at, self.out = at, out
        (self.own, self.other, self.half, self.r1, self.r2, self.zs, self.zr, self.full,
         self.send, self.recv, self.local) = scratch

    def core_copy(self, p):
        s, at = p % 4, self.at
        return rcopy(self.own.at[p % 2, rows_at(1 - at["core"], 512)], self.other.at[s],
                     self.send.at[0, s], self.recv.at[0, s], at["dev_core"])

    def first_copies(self, p):
        s, at = p % 4, self.at
        top = self.half.at[s, rows_at(at["yo"], 128, 64)]
        low = self.half.at[s, pl.ds(pl.multiple_of(at["yo"] * 128 + 64, 64), 64)]
        return (rcopy(top, self.r1.at[s, 0], self.send.at[1, s], self.recv.at[1, s], at["dev_yr"]),
                rcopy(low, self.r1.at[s, 1], self.send.at[2, s], self.recv.at[2, s], at["dev_yl"]))

    def second_copies(self, p):
        s, at = p % 4, self.at
        return (rcopy(self.half.at[s, rows_at(at["yr"], 128)], self.r2.at[s, 0],
                      self.send.at[3, s], self.recv.at[3, s], at["dev_yr"]),
                rcopy(self.half.at[s, rows_at(at["yl"], 128)], self.r2.at[s, 1],
                      self.send.at[4, s], self.recv.at[4, s], at["dev_yl"]))

    def z_copy(self, p):
        s = p % 4
        return rcopy(self.zs.at[s], self.zr.at[s], self.send.at[5, s], self.recv.at[5, s],
                     self.at["dev_zh"])

    def back_first(self, p):
        s, at = p % 4, self.at
        mine = self.out.at[p, rows_at(at["core"] * 4 + at["y"], 128)]
        return (rcopy(self.full.at[s], mine, self.send.at[6, s], self.recv.at[6, s], at["dev_yr"]),
                rcopy(self.full.at[s], mine, self.send.at[7, s], self.recv.at[7, s], at["dev_yl"]),
                pltpu.make_async_copy(self.full.at[s], mine, self.local.at[s]))

    def back_second(self, p):
        s, at = p % 4, self.at
        top = self.out.at[p, rows_at(at["core"] * 4 + at["yl"], 128, 64)]
        low = self.out.at[p, pl.ds(pl.multiple_of((at["core"] * 4 + at["yr"]) * 128 + 64, 64), 64)]
        return (rcopy(top, top, self.send.at[9, s], self.recv.at[9, s], at["dev_yr"]),
                rcopy(low, low, self.send.at[10, s], self.recv.at[10, s], at["dev_yl"]))

    def back_core(self, p):
        s, at = p % 4, self.at
        mine = self.out.at[p, rows_at(at["core"], 512)]
        return rcopy(mine, mine, self.send.at[8, s], self.recv.at[8, s], at["dev_core"])

    def send_piece(self, p):
        self.core_copy(p).start()

    def add_core(self, p):
        s = p % 4
        self.core_copy(p).wait()

        @pl.loop(0, 4)
        def _(j):
            rows = rows_at(j, 128)
            mine = self.own[p % 2, pl.ds(pl.multiple_of(self.at["core"] * 512 + j * 128, 128), 128)]
            self.half[s, rows] = (mine.astype(F32) + self.other[s, rows].astype(F32)).astype(BF)

        for copy in self.first_copies(p):
            copy.start()

    def add_first(self, p):
        s, at = p % 4, self.at
        for copy in self.first_copies(p):
            copy.wait()
        top = rows_at(at["yr"], 128, 64)
        low = pl.ds(pl.multiple_of(at["yl"] * 128 + 64, 64), 64)
        self.half[s, top] = (self.half[s, top].astype(F32) + self.r1[s, 0].astype(F32)).astype(BF)
        self.half[s, low] = (self.half[s, low].astype(F32) + self.r1[s, 1].astype(F32)).astype(BF)
        for copy in self.second_copies(p):
            copy.start()

    def add_second(self, p):
        s = p % 4
        for copy in self.second_copies(p):
            copy.wait()
        mine = self.half[s, rows_at(self.at["y"], 128)].astype(F32)
        self.zs[s] = (mine + self.r2[s, 0].astype(F32) + self.r2[s, 1].astype(F32)).astype(BF)
        self.z_copy(p).start()

    def add_z(self, p):
        s = p % 4
        self.z_copy(p).wait()
        self.full[s] = (self.zs[s].astype(F32) + self.zr[s].astype(F32)).astype(BF)
        for copy in self.back_first(p):
            copy.start()

    def forward_y(self, p):
        for copy in self.back_first(p):
            copy.wait()
        for copy in self.back_second(p):
            copy.start()

    def forward_core(self, p):
        for copy in self.back_second(p):
            copy.wait()
        self.back_core(p).start()

    def finish(self, p):
        self.back_core(p).wait()

    def steps(self, t, begin=0):
        for lag, step in enumerate((self.add_core, self.add_first, self.add_second, self.add_z,
                                    self.forward_y, self.forward_core, self.finish), 1):
            p = t - lag
            pl.when((p >= 0) & (p < NP))(lambda step=step, p=p: step(p))


def dot(a, b):
    return lax.dot_general(a, b, (((1,), (0,)), ((), ())), preferred_element_type=F32)


def dot_nt(a, b):
    return lax.dot_general(a, b, (((1,), (1,)), ((), ())), preferred_element_type=F32)


def at_rows(index, size=256):
    return pl.ds(pl.multiple_of(index * size, size), size)


class Gather:
    def scratch():
        return [
            pltpu.VMEM((16, 128, 256), BF),
            pltpu.VMEM((8, 1024, 256), BF),
            pltpu.SemaphoreType.DMA((9, 4)),
            pltpu.SemaphoreType.DMA((9, 4)),
        ]

    def __init__(self, at, scratch):
        self.at = at
        self.own, self.all, self.send, self.recv = scratch

    def copy(self, kind, c, src, dst, device):
        s = c % 4
        return rcopy(src, dst, self.send.at[kind, s], self.recv.at[kind, s], device)

    def part(self, c, zl, x, begin=0, count=128):
        first = pl.multiple_of((zl * 4 + x) * 128 + begin, 64)
        return self.all.at[c % 8, pl.ds(first, count)]

    def first(self, c):
        at = self.at
        src, dst = self.own.at[c], self.part(c, at["zl"], at["x"])
        return [self.copy(0, c, src, dst, at["dev_xr"]), self.copy(1, c, src, dst, at["dev_xl"]),
                self.copy(2, c, src, dst, at["dev_zl"])]

    def second(self, c):
        at = self.at
        top = self.part(c, at["zl"], at["xl"], 0, 64)
        low = self.part(c, at["zl"], at["xr"], 64, 64)
        other = self.part(c, 1 - at["zl"], at["x"])
        return [self.copy(3, c, top, top, at["dev_xr"]), self.copy(4, c, low, low, at["dev_xl"]),
                self.copy(5, c, other, other, at["dev_xr"]), self.copy(6, c, other, other, at["dev_xl"])]

    def third(self, c):
        at = self.at
        top = self.part(c, 1 - at["zl"], at["xl"], 0, 64)
        low = self.part(c, 1 - at["zl"], at["xr"], 64, 64)
        return [self.copy(7, c, top, top, at["dev_xr"]), self.copy(8, c, low, low, at["dev_xl"])]

    def steps(self, t):
        @pl.when(t < 16)
        def _():
            for copy in self.first(t):
                copy.start()
            self.part(t, self.at["zl"], self.at["x"])[...] = self.own[t]

        @pl.when((t >= 1) & (t < 17))
        def _():
            for copy in self.first(t - 1):
                copy.wait()
            for copy in self.second(t - 1):
                copy.start()

        @pl.when((t >= 2) & (t < 18))
        def _():
            for copy in self.second(t - 2):
                copy.wait()
            for copy in self.third(t - 2):
                copy.start()

        @pl.when((t >= 3) & (t < 19))
        def _():
            for copy in self.third(t - 3):
                copy.wait()


class RowSum:
    def scratch():
        return [
            pltpu.VMEM((4, 2, 4, 128, 256), BF),
            pltpu.VMEM((4, 2, 2, 64, 256), BF),
            pltpu.VMEM((4, 2, 2, 128, 256), BF),
            pltpu.VMEM((4, 128, 256), BF),
            pltpu.VMEM((4, 128, 256), BF),
            pltpu.VMEM((4, 128, 256), F32),
            pltpu.SemaphoreType.DMA((5, 4)),
            pltpu.SemaphoreType.DMA((5, 4)),
        ]

    def __init__(self, at, scratch, result):
        self.at, self.result = at, result
        self.part, self.r1, self.r2, self.zs, self.zr, self.mine, self.send, self.recv = scratch

    def copy(self, kind, c, src, dst, device):
        s = c % 4
        return rcopy(src, dst, self.send.at[kind, s], self.recv.at[kind, s], device)

    def first(self, c):
        s, at = c % 4, self.at
        return [self.copy(0, c, self.part.at[s, :, at["xo"], pl.ds(0, 64)], self.r1.at[s, 0], at["dev_xr"]),
                self.copy(1, c, self.part.at[s, :, at["xo"], pl.ds(64, 64)], self.r1.at[s, 1], at["dev_xl"])]

    def second(self, c):
        s, at = c % 4, self.at
        return [self.copy(2, c, self.part.at[s, :, at["xr"]], self.r2.at[s, 0], at["dev_xr"]),
                self.copy(3, c, self.part.at[s, :, at["xl"]], self.r2.at[s, 1], at["dev_xl"])]

    def third(self, c):
        s = c % 4
        return [self.copy(4, c, self.zs.at[s], self.zr.at[s], self.at["dev_zl"])]

    def store(self, c, block, value):
        for k in range(2):
            r = block * 2 + k
            self.part[c % 4, r // 4, r % 4] = value[k * 128:(k + 1) * 128].astype(BF)

    def send_chunk(self, c):
        for copy in self.first(c):
            copy.start()

    def add_first(self, c):
        s, at = c % 4, self.at
        for copy in self.first(c):
            copy.wait()
        for z in range(2):
            top = self.part[s, z, at["xr"], 0:64].astype(F32) + self.r1[s, 0, z].astype(F32)
            self.part[s, z, at["xr"], 0:64] = top.astype(BF)
            low = self.part[s, z, at["xl"], 64:128].astype(F32) + self.r1[s, 1, z].astype(F32)
            self.part[s, z, at["xl"], 64:128] = low.astype(BF)
        for copy in self.second(c):
            copy.start()

    def add_second(self, c):
        s, at = c % 4, self.at
        for copy in self.second(c):
            copy.wait()

        def total(z):
            own = self.part[s, z, at["x"]].astype(F32)
            return own + self.r2[s, 0, z].astype(F32) + self.r2[s, 1, z].astype(F32)

        self.zs[s] = total(1 - at["zl"]).astype(BF)
        for copy in self.third(c):
            copy.start()
        self.mine[s] = total(at["zl"])

    def add_third(self, c):
        s = c % 4
        for copy in self.third(c):
            copy.wait()
        self.result(c, self.mine[s] + self.zr[s].astype(F32))

    def steps(self, t):
        for lag, step in enumerate((self.add_first, self.add_second, self.add_third), 1):
            c = t - lag
            pl.when((c >= 0) & (c < 8))(lambda step=step, c=c: step(c))
            pl.when((c >= 10) & (c < 18))(lambda step=step, c=c - 2: step(c))


class SmallSum:
    def scratch():
        return [
            pltpu.VMEM((8, 8, 1024), F32),
            pltpu.VMEM((4, 8, 1024), F32),
            pltpu.VMEM((4, 8, 1024), F32),
            pltpu.SemaphoreType.DMA((13,)),
            pltpu.SemaphoreType.DMA((13,)),
        ]

    def __init__(self, scratch):
        self.b1, self.b2, self.b3, self.send, self.recv = scratch
        dp, tensor = lax.axis_index("dp"), lax.axis_index("tensor")
        y, self.zh, core = dp // 4, (dp // 2) % 2, dp % 2
        self.zl, self.x = tensor // 4, tensor % 4
        self.i1 = y * 2 + core
        self.i2 = self.zh * 2 + self.zl
        self.d1, self.d2, self.d3 = [], [], []
        for k in range(1, 8):
            j = (self.i1 + k) % 8
            self.d1.append(((j // 2) * 4 + self.zh * 2 + j % 2, tensor))
        for k in range(1, 4):
            j = (self.i2 + k) % 4
            self.d2.append((y * 4 + (j // 2) * 2 + core, (j % 2) * 4 + self.x))
            self.d3.append((dp, self.zl * 4 + (self.x + k) % 4))

    def devices(self):
        return self.d1 + self.d2 + self.d3

    def copies(self, stage):
        buf, mine, devices, base = ((self.b1, self.i1, self.d1, 0), (self.b2, self.i2, self.d2, 7),
                                    (self.b3, self.x, self.d3, 10))[stage]
        return [rcopy(buf.at[mine], buf.at[mine], self.send.at[base + k], self.recv.at[base + k], device)
                for k, device in enumerate(devices)]

    def start(self, stage):
        for copy in self.copies(stage):
            copy.start()

    def wait(self, stage):
        for copy in self.copies(stage):
            copy.wait()

    def second(self):
        self.wait(0)
        total = self.b1[0]
        for k in range(1, 8):
            total = total + self.b1[k]
        self.b2[self.i2] = total
        self.start(1)

    def third(self):
        self.wait(1)
        wide = self.b2[0] + self.b2[1] + self.b2[2] + self.b2[3]
        narrow = self.b2[self.zl] + self.b2[2 + self.zl]
        row = lax.broadcasted_iota(jnp.int32, (8, 1024), 0)
        self.b3[self.x] = jnp.where(row < 6, wide, narrow)
        self.start(2)

    def result(self):
        self.wait(2)
        wide = self.b3[0] + self.b3[1] + self.b3[2] + self.b3[3]
        row = lax.broadcasted_iota(jnp.int32, (8, 1024), 0)
        return jnp.where(row < 6, wide, self.b3[self.x])


def gelu_parts(u):
    inner = 0.7978845608028654 * (u + 0.044715 * (u * u * u))
    return jnp.tanh(inner)


def swap_pairs(v):
    lane = lax.broadcasted_iota(jnp.int32, v.shape, 1)
    return jnp.where(lane % 32 < 16, pltpu.roll(v, 112, 1), pltpu.roll(v, 16, 1))


def turn(v, cosine, sine):
    return v * cosine + swap_pairs(v) * sine


HO = 12
RS = 20


def block_kernel(
    tokens, cotangent, seg_row, inverse, gain, shift, b_qkv, b_out, b_up, b_down,
    w_qkv_h, w_out_h, w_up_h, w_down_h,
    pieces, output, input_grad, sums,
    w_qkv, w_out, w_up, w_down, w_sem,
    normed_t, up, grad_act, qkv_f, rows, turned, act, act_t, heads, heads_t, outs_g, outs_gt, gqkv,
    cos_t, sin_t, seg_c, seg_r, lse, bias, p_f, dp_f, q_m, g_m, unit, rstd, grad_n,
    *scratch,
):
    at = neighbours()
    n1, n2, n3 = len(GradSum.scratch()), len(Gather.scratch()), len(RowSum.scratch())
    small = SmallSum(scratch[n1 + n2 + n3:])
    grads = GradSum(at, pieces, scratch[:n1])
    gather = Gather(at, scratch[n1:n1 + n2])

    def keep_rows(c, value):
        @pl.when(c < 8)
        def _():
            cols = at_rows(c)
            own = tokens[:, cols].astype(F32) + value
            own = own + b_out[0:1, cols].astype(F32) + b_down[0:1, cols].astype(F32)
            output[:, cols] = own.astype(BF)

        @pl.when(c >= 8)
        def _():
            grad_n[c - 8] = value

    row_sum = RowSum(at, scratch[n1 + n2:n1 + n2 + n3], keep_rows)
    do_acc = dp_f
    grad_up = act_t

    weights = [pltpu.make_async_copy(src, dst, w_sem.at[i]) for i, (src, dst) in enumerate(
        ((w_up_h, w_up), (w_qkv_h, w_qkv), (w_down_h, w_down), (w_out_h, w_out)))]
    for copy in weights:
        copy.start()

    barrier = pltpu.get_barrier_semaphore()
    greeted = small.devices()
    for device in greeted:
        pl.semaphore_signal(barrier, inc=1, device_id=device, device_id_type=MESH)

    x = tokens[...].astype(F32)
    centered = x - jnp.mean(x, axis=1, keepdims=True)
    scale = lax.rsqrt(jnp.mean(centered * centered, axis=1, keepdims=True) + EPSILON)
    rstd[...] = jnp.broadcast_to(scale, (128, 128))
    unit[...] = centered * scale
    for c in range(8):
        cols = slice(c * 256, c * 256 + 256)
        value = unit[:, cols] * gain[0:1, cols].astype(F32) + shift[0:1, cols].astype(F32)
        gather.own[c] = value.astype(BF)
        gather.own[8 + c] = cotangent[:, cols]

    pl.semaphore_wait(barrier, len(greeted))
    gather.steps(0)

    seg_f = seg_row[...].astype(F32)
    seg_r[...] = jnp.broadcast_to(seg_f, (8, 1024))
    seg_c[...] = jnp.broadcast_to(seg_f, (128, 1024)).T
    for ref in (q_m, g_m):
        ref[...] = jnp.zeros_like(ref)

    @pl.loop(0, 4)
    def _(b):
        r = at_rows(b)
        own_id = seg_c[r, 0:1]
        other = seg_r[0:1, :]
        i = lax.broadcasted_iota(jnp.int32, (256, 1024), 0) + b * 256
        j = lax.broadcasted_iota(jnp.int32, (256, 1024), 1)
        same = jnp.where((own_id == other) & (j < i), 1.0, 0.0)
        position = jnp.sum(same, axis=1, keepdims=True)
        angle = position * inverse[0:1, :]
        lane = lax.broadcasted_iota(jnp.int32, (256, 128), 1) % 64
        sine = jnp.sin(angle)
        cos_t[r, :] = jnp.where(lane < ROT, jnp.cos(angle), 1.0)
        sin_t[r, :] = jnp.where(lane < ROT // 2, -sine, jnp.where(lane < ROT, sine, 0.0))
        up[r, :] = jnp.broadcast_to(b_up[0:1, :].astype(F32), (256, 1024))
        for k in range(3):
            qkv_f[k, r, :] = jnp.broadcast_to(b_qkv[k:k + 1, :].astype(F32), (256, 256))

    @pl.loop(1, 11)
    def _(t):
        gather.steps(t)

        @pl.when(t == 3)
        def _():
            weights[0].wait()
            weights[1].wait()

        @pl.when(t >= 3)
        def _():
            c = t - 3

            @pl.loop(0, 4)
            def _(b):
                r = at_rows(b)
                a = gather.all[c % 8, r, :]
                for k in range(4):
                    cols = slice(k * 256, k * 256 + 256)
                    up[r, cols] += dot(a, w_up[at_rows(c), cols])
                for k in range(3):
                    qkv_f[k, r, :] += dot(a, w_qkv[k, at_rows(c), :])
                normed_t[at_rows(c), r] = a.T

    gather.steps(11)

    @pl.loop(0, 4)
    def _(b):
        r = at_rows(b)
        for k in range(4):
            cols = slice(k * 256, k * 256 + 256)
            u = up[r, cols]
            a = (u * (0.5 * (1.0 + gelu_parts(u)))).astype(BF)
            act[r, cols] = a
            act_t[cols, r] = a.T

    def make_rows(b):
        r = at_rows(b)
        for k in range(3):
            for half in range(2):
                cols = slice(half * 128, half * 128 + 128)
                v = qkv_f[k, r, cols]
                if k < 2:
                    v = turn(v, cos_t[r, :], sin_t[r, :])
                if k == 0:
                    v = v * HEAD_DIM ** -0.5
                v = v.astype(BF)
                rows[k, r, cols] = v
                turned[k, cols, r] = v.T

    def attend_bias(qb):
        cols = slice(qb * 256, qb * 256 + 256)
        for kb in range(qb + 1):
            r = slice(kb * 256, kb * 256 + 256)
            keep = seg_c[r, 0:1] == seg_r[0:1, cols]
            if kb == qb:
                i = lax.broadcasted_iota(jnp.int32, (256, 256), 0)
                j = lax.broadcasted_iota(jnp.int32, (256, 256), 1)
                keep = keep & (i <= j)
            bias[r, :] = jnp.where(keep, 0.0, -1e30)

    def head_rows(h):
        return pl.ds(pl.multiple_of(h * 64, 64), 64)

    def attend(qb):
        cols = slice(qb * 256, qb * 256 + 256)
        attend_bias(qb)

        @pl.loop(0, 4)
        def _(h):
            hr = head_rows(h)
            q_m[h, hr, :] = turned[0, hr, cols]
            most = jnp.full((1, 256), -jnp.inf, F32)
            for kb in range(qb + 1):
                r = slice(kb * 256, kb * 256 + 256)
                s = dot(rows[1, r, :], q_m[h]) + bias[r, :]
                p_f[r, :] = s
                most = jnp.maximum(most, jnp.max(s, axis=0, keepdims=True))
            total = jnp.zeros((1, 256), F32)
            for kb in range(qb + 1):
                r = slice(kb * 256, kb * 256 + 256)
                e = jnp.exp(p_f[r, :] - most)
                p_f[r, :] = e
                total = total + jnp.sum(e, axis=0, keepdims=True)
            share = 1.0 / total
            out = jnp.zeros((64, 256), F32)
            for kb in range(qb + 1):
                r = slice(kb * 256, kb * 256 + 256)
                p = (p_f[r, :] * share).astype(BF)
                out = out + dot(turned[2, hr, r], p)
            heads_t[hr, cols] = out.astype(BF)
            lse[pl.ds(h, 1), cols] = most + jnp.log(total)

    def attend_back(qb, first_head):
        cols = slice(qb * 256, qb * 256 + 256)
        if first_head == 0:
            attend_bias(qb)

        @pl.loop(first_head, first_head + 2)
        def _(h):
            hr = head_rows(h)
            q_m[h, hr, :] = turned[0, hr, cols]
            g_m[h, hr, :] = outs_gt[hr, cols]
            log_total = lse[pl.ds(h, 1), cols]
            delta = jnp.zeros((1, 256), F32)
            for kb in range(qb + 1):
                r = slice(kb * 256, kb * 256 + 256)
                p = jnp.exp(dot(rows[1, r, :], q_m[h]) + bias[r, :] - log_total)
                d = dot(rows[2, r, :], g_m[h])
                p_f[r, :] = p
                dp_f[r, :] = d
                delta = delta + jnp.sum(p * d, axis=0, keepdims=True)
            lane = lax.broadcasted_iota(jnp.int32, (256, 256), 1) // 64
            q_h = jnp.where(lane == h, rows[0, cols, :].astype(F32), 0.0).astype(BF)
            g_h = jnp.where(lane == h, outs_g[cols, :].astype(F32), 0.0).astype(BF)
            grad_q = jnp.zeros((64, 256), F32)
            for kb in range(qb + 1):
                r = slice(kb * 256, kb * 256 + 256)
                p = p_f[r, :]
                ds = (p * (dp_f[r, :] - delta)).astype(BF)
                qkv_f[1, r, :] += dot(ds, q_h)
                qkv_f[2, r, :] += dot(p.astype(BF), g_h)
                grad_q = grad_q + dot(turned[1, hr, r], ds)
            for half in range(2):
                qkv_f[0, pl.ds(pl.multiple_of(qb * 256 + h * 64, 64), 64),
                      half * 128:half * 128 + 128] = grad_q[:, half * 128:half * 128 + 128]

    @pl.loop(12, 20)
    def _(t):
        grads.steps(t - HO)
        gather.steps(t)
        c = t - 12

        @pl.when(t == 12)
        def _():
            weights[2].wait()
            weights[3].wait()

        @pl.loop(0, 4)
        def _(b):
            r = at_rows(b)
            grads.own[c % 2, r, :] = dot(act_t[r, :], gather.all[c % 8]).astype(BF)

        grads.send_piece(c)

        @pl.loop(0, 4)
        def _(b):
            r = at_rows(b)
            a = gather.all[c % 8, r, :]
            fresh = c == 0
            for k in range(4):
                cols = slice(k * 256, k * 256 + 256)
                grad_act[r, cols] = jnp.where(fresh, 0.0, grad_act[r, cols]) + dot_nt(a, w_down[cols, at_rows(c)])
            do_acc[r, :] = jnp.where(fresh, 0.0, do_acc[r, :]) + dot_nt(a, w_out[:, at_rows(c)])

        @pl.when(t < 16)
        def _():
            make_rows(t - 12)

        for qb in range(4):
            pl.when(t == 16 + qb)(lambda qb=qb: attend(qb))

    def branch_chunk(c):
        @pl.loop(0, 4)
        def _(b):
            r = at_rows(b)
            value = dot(act[r, :], w_down[:, at_rows(c)]) + dot(heads[r, :], w_out[:, at_rows(c)])
            row_sum.store(c, b, value)
        row_sum.send_chunk(c)

    def normed_chunk(c):
        @pl.loop(0, 4)
        def _(b):
            r = at_rows(b)
            d = at_rows(c)
            value = dot_nt(grad_up[r, :], w_up[d, :])
            for k in range(3):
                value = value + dot_nt(gqkv[k, r, :], w_qkv[k, d, :])
            row_sum.store(c + 8, b, value)
        row_sum.send_chunk(c + 8)

    @pl.loop(0, 4)
    def _(b):
        r = at_rows(b)
        heads[r, :] = heads_t[:, r].T
        g = do_acc[r, :].astype(BF)
        outs_g[r, :] = g
        outs_gt[:, r] = g.T

    @pl.loop(20, 22)
    def _(t):
        grads.steps(t - HO)
        row_sum.steps(t - RS)
        p = t - HO
        for j in range(4):
            r = slice(j * 256, j * 256 + 256)
            grads.own[p % 2, r, :] = dot(heads_t[...], gather.all[4 * (p - 8) + j]).astype(BF)
        grads.send_piece(p)
        branch_chunk(t - RS)

        @pl.loop(2 * (t - 20), 2 * (t - 20) + 2)
        def _(b):
            r = at_rows(b)
            for k in range(4):
                cols = slice(k * 256, k * 256 + 256)
                u = up[r, cols]
                th = gelu_parts(u)
                slope = 0.5 * (1.0 + th) + 0.5 * u * (1.0 - th * th) * (
                    0.7978845608028654 * (1.0 + 3 * 0.044715 * (u * u)))
                grad_up[r, cols] = (slope * grad_act[r, cols]).astype(BF)

        @pl.loop(0, 2)
        def _(half):
            for k in range(3):
                qkv_f[k, at_rows((t - 20) * 2 + half), :] = jnp.zeros((256, 256), F32)

    @pl.loop(22, 30)
    def _(t):
        grads.steps(t - HO)
        row_sum.steps(t - RS)
        p = t - HO
        q = p - 10

        @pl.loop(0, 4)
        def _(b):
            r = at_rows((q % 2) * 4 + b)
            grads.own[p % 2, at_rows(b), :] = dot(normed_t[r, :], grad_up[:, at_rows(q // 2)]).astype(BF)

        grads.send_piece(p)

        @pl.when(t < 28)
        def _():
            branch_chunk(t - RS)

        for qb in range(4):
            for half in range(2):
                pl.when(t == 22 + 2 * qb + half)(lambda qb=qb, half=half: attend_back(qb, 2 * half))

    mine = small.i1

    def column_sum(value):
        return jnp.sum(value.astype(F32), axis=0, keepdims=True)

    for b in range(4):
        r = slice(b * 256, b * 256 + 256)
        grad_q = qkv_f[0, r, :].T * HEAD_DIM ** -0.5
        for half in range(2):
            cols = slice(half * 128, half * 128 + 128)
            cosine, sine = cos_t[r, :], -sin_t[r, :]
            gqkv[0, r, cols] = turn(grad_q[:, cols], cosine, sine).astype(BF)
            gqkv[1, r, cols] = turn(qkv_f[1, r, cols], cosine, sine).astype(BF)
            gqkv[2, r, cols] = qkv_f[2, r, cols].astype(BF)

    @pl.loop(30, 36)
    def _(t):
        grads.steps(t - HO)
        row_sum.steps(t - RS)
        p = t - HO
        q = p - 18

        @pl.loop(0, 4)
        def _(b):
            r = at_rows((q % 2) * 4 + b)
            grads.own[p % 2, at_rows(b), :] = dot(normed_t[r, :], gqkv[q // 2]).astype(BF)

        grads.send_piece(p)
        normed_chunk(t - 30)

    @pl.loop(36, 41)
    def _(t):
        grads.steps(t - HO)
        row_sum.steps(t - RS)

        @pl.when(t < 38)
        def _():
            normed_chunk(t - 30)

    small.b1[mine] = jnp.zeros((8, 1024), F32)
    mean_plain = jnp.zeros((128, 1), F32)
    mean_unit = jnp.zeros((128, 1), F32)
    for c in range(8):
        cols = slice(c * 256, c * 256 + 256)
        row, lanes = c // 4, slice((c % 4) * 256, (c % 4) * 256 + 256)
        g = grad_n[c]
        n = unit[:, cols]
        scaled = g * gain[0:1, cols].astype(F32)
        mean_plain = mean_plain + jnp.sum(scaled, axis=1, keepdims=True)
        mean_unit = mean_unit + jnp.sum(scaled * n, axis=1, keepdims=True)
        small.b1[mine, row:row + 1, lanes] = column_sum(g * n)
        small.b1[mine, 2 + row:3 + row, lanes] = column_sum(g)
        small.b1[mine, 4 + row:5 + row, lanes] = column_sum(cotangent[:, cols])
    for k in range(4):
        cols = slice(k * 256, k * 256 + 256)
        small.b1[mine, 6:7, cols] = column_sum(grad_up[:, cols])
    for k in range(3):
        small.b1[mine, 7:8, k * 256:k * 256 + 256] = column_sum(gqkv[k])
    small.start(0)
    mean_plain = mean_plain / 2048.0
    mean_unit = mean_unit / 2048.0
    for c in range(8):
        cols = slice(c * 256, c * 256 + 256)
        scaled = grad_n[c] * gain[0:1, cols].astype(F32)
        inner = scaled - mean_plain - unit[:, cols] * mean_unit
        input_grad[:, cols] = (cotangent[:, cols].astype(F32) + rstd[:, 0:1] * inner).astype(BF)

    grads.steps(41 - HO)
    small.second()
    grads.steps(42 - HO)
    small.third()
    sums[...] = small.result()


def run_block(tokens, segment, ln_gain, ln_bias, w_qkv, b_qkv, w_out, b_out, w_up, b_up, w_down,
              b_down, cotangent):
    exponent = jnp.arange(ROT // 2, dtype=F32) * (2.0 / ROT)
    inverse = jnp.tile(jnp.power(10000.0, -exponent), 8).reshape(1, 128)
    vmem = pl.BlockSpec(memory_space=pltpu.VMEM)
    hbm = pl.BlockSpec(memory_space=pl.ANY)
    V = pltpu.VMEM
    scratch = [
        V((3, 2048, 256), BF), V((256, 2048), BF), V((2048, 1024), BF), V((1024, 2048), BF),
        pltpu.SemaphoreType.DMA((4,)),
        V((2048, 1024), BF),
        V((1024, 1024), F32), V((1024, 1024), F32),
        V((3, 1024, 256), F32),
        V((3, 1024, 256), BF), V((3, 256, 1024), BF),
        V((1024, 1024), BF), V((1024, 1024), BF),
        V((1024, 256), BF), V((256, 1024), BF),
        V((1024, 256), BF), V((256, 1024), BF),
        V((3, 1024, 256), BF),
        V((1024, 128), F32), V((1024, 128), F32),
        V((1024, 128), F32), V((8, 1024), F32),
        V((8, 1024), F32),
        V((1024, 256), F32), V((1024, 256), F32), V((1024, 256), F32),
        V((4, 256, 256), BF), V((4, 256, 256), BF),
        V((128, 2048), F32), V((128, 128), F32), V((8, 128, 256), F32),
    ] + GradSum.scratch() + Gather.scratch() + RowSum.scratch() + SmallSum.scratch()
    return pl.pallas_call(
        block_kernel,
        out_shape=(
            jax.ShapeDtypeStruct((NP, 1024, 256), BF),
            jax.ShapeDtypeStruct((128, 2048), BF),
            jax.ShapeDtypeStruct((128, 2048), BF),
            jax.ShapeDtypeStruct((8, 1024), F32),
        ),
        in_specs=[vmem] * 10 + [hbm] * 4,
        out_specs=(hbm, vmem, vmem, vmem),
        scratch_shapes=scratch,
        compiler_params=pltpu.CompilerParams(
            collective_id=0, has_side_effects=True, vmem_limit_bytes=VMEM_LIMIT),
        cost_estimate=pl.CostEstimate(flops=50 * 10**9, bytes_accessed=30 << 20, transcendentals=10**7),
    )(
        tokens, cotangent, segment.reshape(1, 1024), inverse, ln_gain.reshape(1, 2048),
        ln_bias.reshape(1, 2048), b_qkv, b_out.reshape(1, 2048), b_up.reshape(1, 1024),
        b_down.reshape(1, 2048), w_qkv.transpose(1, 0, 2), w_out, w_up, w_down,
    )


def widen_kernel(piece, down, out, up, qkv):
    i = pl.program_id(0)
    value = piece[0]

    @pl.when(i < 8)
    def _():
        down[...] = value.astype(F32)

    @pl.when((i >= 8) & (i < 10))
    def _():
        for j in range(4):
            out[:, j * 256:j * 256 + 256] = piece[0, j * 256:j * 256 + 256, :].astype(F32)

    @pl.when((i >= 10) & (i < 18))
    def _():
        up[...] = value.astype(F32)

    @pl.when(i >= 18)
    def _():
        qkv[0] = value.astype(F32)


def widen(pieces):
    down, out, up, qkv = pl.pallas_call(
        widen_kernel,
        grid=(NP,),
        out_shape=(
            jax.ShapeDtypeStruct((1024, 2048), F32),
            jax.ShapeDtypeStruct((256, 2048), F32),
            jax.ShapeDtypeStruct((2048, 1024), F32),
            jax.ShapeDtypeStruct((3, 2048, 256), F32),
        ),
        in_specs=[pl.BlockSpec((1, 1024, 256), lambda i: (i, 0, 0))],
        out_specs=(
            pl.BlockSpec((1024, 256), lambda i: (0, jnp.minimum(i, 7))),
            pl.BlockSpec((256, 1024), lambda i: (0, jnp.clip(i - 8, 0, 1))),
            pl.BlockSpec((1024, 256), lambda i: (jnp.clip(i - 10, 0, 7) % 2, jnp.clip(i - 10, 0, 7) // 2)),
            pl.BlockSpec((1, 1024, 256), lambda i: (jnp.clip(i - 18, 0, 5) // 2, jnp.clip(i - 18, 0, 5) % 2, 0)),
        ),
        compiler_params=pltpu.CompilerParams(vmem_limit_bytes=32 << 20),
    )(pieces)
    return down, out, up, qkv.transpose(1, 0, 2)


def on_device(*args):
    pieces, output, input_grad, sums = run_block(*args)
    grad_w_down, grad_w_out, grad_w_up, grad_w_qkv = widen(pieces)
    wide = sums[:6].reshape(3, 2048)
    bias_total = wide[2]
    return (
        output, input_grad, wide[0], wide[1], grad_w_qkv, sums[7, :768].reshape(3, 256), grad_w_out,
        bias_total, grad_w_up, sums[6], grad_w_down, bias_total,
    )


def solution(mesh):
    placed = (
        P(("dp", "tensor"), None),
        P("dp"),
        P(),
        P(),
        P(None, None, "tensor"),
        P(None, "tensor"),
        P("tensor", None),
        P(),
        P(None, "tensor"),
        P("tensor"),
        P("tensor", None),
        P(),
        P(("dp", "tensor"), None),
    )
    return jax.shard_map(
        on_device,
        mesh=mesh,
        in_specs=placed,
        out_specs=(
            P(("dp", "tensor"), None),
            P(("dp", "tensor"), None),
            P(),
            P(),
            P(None, None, "tensor"),
            P(None, "tensor"),
            P("tensor", None),
            P(),
            P(None, "tensor"),
            P("tensor"),
            P("tensor", None),
            P(),
        ),
        check_vma=False,
    )
```

time: 672 us -> 289 us (0.43)
  blocking collectives: 129 us -> 0 us
  matrix products: 98.2 us -> 0 us
  waiting for transfers between devices: 90.5 us -> 0 us
  Pallas kernels: 209 us -> 268 us
  local copies, waits for them, and re-layouts: 73.1 us -> 18.6 us
  other arithmetic: 52.2 us -> 0.01 us
  between operations: 14.6 us -> 0.68 us
    psum x2 -> x0, blocking collectives: 129 us -> none  [the longest x1 67.6 us: on_device(): lax.psum((gain_part, shift_part), ('dp', 'tensor'))]
    dot_general x24 -> x0, matrix products: 98.2 us -> none  [the longest x1 10.6 us: on_device(): jnp.einsum('td,fd->tf', grad_rows, w_down, preferred_element_type=jnp.flo...]
    all_gather x2 -> x0, waiting for transfers between devices: 89.8 us -> none  [the longest x1 49 us: on_device(): gathered = lax.all_gather(normed, 'tensor', axis=0, tiled=True)]
    pallas_call x1 -> x2, Pallas kernels: 209 us -> 268 us  [the longest x1 254 us: run_block(): pl.pallas_call(block_kernel, out_shape=(jax.ShapeDtypeStruct((NP, 1024, 2...]
    convert_element_type x13 -> x0, other arithmetic: 24.2 us -> none  [the longest x1 7.31 us: from_pieces(): down = total[:8].transpose(1, 0, 2).reshape(1024, 2048).astype(F32)]
    convert_element_type x4 -> x0, local copies, waits for them, and re-layouts: 21.8 us -> none  [the longest x1 9.12 us: from_pieces(): down = total[:8].transpose(1, 0, 2).reshape(1024, 2048).astype(F32)]
    unnamed x96 -> x13, local copies, waits for them, and re-layouts: 22.6 us -> 8.25 us
    reshape x4 -> x5, local copies, waits for them, and re-layouts: 19.4 us -> 6.44 us  [the longest x1 1.29 us: run_block(): ln_gain.reshape(1, 2048)]
  transfers between devices with their start and end apart: 4 -> 0, of which waited for: 2 -> 0; matrix products, arithmetic and copies ran while one was open for 20% -> 0% of each run, Pallas kernels for 31% -> 0%
where the time goes in v2:
time: 289 us; the launch traced here: 288 us
  Pallas kernels  268 us (93%)
  local copies, waits for them, and re-layouts  18.6 us (6%)
    pallas_call x1, Pallas kernels, run_block(): pl.pallas_call(block_kernel, out_shape=(jax.ShapeDtypeStruct((NP, 1024, 2...  254 us
    pallas_call x1, Pallas kernels, widen(): pl.pallas_call(widen_kernel, grid=(NP,), out_shape=(jax.ShapeDtypeStruct(...  14.3 us
    unnamed x13, local copies, waits for them, and re-layouts  8.25 us

profile of v2, /device:TPU:1, one launch (start us, length us, event | category | flops | bytes accessed | tf_op | source)
XLA Modules:
  0.0 287.6 jit_solution(898426874050014191)
XLA Ops:
  0.7 0.6 reshape_tile.3.inverse
  1.3 1.3 reshape.59.b_up
  2.5 1.3 reshape.56.gain
  3.8 1.3 reshape.57.shift
  5.1 1.3 reshape.58.b_out
  6.4 1.3 reshape.60.b_down
  7.7 254.0 %shard_map.220 = (bf16[24,1024,256]{2,1,0:T(8,128)(2,1)}, bf16[128,2048]{1,0:T(8,128)(2,1)}, bf16[128,2048]{1,0:T(8,128)(2,1)}, f32[8,1024]{1,0:T(8,128)}) custom-call(bf16[128,2048]{1,0:T(8,128)(2,1)} %tokens.1, bf16[128,2048]{1,0:T(8,128)(2,1)} %cotangent.1, s32[1,1024]{1,0:T(1,128)} %bitcast.21, f32[1,128]{1,0:T(1,128)} %reshape_tile.3.inverse, ...), custom_call_target="tpu_custom_call" | custom-call | flops 49999998976 | bytes 31457280 | tf_op jit(solution)/shard_map/pallas_call | solution.py:843
  261.7 0.8 slice_reduce_fusion
  262.4 0.6 reshape_squeeze.3
  263.0 1.4 slice.26
  264.4 0.9 slice_bitcast_fusion
  265.3 0.6 copy_bitcast_fusion
  265.9 0.0 copy-start.3
  265.9 0.6 copy.31
  266.5 4.6 %copy-done = bf16[24,1024,256]{2,1,0:T(8,128)(2,1)S(1)} copy-done((bf16[24,1024,256]{2,1,0:T(8,128)(2,1)S(1)}, bf16[24,1024,256]{2,1,0:T(8,128)(2,1)}, u32[]{:S(2)}) %copy-start) | copy-done | bytes 12582936
  271.0 0.0 copy-start.2
  271.0 0.0 copy-start.1
  271.0 14.3 %shard_map.221 = (f32[1024,2048]{1,0:T(8,128)}, f32[256,2048]{1,0:T(8,128)}, f32[2048,1024]{1,0:T(8,128)}, f32[3,2048,256]{2,1,0:T(8,128)}) custom-call(bf16[24,1024,256]{2,1,0:T(8,128)(2,1)S(1)} %copy-done), custom_call_target="tpu_custom_call" | custom-call | tf_op jit(solution)/shard_map/pallas_call | solution.py:887
  285.4 0.0 copy-done.3
  285.4 0.6 copy.35
  286.0 0.0 copy-done.2
  286.0 0.8 copy.36
  286.8 0.0 copy-done.1
  286.8 0.8 copy.37
  (3 shorter events, 0.0 us)
Async XLA Ops:
  265.9 19.5 %copy-start.3 = (f32[2048]{0:T(1024)}, f32[2048]{0:T(1024)S(1)}, u32[]{:S(2)}) copy-start(f32[2048]{0:T(1024)S(1)} %get-tuple-element.76) | copy-start | bytes 24580
  266.5 4.6 %copy-start = (bf16[24,1024,256]{2,1,0:T(8,128)(2,1)S(1)}, bf16[24,1024,256]{2,1,0:T(8,128)(2,1)}, u32[]{:S(2)}) copy-start(bf16[24,1024,256]{2,1,0:T(8,128)(2,1)} %get-tuple-element.23.piece) | copy-start | bytes 37748740
  271.0 14.9 %copy-start.2 = (bf16[128,2048]{1,0:T(8,128)(2,1)S(1)}, bf16[128,2048]{1,0:T(8,128)(2,1)}, u32[]{:S(2)}) copy-start(bf16[128,2048]{1,0:T(8,128)(2,1)} %get-tuple-element.69) | copy-start | bytes 1572868
  271.0 15.7 %copy-start.1 = (bf16[128,2048]{1,0:T(8,128)(2,1)S(1)}, bf16[128,2048]{1,0:T(8,128)(2,1)}, u32[]{:S(2)}) copy-start(bf16[128,2048]{1,0:T(8,128)(2,1)} %get-tuple-element.70) | copy-start | bytes 1572868

commit v3 on v2

v3 whole, which is shorter than its diff:
```python
import jax
import jax.numpy as jnp
from jax import lax
from jax.experimental import pallas as pl
from jax.experimental.pallas import tpu as pltpu
from jax.sharding import PartitionSpec as P

HEAD_DIM = 64
ROT = 32
EPSILON = 1e-05
MESH = pl.DeviceIdType.MESH
BF = jnp.bfloat16
F32 = jnp.float32
NP = 24
VMEM_LIMIT = 64 << 20


def neighbours():
    dp = lax.axis_index("dp")
    tensor = lax.axis_index("tensor")
    y, zh, core = dp // 4, (dp // 2) % 2, dp % 2
    zl, x = tensor // 4, tensor % 4
    yl, yr, yo = (y + 3) % 4, (y + 1) % 4, (y + 2) % 4
    xl, xr, xo = (x + 3) % 4, (x + 1) % 4, (x + 2) % 4
    where = dict(y=y, core=core, zl=zl, x=x, yl=yl, yr=yr, yo=yo, xl=xl, xr=xr, xo=xo)
    where["dev_yl"] = (yl * 4 + zh * 2 + core, tensor)
    where["dev_yr"] = (yr * 4 + zh * 2 + core, tensor)
    where["dev_zh"] = (y * 4 + (1 - zh) * 2 + core, tensor)
    where["dev_core"] = (y * 4 + zh * 2 + 1 - core, tensor)
    where["dev_xl"] = (dp, zl * 4 + xl)
    where["dev_xr"] = (dp, zl * 4 + xr)
    where["dev_zl"] = (dp, (1 - zl) * 4 + x)
    return where


def greet(devices):
    barrier = pltpu.get_barrier_semaphore()
    for device in devices:
        pl.semaphore_signal(barrier, inc=1, device_id=device, device_id_type=MESH)
    pl.semaphore_wait(barrier, len(devices))


def rcopy(src, dst, send, recv, device):
    return pltpu.make_async_remote_copy(
        src_ref=src, dst_ref=dst, send_sem=send, recv_sem=recv, device_id=device, device_id_type=MESH
    )


def rows_at(index, size, count=None):
    return pl.ds(pl.multiple_of(index * size, size), size if count is None else count)


class GradSum:
    def scratch():
        return [
            pltpu.VMEM((2, 1024, 256), BF),
            pltpu.VMEM((2, 512, 256), BF),
            pltpu.VMEM((4, 512, 256), BF),
            pltpu.VMEM((4, 2, 64, 256), BF),
            pltpu.VMEM((4, 2, 128, 256), BF),
            pltpu.VMEM((4, 128, 256), BF),
            pltpu.VMEM((4, 128, 256), BF),
            pltpu.VMEM((4, 128, 256), BF),
            pltpu.SemaphoreType.DMA((11, 8)),
            pltpu.SemaphoreType.DMA((11, 8)),
            pltpu.SemaphoreType.DMA((8,)),
        ]

    def __init__(self, at, out, scratch):
        self.at, self.out = at, out
        (self.own, self.other, self.half, self.r1, self.r2, self.zs, self.zr, self.full,
         self.send, self.recv, self.local) = scratch

    def core_copy(self, p):
        s, at = p % 4, self.at
        return rcopy(self.own.at[p % 2, rows_at(1 - at["core"], 512)], self.other.at[p % 2],
                     self.send.at[0, p % 8], self.recv.at[0, p % 8], at["dev_core"])

    def first_copies(self, p):
        s, at = p % 4, self.at
        top = self.half.at[s, rows_at(at["yo"], 128, 64)]
        low = self.half.at[s, pl.ds(pl.multiple_of(at["yo"] * 128 + 64, 64), 64)]
        return (rcopy(top, self.r1.at[s, 0], self.send.at[1, p % 8], self.recv.at[1, p % 8], at["dev_yr"]),
                rcopy(low, self.r1.at[s, 1], self.send.at[2, p % 8], self.recv.at[2, p % 8], at["dev_yl"]))

    def second_copies(self, p):
        s, at = p % 4, self.at
        return (rcopy(self.half.at[s, rows_at(at["yr"], 128)], self.r2.at[s, 0],
                      self.send.at[3, p % 8], self.recv.at[3, p % 8], at["dev_yr"]),
                rcopy(self.half.at[s, rows_at(at["yl"], 128)], self.r2.at[s, 1],
                      self.send.at[4, p % 8], self.recv.at[4, p % 8], at["dev_yl"]))

    def z_copy(self, p):
        s = p % 4
        return rcopy(self.zs.at[s], self.zr.at[s], self.send.at[5, p % 8], self.recv.at[5, p % 8],
                     self.at["dev_zh"])

    def back_first(self, p):
        s, at = p % 4, self.at
        mine = self.out.at[p, rows_at(at["core"] * 4 + at["y"], 128)]
        return (rcopy(self.full.at[s], mine, self.send.at[6, p % 8], self.recv.at[6, p % 8], at["dev_yr"]),
                rcopy(self.full.at[s], mine, self.send.at[7, p % 8], self.recv.at[7, p % 8], at["dev_yl"]),
                pltpu.make_async_copy(self.full.at[s], mine, self.local.at[p % 8]))

    def back_second(self, p):
        s, at = p % 4, self.at
        top = self.out.at[p, rows_at(at["core"] * 4 + at["yl"], 128, 64)]
        low = self.out.at[p, pl.ds(pl.multiple_of((at["core"] * 4 + at["yr"]) * 128 + 64, 64), 64)]
        return (rcopy(top, top, self.send.at[9, p % 8], self.recv.at[9, p % 8], at["dev_yr"]),
                rcopy(low, low, self.send.at[10, p % 8], self.recv.at[10, p % 8], at["dev_yl"]))

    def back_core(self, p):
        s, at = p % 4, self.at
        mine = self.out.at[p, rows_at(at["core"], 512)]
        return rcopy(mine, mine, self.send.at[8, p % 8], self.recv.at[8, p % 8], at["dev_core"])

    def send_piece(self, p):
        self.core_copy(p).start()

    def add_core(self, p):
        s = p % 4
        self.core_copy(p).wait()

        @pl.loop(0, 4)
        def _(j):
            rows = rows_at(j, 128)
            mine = self.own[p % 2, pl.ds(pl.multiple_of(self.at["core"] * 512 + j * 128, 128), 128)]
            self.half[s, rows] = (mine.astype(F32) + self.other[p % 2, rows].astype(F32)).astype(BF)

        for copy in self.first_copies(p):
            copy.start()

    def add_first(self, p):
        s, at = p % 4, self.at
        for copy in self.first_copies(p):
            copy.wait()
        top = rows_at(at["yr"], 128, 64)
        low = pl.ds(pl.multiple_of(at["yl"] * 128 + 64, 64), 64)
        self.half[s, top] = (self.half[s, top].astype(F32) + self.r1[s, 0].astype(F32)).astype(BF)
        self.half[s, low] = (self.half[s, low].astype(F32) + self.r1[s, 1].astype(F32)).astype(BF)
        for copy in self.second_copies(p):
            copy.start()

    def add_second(self, p):
        s = p % 4
        for copy in self.second_copies(p):
            copy.wait()
        mine = self.half[s, rows_at(self.at["y"], 128)].astype(F32)
        self.zs[s] = (mine + self.r2[s, 0].astype(F32) + self.r2[s, 1].astype(F32)).astype(BF)
        self.z_copy(p).start()

    def add_z(self, p):
        s = p % 4
        self.z_copy(p).wait()
        self.full[s] = (self.zs[s].astype(F32) + self.zr[s].astype(F32)).astype(BF)
        for copy in self.back_first(p):
            copy.start()

    def forward_y(self, p):
        for copy in self.back_first(p):
            copy.wait()
        for copy in self.back_second(p):
            copy.start()

    def forward_core(self, p):
        for copy in self.back_second(p):
            copy.wait()
        self.back_core(p).start()

    def finish(self, p):
        self.back_core(p).wait()

    def steps(self, t):
        for lag, step in ((1, self.add_core), (2, self.add_first), (3, self.add_second), (4, self.add_z),
                          (6, self.forward_y), (8, self.forward_core), (9, self.finish)):
            p = t - lag
            pl.when((p >= 0) & (p < NP))(lambda step=step, p=p: step(p))


def dot(a, b):
    return lax.dot_general(a, b, (((1,), (0,)), ((), ())), preferred_element_type=F32)


def dot_nt(a, b):
    return lax.dot_general(a, b, (((1,), (1,)), ((), ())), preferred_element_type=F32)


def at_rows(index, size=256):
    return pl.ds(pl.multiple_of(index * size, size), size)


class Gather:
    AHEAD = 2

    def scratch():
        return [
            pltpu.VMEM((16, 128, 256), BF),
            pltpu.VMEM((8, 1024, 256), BF),
            pltpu.SemaphoreType.DMA((9, 8)),
            pltpu.SemaphoreType.DMA((9, 8)),
        ]

    def __init__(self, at, scratch):
        self.at = at
        self.own, self.all, self.send, self.recv = scratch

    def copy(self, kind, c, src, dst, device):
        s = c % 8
        return rcopy(src, dst, self.send.at[kind, s], self.recv.at[kind, s], self.at[device])

    def part(self, c, zl, x, begin=0, count=128):
        first = pl.multiple_of((zl * 4 + x) * 128 + begin, 64)
        return self.all.at[c % 8, pl.ds(first, count)]

    def same(self, kind, c, block, device):
        return self.copy(kind, c, block, block, device)

    def first(self, c, wide):
        at = self.at
        src, dst = self.own.at[c], self.part(c, at["zl"], at["x"])
        copies = [self.copy(0, c, src, dst, "dev_xr"), self.copy(1, c, src, dst, "dev_xl")]
        return copies if wide else copies + [self.copy(2, c, src, dst, "dev_zl")]

    def ring(self, c):
        at = self.at
        return [self.same(3, c, self.part(c, at["zl"], at["xl"], 0, 64), "dev_xr"),
                self.same(4, c, self.part(c, at["zl"], at["xr"], 64, 64), "dev_xl")]

    def second(self, c, wide):
        at = self.at
        if wide:
            return [self.copy(5, c, self.own.at[c], self.part(c, at["zl"], at["x"]), "dev_zl"),
                    self.same(6, c, self.part(c, at["zl"], at["xl"]), "dev_zl"),
                    self.same(7, c, self.part(c, at["zl"], at["xr"]), "dev_zl")]
        other = self.part(c, 1 - at["zl"], at["x"])
        return [self.same(5, c, other, "dev_xr"), self.same(6, c, other, "dev_xl")]

    def third(self, c, wide):
        at = self.at
        if wide:
            return [self.same(8, c, self.part(c, at["zl"], at["xo"]), "dev_zl")]
        return [self.same(7, c, self.part(c, 1 - at["zl"], at["xl"], 0, 64), "dev_xr"),
                self.same(8, c, self.part(c, 1 - at["zl"], at["xr"], 64, 64), "dev_xl")]

    def begin(self, c):
        def start(wide):
            for copy in self.first(c, wide):
                copy.start()

        self.either(c, start)
        self.part(c, self.at["zl"], self.at["x"])[...] = self.own[c]

    def either(self, c, step):
        wide = (c % 2 == 1) & (c < WIDE)
        pl.when((c >= 0) & (c < 16) & wide)(lambda: step(True))
        pl.when((c >= 0) & (c < 16) & jnp.logical_not(wide))(lambda: step(False))

    def steps(self, c):
        def second(wide):
            for copy in self.first(c, wide):
                copy.wait()
            for copy in self.ring(c) + self.second(c, wide):
                copy.start()

        def third(wide):
            for copy in self.ring(c - 1) if wide else self.ring(c - 1) + self.second(c - 1, wide):
                copy.wait()
            for copy in self.third(c - 1, wide):
                copy.start()

        def last(wide):
            for copy in self.second(c - 2, wide) + self.third(c - 2, wide) if wide else self.third(c - 2, wide):
                copy.wait()

        self.either(c, second)
        pl.when(c + self.AHEAD < 16)(lambda: self.begin(c + self.AHEAD))
        self.either(c - 1, third)
        self.either(c - 2, last)


class RowSum:
    def scratch():
        return [
            pltpu.VMEM((4, 2, 4, 128, 256), BF),
            pltpu.VMEM((8, 2, 2, 64, 256), BF),
            pltpu.VMEM((4, 2, 2, 128, 256), BF),
            pltpu.VMEM((4, 128, 256), BF),
            pltpu.VMEM((4, 128, 256), BF),
            pltpu.VMEM((4, 128, 256), F32),
            pltpu.SemaphoreType.DMA((5, 8)),
            pltpu.SemaphoreType.DMA((5, 8)),
        ]

    def __init__(self, at, scratch, result):
        self.at, self.result = at, result
        self.part, self.r1, self.r2, self.zs, self.zr, self.mine, self.send, self.recv = scratch

    def copy(self, kind, c, src, dst, device):
        s = c % 8
        return rcopy(src, dst, self.send.at[kind, s], self.recv.at[kind, s], device)

    def first(self, c):
        s, at = c % 4, self.at
        return [self.copy(0, c, self.part.at[s, :, at["xo"], pl.ds(0, 64)], self.r1.at[c % 8, 0], at["dev_xr"]),
                self.copy(1, c, self.part.at[s, :, at["xo"], pl.ds(64, 64)], self.r1.at[c % 8, 1], at["dev_xl"])]

    def second(self, c):
        s, at = c % 4, self.at
        return [self.copy(2, c, self.part.at[s, :, at["xr"]], self.r2.at[s, 0], at["dev_xr"]),
                self.copy(3, c, self.part.at[s, :, at["xl"]], self.r2.at[s, 1], at["dev_xl"])]

    def third(self, c):
        s = c % 4
        return [self.copy(4, c, self.zs.at[s], self.zr.at[s], self.at["dev_zl"])]

    def store(self, c, value):
        for k in range(8):
            self.part[c % 4, k // 4, k % 4] = value[k * 128:(k + 1) * 128].astype(BF)

    def send_chunk(self, c):
        for copy in self.first(c):
            copy.start()

    def add_first(self, c):
        s, at = c % 4, self.at
        for copy in self.first(c):
            copy.wait()
        for z in range(2):
            top = self.part[s, z, at["xr"], 0:64].astype(F32) + self.r1[c % 8, 0, z].astype(F32)
            self.part[s, z, at["xr"], 0:64] = top.astype(BF)
            low = self.part[s, z, at["xl"], 64:128].astype(F32) + self.r1[c % 8, 1, z].astype(F32)
            self.part[s, z, at["xl"], 64:128] = low.astype(BF)
        for copy in self.second(c):
            copy.start()

    def add_second(self, c):
        s, at = c % 4, self.at
        for copy in self.second(c):
            copy.wait()

        def total(z):
            own = self.part[s, z, at["x"]].astype(F32)
            return own + self.r2[s, 0, z].astype(F32) + self.r2[s, 1, z].astype(F32)

        self.zs[s] = total(1 - at["zl"]).astype(BF)
        for copy in self.third(c):
            copy.start()
        self.mine[s] = total(at["zl"])

    def add_third(self, c):
        s = c % 4
        for copy in self.third(c):
            copy.wait()
        self.result(c, self.mine[s] + self.zr[s].astype(F32))

    def steps(self, t):
        for lag, step in ((2, self.add_first), (3, self.add_second), (4, self.add_third)):
            c = t - lag
            pl.when((c >= 0) & (c < 8))(lambda step=step, c=c: step(c))
            pl.when((c >= 10) & (c < 18))(lambda step=step, c=c - 2: step(c))


class SmallSum:
    def scratch():
        return [
            pltpu.VMEM((8, 8, 1024), F32),
            pltpu.VMEM((4, 8, 1024), F32),
            pltpu.VMEM((4, 8, 1024), F32),
            pltpu.SemaphoreType.DMA((13,)),
            pltpu.SemaphoreType.DMA((13,)),
        ]

    def __init__(self, scratch):
        self.b1, self.b2, self.b3, self.send, self.recv = scratch
        dp, tensor = lax.axis_index("dp"), lax.axis_index("tensor")
        y, self.zh, core = dp // 4, (dp // 2) % 2, dp % 2
        self.zl, self.x = tensor // 4, tensor % 4
        self.i1 = y * 2 + core
        self.i2 = self.zh * 2 + self.zl
        self.d1, self.d2, self.d3 = [], [], []
        for k in range(1, 8):
            j = (self.i1 + k) % 8
            self.d1.append(((j // 2) * 4 + self.zh * 2 + j % 2, tensor))
        for k in range(1, 4):
            j = (self.i2 + k) % 4
            self.d2.append((y * 4 + (j // 2) * 2 + core, (j % 2) * 4 + self.x))
            self.d3.append((dp, self.zl * 4 + (self.x + k) % 4))

    def devices(self):
        return self.d1 + self.d2 + self.d3

    def copies(self, stage):
        buf, mine, devices, base = ((self.b1, self.i1, self.d1, 0), (self.b2, self.i2, self.d2, 7),
                                    (self.b3, self.x, self.d3, 10))[stage]
        return [rcopy(buf.at[mine], buf.at[mine], self.send.at[base + k], self.recv.at[base + k], device)
                for k, device in enumerate(devices)]

    def start(self, stage):
        for copy in self.copies(stage):
            copy.start()

    def wait(self, stage):
        for copy in self.copies(stage):
            copy.wait()

    def second(self):
        self.wait(0)
        total = self.b1[0]
        for k in range(1, 8):
            total = total + self.b1[k]
        self.b2[self.i2] = total
        self.start(1)

    def third(self):
        self.wait(1)
        wide = self.b2[0] + self.b2[1] + self.b2[2] + self.b2[3]
        narrow = self.b2[self.zl] + self.b2[2 + self.zl]
        row = lax.broadcasted_iota(jnp.int32, (8, 1024), 0)
        self.b3[self.x] = jnp.where(row < 6, wide, narrow)
        self.start(2)

    def result(self):
        self.wait(2)
        wide = self.b3[0] + self.b3[1] + self.b3[2] + self.b3[3]
        row = lax.broadcasted_iota(jnp.int32, (8, 1024), 0)
        return jnp.where(row < 6, wide, self.b3[self.x])


def gelu_parts(u):
    inner = 0.7978845608028654 * (u + 0.044715 * (u * u * u))
    return jnp.tanh(inner)


def swap_pairs(v):
    lane = lax.broadcasted_iota(jnp.int32, v.shape, 1)
    return jnp.where(lane % 32 < 16, pltpu.roll(v, 112, 1), pltpu.roll(v, 16, 1))


def turn(v, cosine, sine):
    return v * cosine + swap_pairs(v) * sine


WIDE = 14
RS = 8
FEAT, MID = 1792, 1280


def block_kernel(
    tokens, cotangent, seg_row, gain_h, shift_h, b_qkv, b_out_h, b_up_h, b_down_h,
    w_qkv_h, w_out_h, w_up_h, w_down_h,
    pieces, output, input_grad, sums,
    w_in, w_mid, w_sem,
    gain, shift, b_sum,
    normed_t, pre, grad_mid, rows, turned, mid, heads_t, outs_g, outs_gt, grad_feat,
    cos_t, sin_t, seg_c, seg_r, lse, bias, p_f, q_m, g_m, ds_b, mean_row, rstd,
    *scratch,
):
    at = neighbours()
    grad_n = p_f
    dp_f = grad_mid.at[:, pl.ds(0, 256)]
    act_t = grad_feat
    n1, n2, n3 = len(GradSum.scratch()), len(Gather.scratch()), len(RowSum.scratch())
    small = SmallSum(scratch[n1 + n2 + n3:])
    grads = GradSum(at, pieces, scratch[:n1])
    gather = Gather(at, scratch[n1:n1 + n2])

    def keep_rows(c, value):
        @pl.when(c < 8)
        def _():
            cols = at_rows(c)
            own = tokens[:, cols].astype(F32) + value + b_sum[0:1, cols]
            output[:, cols] = own.astype(BF)

        @pl.when(c >= 8)
        def _():
            grad_n[at_rows(c - 8, 128), :] = value

    row_sum = RowSum(at, scratch[n1 + n2:n1 + n2 + n3], keep_rows)

    moves = [(w_up_h, w_in.at[:, pl.ds(0, 1024)])]
    moves += [(w_qkv_h.at[k], w_in.at[:, pl.ds(1024 + 256 * k, 256)]) for k in range(3)]
    moves += [(w_down_h, w_mid.at[pl.ds(0, 1024)]), (w_out_h, w_mid.at[pl.ds(1024, 256)])]
    weights = [pltpu.make_async_copy(src, dst, w_sem.at[i]) for i, (src, dst) in enumerate(moves)]

    barrier = pltpu.get_barrier_semaphore()
    greeted = small.devices()
    for device in greeted:
        pl.semaphore_signal(barrier, inc=1, device_id=device, device_id_type=MESH)
    for copy in weights:
        copy.start()

    gain[...] = gain_h[...].astype(F32)
    shift[...] = shift_h[...].astype(F32)
    b_sum[...] = b_out_h[...].astype(F32) + b_down_h[...].astype(F32)
    x = tokens[...].astype(F32)
    mean = jnp.mean(x, axis=1, keepdims=True)
    centered = x - mean
    scale = lax.rsqrt(jnp.mean(centered * centered, axis=1, keepdims=True) + EPSILON)
    rstd[...] = jnp.broadcast_to(scale, (128, 128))
    mean_row[...] = jnp.broadcast_to(mean, (128, 128))

    def unit(cols):
        return (tokens[:, cols].astype(F32) - mean_row[:, 0:1]) * rstd[:, 0:1]

    for c in range(8):
        cols = slice(c * 256, c * 256 + 256)
        gather.own[c] = (unit(cols) * gain[0:1, cols] + shift[0:1, cols]).astype(BF)
        gather.own[8 + c] = cotangent[:, cols]

    pl.semaphore_wait(barrier, len(greeted))
    for c in range(Gather.AHEAD):
        gather.begin(c)

    seg_f = seg_row[...].astype(F32)
    seg_r[...] = jnp.broadcast_to(seg_f, (8, 1024))
    seg_c[...] = jnp.broadcast_to(seg_f, (128, 1024)).T
    @pl.loop(0, 4)
    def _(b):
        r = at_rows(b)
        i = lax.broadcasted_iota(jnp.int32, (256, 1024), 0) + b * 256
        j = lax.broadcasted_iota(jnp.int32, (256, 1024), 1)
        same = jnp.where((seg_c[r, 0:1] == seg_r[0:1, :]) & (j < i), 1.0, 0.0)
        position = jnp.sum(same, axis=1, keepdims=True)
        lane = lax.broadcasted_iota(jnp.int32, (256, 128), 1) % 64
        power = jnp.exp((lane % 16).astype(F32) * (-2.0 / ROT * 9.210340371976184))
        angle = position * power
        sine = jnp.sin(angle)
        cos_t[r, :] = jnp.where(lane < ROT, jnp.cos(angle), 1.0)
        sin_t[r, :] = jnp.where(lane < ROT // 2, -sine, jnp.where(lane < ROT, sine, 0.0))
        pre[r, 0:1024] = jnp.broadcast_to(b_up_h[...].astype(F32), (256, 1024))
        for k in range(3):
            cols = slice(1024 + k * 256, 1280 + k * 256)
            pre[r, cols] = jnp.broadcast_to(b_qkv[k:k + 1, :].astype(F32), (256, 256))

    @pl.loop(0, 10)
    def _(i):
        gather.steps(i)

        @pl.when(i == 2)
        def _():
            for copy in weights[:4]:
                copy.wait()

        @pl.when(i >= 2)
        def _():
            c = i - 2

            @pl.loop(0, 2)
            def _(b):
                r = at_rows(b, 512)
                a = gather.all[c % 8, r, :]
                pre[r, :] += dot(a, w_in[at_rows(c), :])
            normed_t[at_rows(c), :] = gather.all[c % 8].T

    @pl.loop(0, 4)
    def _(b):
        r = at_rows(b)
        for k in range(4):
            cols = slice(k * 256, k * 256 + 256)
            u = pre[r, cols]
            a = (u * (0.5 * (1.0 + gelu_parts(u)))).astype(BF)
            mid[r, cols] = a
            act_t[cols, r] = a.T

    for copy in weights[4:]:
        copy.wait()
    gather.steps(10)

    def make_rows(b):
        r = at_rows(b)
        for k in range(3):
            for half in range(2):
                v = pre[r, 1024 + k * 256 + half * 128:1152 + k * 256 + half * 128]
                if k < 2:
                    v = turn(v, cos_t[r, :], sin_t[r, :])
                if k == 0:
                    v = v * HEAD_DIM ** -0.5
                v = v.astype(BF)
                cols = slice(half * 128, half * 128 + 128)
                rows[k, r, cols] = v
                turned[k, cols, r] = v.T

    def attend_bias(qb):
        cols = slice(qb * 256, qb * 256 + 256)
        for kb in range(qb + 1):
            r = slice(kb * 256, kb * 256 + 256)
            keep = seg_c[r, 0:1] == seg_r[0:1, cols]
            if kb == qb:
                i = lax.broadcasted_iota(jnp.int32, (256, 256), 0)
                j = lax.broadcasted_iota(jnp.int32, (256, 256), 1)
                keep = keep & (i <= j)
            bias[r, :] = jnp.where(keep, 0.0, -1e30).astype(BF)

    def one_head(ref, source, h, cols):
        ref[...] = jnp.zeros_like(ref)
        ref[head_rows(h), :] = source[head_rows(h), cols]

    def head_rows(h):
        return pl.ds(pl.multiple_of(h * 64, 64), 64)

    def attend(qb):
        cols = slice(qb * 256, qb * 256 + 256)
        n = (qb + 1) * 256
        attend_bias(qb)

        @pl.loop(0, 4)
        def _(h):
            hr = head_rows(h)
            one_head(q_m, turned.at[0], h, cols)
            s = dot(rows[1, 0:n, :], q_m[...]) + bias[0:n, :].astype(F32)
            p_f[0:n, :] = s
            most = jnp.max(s, axis=0, keepdims=True)
            e = jnp.exp(p_f[0:n, :] - most)
            p_f[0:n, :] = e
            total = jnp.sum(e, axis=0, keepdims=True)
            ds_b[0:n, :] = (p_f[0:n, :] * (1.0 / total)).astype(BF)
            heads_t[hr, cols] = dot(
                turned[2, hr, 0:n], ds_b[0:n, :]).astype(BF)
            lse[pl.ds(h, 1), cols] = most + jnp.log(total)

    def attend_back(qb, first_head):
        cols = slice(qb * 256, qb * 256 + 256)
        n = (qb + 1) * 256
        if first_head == 0:
            attend_bias(qb)

        @pl.loop(first_head, first_head + 2)
        def _(h):
            hr = head_rows(h)
            one_head(q_m, turned.at[0], h, cols)
            one_head(g_m, outs_gt, h, cols)
            p = jnp.exp(dot(rows[1, 0:n, :], q_m[...]) + bias[0:n, :].astype(F32) - lse[pl.ds(h, 1), cols])
            p_f[0:n, :] = p
            d = dot(rows[2, 0:n, :], g_m[...])
            dp_f[0:n, :] = d
            delta = jnp.sum(p_f[0:n, :] * d, axis=0, keepdims=True)
            lane = lax.broadcasted_iota(jnp.int32, (256, 256), 1) // 64
            q_h = jnp.where(lane == h, rows[0, cols, :].astype(F32), 0.0).astype(BF)
            g_h = jnp.where(lane == h, outs_g[cols, :].astype(F32), 0.0).astype(BF)
            pre[0:n, 1536:1792] += dot(p_f[0:n, :].astype(BF), g_h)
            ds_b[0:n, :] = (p_f[0:n, :] * (dp_f[0:n, :] - delta)).astype(BF)
            pre[0:n, 1280:1536] += dot(ds_b[0:n, :], q_h)
            pre[pl.ds(pl.multiple_of(qb * 256 + h * 64, 64), 64), 1024:1280] = dot(
                turned[1, hr, 0:n], ds_b[0:n, :])

    @pl.loop(0, 8)
    def _(t):
        grads.steps(t)
        chunk = gather.all[t]
        grads.own[t % 2] = dot(act_t[:, 0:1024], chunk).astype(BF)
        grads.send_piece(t)
        gather.steps(11 + t)

        @pl.when(t == 0)
        def _():
            grad_mid[...] = jnp.zeros_like(grad_mid)

        @pl.loop(0, 2)
        def _(b):
            r = at_rows(b, 512)
            grad_mid[r, :] += dot_nt(gather.all[t, r, :], w_mid[:, at_rows(t)])

        pl.when(t < 4)(lambda: make_rows(t))
        for qb in range(4):
            pl.when(t == 4 + qb)(lambda qb=qb: attend(qb))

    def branch_chunk(c):
        row_sum.store(c, dot(mid[...], w_mid[:, at_rows(c)]))
        row_sum.send_chunk(c)

    def normed_chunk(c):
        row_sum.store(c + 8, dot_nt(grad_feat[...], w_in[at_rows(c), :]))
        row_sum.send_chunk(c + 8)

    @pl.loop(0, 4)
    def _(b):
        r = at_rows(b)
        mid[r, 1024:1280] = heads_t[:, r].T
        g = grad_mid[r, 1024:1280].astype(BF)
        outs_g[r, :] = g
        outs_gt[:, r] = g.T

    @pl.loop(8, 10)
    def _(t):
        grads.steps(t)
        row_sum.steps(t - RS)
        for j in range(4):
            r = slice(j * 256, j * 256 + 256)
            grads.own[t % 2, r, :] = dot(heads_t[...], gather.all[4 * (t - 8) + j]).astype(BF)
        grads.send_piece(t)
        branch_chunk(t - RS)

        @pl.loop(2 * (t - 8), 2 * (t - 8) + 2)
        def _(b):
            r = at_rows(b)
            for k in range(4):
                cols = slice(k * 256, k * 256 + 256)
                u = pre[r, cols]
                th = gelu_parts(u)
                slope = 0.5 * (1.0 + th) + 0.5 * u * (1.0 - th * th) * (
                    0.7978845608028654 * (1.0 + 3 * 0.044715 * (u * u)))
                grad_feat[r, cols] = (slope * grad_mid[r, cols]).astype(BF)
            pre[r, 1024:1792] = jnp.zeros((256, 768), F32)

    def feature_piece(t):
        q = t - 10
        grads.own[t % 2] = dot(
            normed_t[at_rows(q % 2, 1024), :], grad_feat[:, at_rows(q // 2)]).astype(BF)
        grads.send_piece(t)

    @pl.loop(10, 18)
    def _(t):
        grads.steps(t)
        row_sum.steps(t - RS)
        feature_piece(t)
        pl.when(t < RS + 8)(lambda: branch_chunk(t - RS))
        for qb in range(4):
            for half in range(2):
                pl.when(t == 10 + 2 * qb + half)(lambda qb=qb, half=half: attend_back(qb, 2 * half))

    for b in range(4):
        r = slice(b * 256, b * 256 + 256)
        grad_q = pre[r, 1024:1280].T * HEAD_DIM ** -0.5
        for half in range(2):
            a = half * 128
            cosine, sine = cos_t[r, :], -sin_t[r, :]
            grad_feat[r, 1024 + a:1152 + a] = turn(grad_q[:, a:a + 128], cosine, sine).astype(BF)
            grad_feat[r, 1280 + a:1408 + a] = turn(pre[r, 1280 + a:1408 + a], cosine, sine).astype(BF)
        grad_feat[r, 1536:1792] = pre[r, 1536:1792].astype(BF)

    @pl.loop(18, 24)
    def _(t):
        grads.steps(t)
        row_sum.steps(t - RS)
        feature_piece(t)
        normed_chunk(t - 18)

    @pl.loop(24, 30)
    def _(t):
        grads.steps(t)
        row_sum.steps(t - RS)
        pl.when(t < 26)(lambda: normed_chunk(t - 18))

    def column_sum(value):
        return jnp.sum(value.astype(F32), axis=0, keepdims=True)

    mine = small.i1
    small.b1[mine] = jnp.zeros((8, 1024), F32)
    mean_plain = jnp.zeros((128, 1), F32)
    mean_unit = jnp.zeros((128, 1), F32)
    for c in range(8):
        cols = slice(c * 256, c * 256 + 256)
        row, lanes = c // 4, slice((c % 4) * 256, (c % 4) * 256 + 256)
        g = grad_n[c * 128:c * 128 + 128, :]
        n = unit(cols)
        scaled = g * gain[0:1, cols]
        mean_plain = mean_plain + jnp.sum(scaled, axis=1, keepdims=True)
        mean_unit = mean_unit + jnp.sum(scaled * n, axis=1, keepdims=True)
        small.b1[mine, row:row + 1, lanes] = column_sum(g * n)
        small.b1[mine, 2 + row:3 + row, lanes] = column_sum(g)
        small.b1[mine, 4 + row:5 + row, lanes] = column_sum(cotangent[:, cols])
    for k in range(7):
        row, lanes = 6 + k // 4, slice((k % 4) * 256, (k % 4) * 256 + 256)
        small.b1[mine, row:row + 1, lanes] = column_sum(grad_feat[:, k * 256:k * 256 + 256])
    small.start(0)
    grads.steps(30)
    mean_plain = mean_plain / 2048.0
    mean_unit = mean_unit / 2048.0
    for c in range(8):
        cols = slice(c * 256, c * 256 + 256)
        inner = grad_n[c * 128:c * 128 + 128, :] * gain[0:1, cols] - mean_plain - unit(cols) * mean_unit
        input_grad[:, cols] = (cotangent[:, cols].astype(F32) + rstd[:, 0:1] * inner).astype(BF)

    small.second()
    grads.steps(31)
    small.third()
    grads.steps(32)
    sums[...] = small.result()


def run_block(tokens, segment, ln_gain, ln_bias, w_qkv, b_qkv, w_out, b_out, w_up, b_up, w_down,
              b_down, cotangent):
    vmem = pl.BlockSpec(memory_space=pltpu.VMEM)
    hbm = pl.BlockSpec(memory_space=pl.ANY)
    V = pltpu.VMEM
    scratch = [
        V((2048, FEAT), BF), V((MID, 2048), BF), pltpu.SemaphoreType.DMA((6,)),
        V((1, 2048), F32), V((1, 2048), F32), V((1, 2048), F32),
        V((2048, 1024), BF),
        V((1024, FEAT), F32), V((1024, MID), F32),
        V((3, 1024, 256), BF), V((3, 256, 1024), BF),
        V((1024, MID), BF), V((256, 1024), BF),
        V((1024, 256), BF), V((256, 1024), BF),
        V((1024, FEAT), BF),
        V((1024, 128), F32), V((1024, 128), F32),
        V((1024, 128), F32), V((8, 1024), F32),
        V((8, 1024), F32),
        V((1024, 256), BF), V((1024, 256), F32),
        V((256, 256), BF), V((256, 256), BF), V((1024, 256), BF),
        V((128, 128), F32), V((128, 128), F32),
    ] + GradSum.scratch() + Gather.scratch() + RowSum.scratch() + SmallSum.scratch()
    return pl.pallas_call(
        block_kernel,
        out_shape=(
            jax.ShapeDtypeStruct((NP, 1024, 256), BF),
            jax.ShapeDtypeStruct((128, 2048), BF),
            jax.ShapeDtypeStruct((128, 2048), BF),
            jax.ShapeDtypeStruct((8, 1024), F32),
        ),
        in_specs=[vmem] * 9 + [hbm] * 4,
        out_specs=(hbm, vmem, vmem, vmem),
        scratch_shapes=scratch,
        compiler_params=pltpu.CompilerParams(
            collective_id=0, has_side_effects=True, vmem_limit_bytes=VMEM_LIMIT),
        cost_estimate=pl.CostEstimate(flops=50 * 10**9, bytes_accessed=30 << 20, transcendentals=10**7),
    )(
        tokens, cotangent, segment.reshape(1, 1024), ln_gain.reshape(1, 2048),
        ln_bias.reshape(1, 2048), b_qkv, b_out.reshape(1, 2048), b_up.reshape(1, 1024),
        b_down.reshape(1, 2048), w_qkv.transpose(1, 0, 2), w_out, w_up, w_down,
    )


def widen_kernel(piece, down, out, up, qkv):
    i = pl.program_id(0)
    value = piece[0]

    @pl.when(i < 8)
    def _():
        down[...] = value.astype(F32)

    @pl.when((i >= 8) & (i < 10))
    def _():
        for j in range(4):
            out[:, j * 256:j * 256 + 256] = piece[0, j * 256:j * 256 + 256, :].astype(F32)

    @pl.when((i >= 10) & (i < 18))
    def _():
        up[...] = value.astype(F32)

    @pl.when(i >= 18)
    def _():
        qkv[0] = value.astype(F32)


def widen(pieces):
    down, out, up, qkv = pl.pallas_call(
        widen_kernel,
        grid=(NP,),
        out_shape=(
            jax.ShapeDtypeStruct((1024, 2048), F32),
            jax.ShapeDtypeStruct((256, 2048), F32),
            jax.ShapeDtypeStruct((2048, 1024), F32),
            jax.ShapeDtypeStruct((3, 2048, 256), F32),
        ),
        in_specs=[pl.BlockSpec((1, 1024, 256), lambda i: (i, 0, 0))],
        out_specs=(
            pl.BlockSpec((1024, 256), lambda i: (0, jnp.minimum(i, 7))),
            pl.BlockSpec((256, 1024), lambda i: (0, jnp.clip(i - 8, 0, 1))),
            pl.BlockSpec((1024, 256), lambda i: (jnp.clip(i - 10, 0, 7) % 2, jnp.clip(i - 10, 0, 7) // 2)),
            pl.BlockSpec((1, 1024, 256), lambda i: (jnp.clip(i - 18, 0, 5) // 2, jnp.clip(i - 18, 0, 5) % 2, 0)),
        ),
        compiler_params=pltpu.CompilerParams(vmem_limit_bytes=VMEM_LIMIT),
    )(pieces)
    return down, out, up, qkv.transpose(1, 0, 2)


def on_device(*args):
    pieces, output, input_grad, sums = run_block(*args)
    grad_w_down, grad_w_out, grad_w_up, grad_w_qkv = widen(pieces)
    wide = sums[:6].reshape(3, 2048)
    bias_total = wide[2]
    return (
        output, input_grad, wide[0], wide[1], grad_w_qkv, sums[7, :768].reshape(3, 256), grad_w_out,
        bias_total, grad_w_up, sums[6], grad_w_down, bias_total,
    )


def solution(mesh):
    placed = (
        P(("dp", "tensor"), None),
        P("dp"),
        P(),
        P(),
        P(None, None, "tensor"),
        P(None, "tensor"),
        P("tensor", None),
        P(),
        P(None, "tensor"),
        P("tensor"),
        P("tensor", None),
        P(),
        P(("dp", "tensor"), None),
    )
    return jax.shard_map(
        on_device,
        mesh=mesh,
        in_specs=placed,
        out_specs=(
            P(("dp", "tensor"), None),
            P(("dp", "tensor"), None),
            P(),
            P(),
            P(None, None, "tensor"),
            P(None, "tensor"),
            P("tensor", None),
            P(),
            P(None, "tensor"),
            P("tensor"),
            P("tensor", None),
            P(),
        ),
        check_vma=False,
    )
```

time: 289 us -> 243 us (0.84)
  Pallas kernels: 268 us -> 225 us
    pallas_call x1, Pallas kernels: 254 us -> 204 us  [run_block(): pl.pallas_call(block_kernel, out_shape=(jax.ShapeDtypeStruct((NP, 1024, 2...]
    pallas_call x1, Pallas kernels: 14.3 us -> 21.3 us  [widen(): pl.pallas_call(widen_kernel, grid=(NP,), out_shape=(jax.ShapeDtypeStruct(...]
    unnamed x13 -> x5, local copies, waits for them, and re-layouts: 8.25 us -> 6.53 us
where the time goes in v3:
time: 243 us; the launch traced here: 242 us
  Pallas kernels  225 us (93%)
  local copies, waits for them, and re-layouts  16.3 us (7%)
    pallas_call x1, Pallas kernels, run_block(): pl.pallas_call(block_kernel, out_shape=(jax.ShapeDtypeStruct((NP, 1024, 2...  204 us
    pallas_call x1, Pallas kernels, widen(): pl.pallas_call(widen_kernel, grid=(NP,), out_shape=(jax.ShapeDtypeStruct(...  21.3 us
    unnamed x5, local copies, waits for them, and re-layouts  6.53 us

profile of v3, /device:TPU:1, one launch (start us, length us, event | category | flops | bytes accessed | tf_op | source)
XLA Modules:
  0.0 242.1 jit_solution(2466900522835299302)
XLA Ops:
  0.6 1.3 reshape.53.b_up_h
  1.9 1.3 reshape.50.gain_h
  3.2 1.3 reshape.51.shift_h
  4.5 1.3 reshape.52.b_out_h
  5.8 1.3 reshape.54.b_down_h
  7.1 203.8 %shard_map.220 = (bf16[24,1024,256]{2,1,0:T(8,128)(2,1)}, bf16[128,2048]{1,0:T(8,128)(2,1)}, bf16[128,2048]{1,0:T(8,128)(2,1)}, f32[8,1024]{1,0:T(8,128)}) custom-call(bf16[128,2048]{1,0:T(8,128)(2,1)} %tokens.1, bf16[128,2048]{1,0:T(8,128)(2,1)} %cotangent.1, s32[1,1024]{1,0:T(1,128)} %bitcast.21, bf16[1,2048]{1,0:T(2,128)(2,1)} %reshape.50.gain_h, ...), custom_call_target="tpu_custom_call" | custom-call | flops 49999998976 | bytes 31457280 | tf_op jit(solution)/shard_map/pallas_call | solution.py:802
  210.9 0.8 slice_reduce_fusion
  211.6 0.6 reshape_squeeze.3
  212.2 1.4 slice.26
  213.6 0.9 slice_bitcast_fusion
  214.5 0.6 copy_bitcast_fusion
  215.1 0.6 copy.31
  215.7 21.3 %shard_map.221 = (f32[1024,2048]{1,0:T(8,128)}, f32[256,2048]{1,0:T(8,128)}, f32[2048,1024]{1,0:T(8,128)}, f32[3,2048,256]{2,1,0:T(8,128)}) custom-call(bf16[24,1024,256]{2,1,0:T(8,128)(2,1)} %get-tuple-element.23.piece), custom_call_target="tpu_custom_call" | custom-call | tf_op jit(solution)/shard_map/pallas_call | solution.py:846
  237.0 1.3 copy.35
  238.3 1.9 copy.36
  240.2 1.9 copy.37

commit v4 on v3

--- a/solution.py
+++ b/solution.py
@@ -71,6 +71,9 @@
         (self.own, self.other, self.half, self.r1, self.r2, self.zs, self.zr, self.full,
          self.send, self.recv, self.local) = scratch
 
+    def place(self, p):
+        return jnp.where(p < 8, p + 8, jnp.where(p < 10, p - 2, jnp.where(p < 18, p + 6, p - 18)))
+
     def core_copy(self, p):
         s, at = p % 4, self.at
         return rcopy(self.own.at[p % 2, rows_at(1 - at["core"], 512)], self.other.at[p % 2],
@@ -97,21 +100,21 @@
 
     def back_first(self, p):
         s, at = p % 4, self.at
-        mine = self.out.at[p, rows_at(at["core"] * 4 + at["y"], 128)]
+        mine = self.out.at[self.place(p), rows_at(at["core"] * 4 + at["y"], 128)]
         return (rcopy(self.full.at[s], mine, self.send.at[6, p % 8], self.recv.at[6, p % 8], at["dev_yr"]),
                 rcopy(self.full.at[s], mine, self.send.at[7, p % 8], self.recv.at[7, p % 8], at["dev_yl"]),
                 pltpu.make_async_copy(self.full.at[s], mine, self.local.at[p % 8]))
 
     def back_second(self, p):
         s, at = p % 4, self.at
-        top = self.out.at[p, rows_at(at["core"] * 4 + at["yl"], 128, 64)]
-        low = self.out.at[p, pl.ds(pl.multiple_of((at["core"] * 4 + at["yr"]) * 128 + 64, 64), 64)]
+        top = self.out.at[self.place(p), rows_at(at["core"] * 4 + at["yl"], 128, 64)]
+        low = self.out.at[self.place(p), pl.ds(pl.multiple_of((at["core"] * 4 + at["yr"]) * 128 + 64, 64), 64)]
         return (rcopy(top, top, self.send.at[9, p % 8], self.recv.at[9, p % 8], at["dev_yr"]),
                 rcopy(low, low, self.send.at[10, p % 8], self.recv.at[10, p % 8], at["dev_yl"]))
 
     def back_core(self, p):
         s, at = p % 4, self.at
-        mine = self.out.at[p, rows_at(at["core"], 512)]
+        mine = self.out.at[self.place(p), rows_at(at["core"], 512)]
         return rcopy(mine, mine, self.send.at[8, p % 8], self.recv.at[8, p % 8], at["dev_core"])
 
     def send_piece(self, p):
@@ -356,8 +359,7 @@
     def steps(self, t):
         for lag, step in ((2, self.add_first), (3, self.add_second), (4, self.add_third)):
             c = t - lag
-            pl.when((c >= 0) & (c < 8))(lambda step=step, c=c: step(c))
-            pl.when((c >= 10) & (c < 18))(lambda step=step, c=c - 2: step(c))
+            pl.when((c >= 0) & (c < 16))(lambda step=step, c=c: step(c))
 
 
 class SmallSum:
@@ -441,6 +443,7 @@
 
 
 WIDE = 14
+UNITS = ((3, (0, 2)), (3, (2, 4)), (2, (0, 2)), (2, (2, 4)), (1, (0, 4)), (0, (0, 4)))
 RS = 8
 FEAT, MID = 1792, 1280
 
@@ -457,7 +460,7 @@
 ):
     at = neighbours()
     grad_n = p_f
-    dp_f = grad_mid.at[:, pl.ds(0, 256)]
+    dp_f = grad_mid.at[:, pl.ds(1024, 256)]
     act_t = grad_feat
     n1, n2, n3 = len(GradSum.scratch()), len(Gather.scratch()), len(RowSum.scratch())
     small = SmallSum(scratch[n1 + n2 + n3:])
@@ -465,15 +468,17 @@
     gather = Gather(at, scratch[n1:n1 + n2])
 
     def keep_rows(c, value):
-        @pl.when(c < 8)
+        branch = (c < 6) | (c >= 14)
+
+        @pl.when(branch)
         def _():
-            cols = at_rows(c)
+            cols = at_rows(jnp.where(c < 6, c, c - 8))
             own = tokens[:, cols].astype(F32) + value + b_sum[0:1, cols]
             output[:, cols] = own.astype(BF)
 
-        @pl.when(c >= 8)
+        @pl.when(jnp.logical_not(branch))
         def _():
-            grad_n[at_rows(c - 8, 128), :] = value
+            grad_n[at_rows(c - 6, 128), :] = value
 
     row_sum = RowSum(at, scratch[n1 + n2:n1 + n2 + n3], keep_rows)
 
@@ -489,9 +494,9 @@
     for copy in weights:
         copy.start()
 
-    gain[...] = gain_h[...].astype(F32)
-    shift[...] = shift_h[...].astype(F32)
-    b_sum[...] = b_out_h[...].astype(F32) + b_down_h[...].astype(F32)
+    gain[...] = gain_h[...].astype(F32).reshape(1, 2048)
+    shift[...] = shift_h[...].astype(F32).reshape(1, 2048)
+    b_sum[...] = (b_out_h[...].astype(F32) + b_down_h[...].astype(F32)).reshape(1, 2048)
     x = tokens[...].astype(F32)
     mean = jnp.mean(x, axis=1, keepdims=True)
     centered = x - mean
@@ -527,7 +532,7 @@
         sine = jnp.sin(angle)
         cos_t[r, :] = jnp.where(lane < ROT, jnp.cos(angle), 1.0)
         sin_t[r, :] = jnp.where(lane < ROT // 2, -sine, jnp.where(lane < ROT, sine, 0.0))
-        pre[r, 0:1024] = jnp.broadcast_to(b_up_h[...].astype(F32), (256, 1024))
+        pre[r, 0:1024] = jnp.broadcast_to(b_up_h[...].astype(F32).reshape(1, 1024), (256, 1024))
         for k in range(3):
             cols = slice(1024 + k * 256, 1280 + k * 256)
             pre[r, cols] = jnp.broadcast_to(b_qkv[k:k + 1, :].astype(F32), (256, 256))
@@ -598,12 +603,13 @@
     def head_rows(h):
         return pl.ds(pl.multiple_of(h * 64, 64), 64)
 
-    def attend(qb):
+    def attend(qb, heads):
         cols = slice(qb * 256, qb * 256 + 256)
         n = (qb + 1) * 256
-        attend_bias(qb)
-
-        @pl.loop(0, 4)
+        if heads[0] == 0:
+            attend_bias(qb)
+
+        @pl.loop(*heads)
         def _(h):
             hr = head_rows(h)
             one_head(q_m, turned.at[0], h, cols)
@@ -618,13 +624,13 @@
                 turned[2, hr, 0:n], ds_b[0:n, :]).astype(BF)
             lse[pl.ds(h, 1), cols] = most + jnp.log(total)
 
-    def attend_back(qb, first_head):
+    def attend_back(qb, heads):
         cols = slice(qb * 256, qb * 256 + 256)
         n = (qb + 1) * 256
-        if first_head == 0:
+        if heads[0] == 0:
             attend_bias(qb)
 
-        @pl.loop(first_head, first_head + 2)
+        @pl.loop(*heads)
         def _(h):
             hr = head_rows(h)
             one_head(q_m, turned.at[0], h, cols)
@@ -660,17 +666,37 @@
             r = at_rows(b, 512)
             grad_mid[r, :] += dot_nt(gather.all[t, r, :], w_mid[:, at_rows(t)])
 
-        pl.when(t < 4)(lambda: make_rows(t))
-        for qb in range(4):
-            pl.when(t == 4 + qb)(lambda qb=qb: attend(qb))
-
-    def branch_chunk(c):
-        row_sum.store(c, dot(mid[...], w_mid[:, at_rows(c)]))
-        row_sum.send_chunk(c)
-
-    def normed_chunk(c):
-        row_sum.store(c + 8, dot_nt(grad_feat[...], w_in[at_rows(c), :]))
-        row_sum.send_chunk(c + 8)
+        @pl.when(t < 2)
+        def _():
+            make_rows(2 * t)
+            make_rows(2 * t + 1)
+
+        for i, (qb, heads) in enumerate(UNITS):
+            pl.when(t == 2 + i)(lambda qb=qb, heads=heads: attend(qb, heads))
+
+    def branch_chunk(t, c):
+        row_sum.store(t - RS, dot(mid[...], w_mid[:, at_rows(c)]))
+        row_sum.send_chunk(t - RS)
+
+    def normed_chunk(t, c):
+        row_sum.store(t - RS, dot_nt(grad_feat[...], w_in[at_rows(c), :]))
+        row_sum.send_chunk(t - RS)
+
+    def gelu_back(k):
+        @pl.loop(0, 4)
+        def _(b):
+            r, cols = at_rows(b), at_rows(k)
+            u = pre[r, cols]
+            th = gelu_parts(u)
+            slope = 0.5 * (1.0 + th) + 0.5 * u * (1.0 - th * th) * (
+                0.7978845608028654 * (1.0 + 3 * 0.044715 * (u * u)))
+            grad_feat[r, cols] = (slope * grad_mid[r, cols]).astype(BF)
+
+    def feature_piece(t):
+        q = t - 10
+        grads.own[t % 2] = dot(
+            normed_t[at_rows(q % 2, 1024), :], grad_feat[:, at_rows(q // 2)]).astype(BF)
+        grads.send_piece(t)
 
     @pl.loop(0, 4)
     def _(b):
@@ -679,6 +705,7 @@
         g = grad_mid[r, 1024:1280].astype(BF)
         outs_g[r, :] = g
         outs_gt[:, r] = g.T
+        pre[r, 1024:1792] = jnp.zeros((256, 768), F32)
 
     @pl.loop(8, 10)
     def _(t):
@@ -688,35 +715,20 @@
             r = slice(j * 256, j * 256 + 256)
             grads.own[t % 2, r, :] = dot(heads_t[...], gather.all[4 * (t - 8) + j]).astype(BF)
         grads.send_piece(t)
-        branch_chunk(t - RS)
-
-        @pl.loop(2 * (t - 8), 2 * (t - 8) + 2)
-        def _(b):
-            r = at_rows(b)
-            for k in range(4):
-                cols = slice(k * 256, k * 256 + 256)
-                u = pre[r, cols]
-                th = gelu_parts(u)
-                slope = 0.5 * (1.0 + th) + 0.5 * u * (1.0 - th * th) * (
-                    0.7978845608028654 * (1.0 + 3 * 0.044715 * (u * u)))
-                grad_feat[r, cols] = (slope * grad_mid[r, cols]).astype(BF)
-            pre[r, 1024:1792] = jnp.zeros((256, 768), F32)
-
-    def feature_piece(t):
-        q = t - 10
-        grads.own[t % 2] = dot(
-            normed_t[at_rows(q % 2, 1024), :], grad_feat[:, at_rows(q // 2)]).astype(BF)
-        grads.send_piece(t)
-
-    @pl.loop(10, 18)
+        branch_chunk(t, t - RS)
+        pl.when(t == 9)(lambda: gelu_back(0))
+        for i, (qb, heads) in enumerate(UNITS[:2]):
+            pl.when(t == 8 + i)(lambda qb=qb, heads=heads: attend_back(qb, heads))
+
+    @pl.loop(10, 14)
     def _(t):
         grads.steps(t)
         row_sum.steps(t - RS)
         feature_piece(t)
-        pl.when(t < RS + 8)(lambda: branch_chunk(t - RS))
-        for qb in range(4):
-            for half in range(2):
-                pl.when(t == 10 + 2 * qb + half)(lambda qb=qb, half=half: attend_back(qb, 2 * half))
+        branch_chunk(t, t - RS)
+        pl.when(t >= 11)(lambda: gelu_back(t - 10))
+        for i, (qb, heads) in enumerate(UNITS[2:]):
+            pl.when(t == 10 + i)(lambda qb=qb, heads=heads: attend_back(qb, heads))
 
     for b in range(4):
         r = slice(b * 256, b * 256 + 256)
@@ -728,18 +740,20 @@
             grad_feat[r, 1280 + a:1408 + a] = turn(pre[r, 1280 + a:1408 + a], cosine, sine).astype(BF)
         grad_feat[r, 1536:1792] = pre[r, 1536:1792].astype(BF)
 
-    @pl.loop(18, 24)
+    @pl.loop(14, 24)
     def _(t):
         grads.steps(t)
         row_sum.steps(t - RS)
         feature_piece(t)
-        normed_chunk(t - 18)
-
-    @pl.loop(24, 30)
-    def _(t):
+        pl.when(t < 22)(lambda: normed_chunk(t, t - 14))
+        pl.when(t >= 22)(lambda: branch_chunk(t, t - 16))
+
+    def late_steps(t):
         grads.steps(t)
         row_sum.steps(t - RS)
-        pl.when(t < 26)(lambda: normed_chunk(t - 18))
+
+    late_steps(24)
+    late_steps(25)
 
     def column_sum(value):
         return jnp.sum(value.astype(F32), axis=0, keepdims=True)
@@ -763,7 +777,7 @@
         row, lanes = 6 + k // 4, slice((k % 4) * 256, (k % 4) * 256 + 256)
         small.b1[mine, row:row + 1, lanes] = column_sum(grad_feat[:, k * 256:k * 256 + 256])
     small.start(0)
-    grads.steps(30)
+    late_steps(26)
     mean_plain = mean_plain / 2048.0
     mean_unit = mean_unit / 2048.0
     for c in range(8):
@@ -771,11 +785,15 @@
         inner = grad_n[c * 128:c * 128 + 128, :] * gain[0:1, cols] - mean_plain - unit(cols) * mean_unit
         input_grad[:, cols] = (cotangent[:, cols].astype(F32) + rstd[:, 0:1] * inner).astype(BF)
 
+    late_steps(27)
     small.second()
-    grads.steps(31)
+    late_steps(28)
+    late_steps(29)
     small.third()
-    grads.steps(32)
+    late_steps(30)
+    late_steps(31)
     sums[...] = small.result()
+    late_steps(32)
 
 
 def run_block(tokens, segment, ln_gain, ln_bias, w_qkv, b_qkv, w_out, b_out, w_up, b_up, w_down,
@@ -814,65 +832,77 @@
             collective_id=0, has_side_effects=True, vmem_limit_bytes=VMEM_LIMIT),
         cost_estimate=pl.CostEstimate(flops=50 * 10**9, bytes_accessed=30 << 20, transcendentals=10**7),
     )(
-        tokens, cotangent, segment.reshape(1, 1024), ln_gain.reshape(1, 2048),
-        ln_bias.reshape(1, 2048), b_qkv, b_out.reshape(1, 2048), b_up.reshape(1, 1024),
-        b_down.reshape(1, 2048), w_qkv.transpose(1, 0, 2), w_out, w_up, w_down,
+        tokens, cotangent, segment.reshape(1, 1024), ln_gain, ln_bias, b_qkv, b_out, b_up, b_down,
+        w_qkv.transpose(1, 0, 2), w_out, w_up, w_down,
     )
 
 
-def widen_kernel(piece, down, out, up, qkv):
-    i = pl.program_id(0)
-    value = piece[0]
-
-    @pl.when(i < 8)
+def widen_kernel(qkv_p, out_p, down_p, up_p, output, input_grad, sums,
+                 down, out, up, qkv, output_o, input_grad_o, gain_o, shift_o, b_out_o, b_down_o, b_up_o, b_qkv_o):
+    for c in range(8):
+        cols = slice(c * 256, c * 256 + 256)
+        down[:, cols] = down_p[c].astype(F32)
+        out[:, cols] = out_p[c].astype(F32)
+    for c in range(4):
+        up[:, c * 256:c * 256 + 256] = up_p[c, 0].astype(F32)
+    qkv[...] = qkv_p[...].astype(F32)
+    output_o[...] = output[...]
+    input_grad_o[...] = input_grad[...]
+
+    @pl.when(pl.program_id(0) == 0)
     def _():
-        down[...] = value.astype(F32)
-
-    @pl.when((i >= 8) & (i < 10))
-    def _():
-        for j in range(4):
-            out[:, j * 256:j * 256 + 256] = piece[0, j * 256:j * 256 + 256, :].astype(F32)
-
-    @pl.when((i >= 10) & (i < 18))
-    def _():
-        up[...] = value.astype(F32)
-
-    @pl.when(i >= 18)
-    def _():
-        qkv[0] = value.astype(F32)
-
-
-def widen(pieces):
-    down, out, up, qkv = pl.pallas_call(
+        gain_o[...] = sums[0:2, :].reshape(2048)
+        shift_o[...] = sums[2:4, :].reshape(2048)
+        b_out_o[...] = sums[4:6, :].reshape(2048)
+        b_down_o[...] = sums[4:6, :].reshape(2048)
+        b_up_o[...] = sums[6:7, :].reshape(1024)
+        for c in range(3):
+            b_qkv_o[c:c + 1, :] = sums[7:8, c * 256:c * 256 + 256]
+
+
+def widen(pieces, output, input_grad, sums):
+    def rows(count, width):
+        return pl.BlockSpec((count, width), lambda i: (i, 0))
+
+    def whole(*shape):
+        return pl.BlockSpec(shape, lambda i: (0,) * len(shape))
+
+    def shape(*dims, kind=F32):
+        return jax.ShapeDtypeStruct(dims, kind)
+
+    down, out, up, qkv, *rest = pl.pallas_call(
         widen_kernel,
-        grid=(NP,),
+        grid=(8,),
         out_shape=(
-            jax.ShapeDtypeStruct((1024, 2048), F32),
-            jax.ShapeDtypeStruct((256, 2048), F32),
-            jax.ShapeDtypeStruct((2048, 1024), F32),
-            jax.ShapeDtypeStruct((3, 2048, 256), F32),
+            shape(1024, 2048), shape(256, 2048), shape(2048, 1024), shape(6144, 256),
+            shape(128, 2048, kind=BF), shape(128, 2048, kind=BF),
+            shape(2048), shape(2048), shape(2048), shape(2048), shape(1024), shape(3, 256),
         ),
-        in_specs=[pl.BlockSpec((1, 1024, 256), lambda i: (i, 0, 0))],
+        in_specs=[
+            rows(768, 256),
+            pl.BlockSpec((8, 32, 256), lambda i: (3, i, 0)),
+            pl.BlockSpec((8, 128, 256), lambda i: (1, i, 0)),
+            pl.BlockSpec((4, 1, 256, 256), lambda i: (2, i // 4, i % 4, 0)),
+            rows(16, 2048), rows(16, 2048), whole(8, 1024),
+        ],
         out_specs=(
-            pl.BlockSpec((1024, 256), lambda i: (0, jnp.minimum(i, 7))),
-            pl.BlockSpec((256, 1024), lambda i: (0, jnp.clip(i - 8, 0, 1))),
-            pl.BlockSpec((1024, 256), lambda i: (jnp.clip(i - 10, 0, 7) % 2, jnp.clip(i - 10, 0, 7) // 2)),
-            pl.BlockSpec((1, 1024, 256), lambda i: (jnp.clip(i - 18, 0, 5) // 2, jnp.clip(i - 18, 0, 5) % 2, 0)),
+            rows(128, 2048), rows(32, 2048), rows(256, 1024), rows(768, 256),
+            rows(16, 2048), rows(16, 2048),
+            whole(2048), whole(2048), whole(2048), whole(2048), whole(1024), whole(3, 256),
         ),
         compiler_params=pltpu.CompilerParams(vmem_limit_bytes=VMEM_LIMIT),
-    )(pieces)
-    return down, out, up, qkv.transpose(1, 0, 2)
+    )(
+        pieces.reshape(NP * 1024, 256), pieces.reshape(NP * 4, 256, 256), pieces,
+        pieces.reshape(NP // 2, 2, 1024, 256), output, input_grad, sums,
+    )
+    return down, out, up, qkv.reshape(3, 2048, 256).transpose(1, 0, 2), rest
 
 
 def on_device(*args):
     pieces, output, input_grad, sums = run_block(*args)
-    grad_w_down, grad_w_out, grad_w_up, grad_w_qkv = widen(pieces)
-    wide = sums[:6].reshape(3, 2048)
-    bias_total = wide[2]
-    return (
-        output, input_grad, wide[0], wide[1], grad_w_qkv, sums[7, :768].reshape(3, 256), grad_w_out,
-        bias_total, grad_w_up, sums[6], grad_w_down, bias_total,
-    )
+    down, out, up, qkv, rest = widen(pieces, output, input_grad, sums)
+    output, input_grad, gain, shift, b_out, b_down, b_up, b_qkv = rest
+    return output, input_grad, gain, shift, qkv, b_qkv, out, b_out, up, b_up, down, b_down
 
 
 def solution(mesh):

time: 243 us -> 212 us (0.87)
  local copies, waits for them, and re-layouts: 16.3 us -> 0 us
  Pallas kernels: 225 us -> 211 us
    pallas_call x1, Pallas kernels: 204 us -> 196 us  [run_block(): pl.pallas_call(block_kernel, out_shape=(jax.ShapeDtypeStruct((NP, 1024, 2...]
    unnamed x5 -> x0, local copies, waits for them, and re-layouts: 6.53 us -> none
    reshape x5 -> x0, local copies, waits for them, and re-layouts: 6.44 us -> none  [the longest x1 1.29 us: run_block(): ln_gain.reshape(1, 2048)]
    pallas_call x1, Pallas kernels: 21.3 us -> 15 us  [widen(): pl.pallas_call(widen_kernel, grid=(8,), out_shape=(shape(1024, 2048), sha...]
where the time goes in v4:
time: 212 us; the launch traced here: 211 us
  Pallas kernels  211 us (100%)
    pallas_call x1, Pallas kernels, run_block(): pl.pallas_call(block_kernel, out_shape=(jax.ShapeDtypeStruct((NP, 1024, 2...  196 us
    pallas_call x1, Pallas kernels, widen(): pl.pallas_call(widen_kernel, grid=(8,), out_shape=(shape(1024, 2048), sha...  15 us

profile of v4, /device:TPU:1, one launch (start us, length us, event | category | flops | bytes accessed | tf_op | source)
XLA Modules:
  0.0 211.4 jit_solution(17006389473673347449)
XLA Ops:
  0.6 195.6 %shard_map.220 = (bf16[24,1024,256]{2,1,0:T(8,128)(2,1)}, bf16[128,2048]{1,0:T(8,128)(2,1)}, bf16[128,2048]{1,0:T(8,128)(2,1)}, f32[8,1024]{1,0:T(8,128)}) custom-call(bf16[128,2048]{1,0:T(8,128)(2,1)} %tokens.1, bf16[128,2048]{1,0:T(8,128)(2,1)} %cotangent.1, s32[1,1024]{1,0:T(1,128)} %bitcast.13, bf16[2048]{0:T(1024)(128)(2,1)} %gain_h.1, ...), custom_call_target="tpu_custom_call" | custom-call | flops 49999998976 | bytes 31457280 | tf_op jit(solution)/shard_map/pallas_call | solution.py:820
  196.3 15.0 %shard_map.221 = (f32[1024,2048]{1,0:T(8,128)}, f32[256,2048]{1,0:T(8,128)}, f32[2048,1024]{1,0:T(8,128)}, f32[6144,256]{1,0:T(8,128)}, bf16[128,2048]{1,0:T(8,1...) custom-call(bf16[24576,256]{1,0:T(8,128)(2,1)} %bitcast.8, ...), custom_call_target="tpu_custom_call" | custom-call | tf_op jit(solution)/shard_map/pallas_call | solution.py:873

commit v5 on v4

--- a/solution.py
+++ b/solution.py
@@ -57,10 +57,10 @@
             pltpu.VMEM((2, 512, 256), BF),
             pltpu.VMEM((4, 512, 256), BF),
             pltpu.VMEM((4, 2, 64, 256), BF),
-            pltpu.VMEM((4, 2, 128, 256), BF),
+            pltpu.VMEM((6, 2, 128, 256), BF),
+            pltpu.VMEM((2, 128, 256), BF),
             pltpu.VMEM((4, 128, 256), BF),
-            pltpu.VMEM((4, 128, 256), BF),
-            pltpu.VMEM((4, 128, 256), BF),
+            pltpu.VMEM((3, 128, 256), BF),
             pltpu.SemaphoreType.DMA((11, 8)),
             pltpu.SemaphoreType.DMA((11, 8)),
             pltpu.SemaphoreType.DMA((8,)),
@@ -88,22 +88,22 @@
 
     def second_copies(self, p):
         s, at = p % 4, self.at
-        return (rcopy(self.half.at[s, rows_at(at["yr"], 128)], self.r2.at[s, 0],
+        return (rcopy(self.half.at[s, rows_at(at["yr"], 128)], self.r2.at[p % 6, 0],
                       self.send.at[3, p % 8], self.recv.at[3, p % 8], at["dev_yr"]),
-                rcopy(self.half.at[s, rows_at(at["yl"], 128)], self.r2.at[s, 1],
+                rcopy(self.half.at[s, rows_at(at["yl"], 128)], self.r2.at[p % 6, 1],
                       self.send.at[4, p % 8], self.recv.at[4, p % 8], at["dev_yl"]))
 
     def z_copy(self, p):
         s = p % 4
-        return rcopy(self.zs.at[s], self.zr.at[s], self.send.at[5, p % 8], self.recv.at[5, p % 8],
+        return rcopy(self.zs.at[p % 2], self.zr.at[s], self.send.at[5, p % 8], self.recv.at[5, p % 8],
                      self.at["dev_zh"])
 
     def back_first(self, p):
         s, at = p % 4, self.at
         mine = self.out.at[self.place(p), rows_at(at["core"] * 4 + at["y"], 128)]
-        return (rcopy(self.full.at[s], mine, self.send.at[6, p % 8], self.recv.at[6, p % 8], at["dev_yr"]),
-                rcopy(self.full.at[s], mine, self.send.at[7, p % 8], self.recv.at[7, p % 8], at["dev_yl"]),
-                pltpu.make_async_copy(self.full.at[s], mine, self.local.at[p % 8]))
+        return (rcopy(self.full.at[p % 3], mine, self.send.at[6, p % 8], self.recv.at[6, p % 8], at["dev_yr"]),
+                rcopy(self.full.at[p % 3], mine, self.send.at[7, p % 8], self.recv.at[7, p % 8], at["dev_yl"]),
+                pltpu.make_async_copy(self.full.at[p % 3], mine, self.local.at[p % 8]))
 
     def back_second(self, p):
         s, at = p % 4, self.at
@@ -149,13 +149,13 @@
         for copy in self.second_copies(p):
             copy.wait()
         mine = self.half[s, rows_at(self.at["y"], 128)].astype(F32)
-        self.zs[s] = (mine + self.r2[s, 0].astype(F32) + self.r2[s, 1].astype(F32)).astype(BF)
+        self.zs[p % 2] = (mine + self.r2[p % 6, 0].astype(F32) + self.r2[p % 6, 1].astype(F32)).astype(BF)
         self.z_copy(p).start()
 
     def add_z(self, p):
         s = p % 4
         self.z_copy(p).wait()
-        self.full[s] = (self.zs[s].astype(F32) + self.zr[s].astype(F32)).astype(BF)
+        self.full[p % 3] = (self.zs[p % 2].astype(F32) + self.zr[s].astype(F32)).astype(BF)
         for copy in self.back_first(p):
             copy.start()
 
@@ -174,8 +174,8 @@
         self.back_core(p).wait()
 
     def steps(self, t):
-        for lag, step in ((1, self.add_core), (2, self.add_first), (3, self.add_second), (4, self.add_z),
-                          (6, self.forward_y), (8, self.forward_core), (9, self.finish)):
+        for lag, step in ((1, self.add_core), (2, self.add_first), (4, self.add_second), (5, self.add_z),
+                          (7, self.forward_y), (9, self.forward_core), (10, self.finish)):
             p = t - lag
             pl.when((p >= 0) & (p < NP))(lambda step=step, p=p: step(p))
 
@@ -197,15 +197,14 @@
 
     def scratch():
         return [
-            pltpu.VMEM((16, 128, 256), BF),
             pltpu.VMEM((8, 1024, 256), BF),
             pltpu.SemaphoreType.DMA((9, 8)),
             pltpu.SemaphoreType.DMA((9, 8)),
         ]
 
-    def __init__(self, at, scratch):
-        self.at = at
-        self.own, self.all, self.send, self.recv = scratch
+    def __init__(self, at, own, scratch):
+        self.at, self.own = at, own
+        self.all, self.send, self.recv = scratch
 
     def copy(self, kind, c, src, dst, device):
         s = c % 8
@@ -220,9 +219,9 @@
 
     def first(self, c, wide):
         at = self.at
-        src, dst = self.own.at[c], self.part(c, at["zl"], at["x"])
-        copies = [self.copy(0, c, src, dst, "dev_xr"), self.copy(1, c, src, dst, "dev_xl")]
-        return copies if wide else copies + [self.copy(2, c, src, dst, "dev_zl")]
+        mine = self.part(c, at["zl"], at["x"])
+        copies = [self.same(0, c, mine, "dev_xr"), self.same(1, c, mine, "dev_xl")]
+        return copies if wide else copies + [self.same(2, c, mine, "dev_zl")]
 
     def ring(self, c):
         at = self.at
@@ -232,7 +231,7 @@
     def second(self, c, wide):
         at = self.at
         if wide:
-            return [self.copy(5, c, self.own.at[c], self.part(c, at["zl"], at["x"]), "dev_zl"),
+            return [self.same(5, c, self.part(c, at["zl"], at["x"]), "dev_zl"),
                     self.same(6, c, self.part(c, at["zl"], at["xl"]), "dev_zl"),
                     self.same(7, c, self.part(c, at["zl"], at["xr"]), "dev_zl")]
         other = self.part(c, 1 - at["zl"], at["x"])
@@ -250,8 +249,8 @@
             for copy in self.first(c, wide):
                 copy.start()
 
+        self.part(c, self.at["zl"], self.at["x"])[...] = self.own(c)
         self.either(c, start)
-        self.part(c, self.at["zl"], self.at["x"])[...] = self.own[c]
 
     def either(self, c, step):
         wide = (c % 2 == 1) & (c < WIDE)
@@ -285,11 +284,11 @@
     def scratch():
         return [
             pltpu.VMEM((4, 2, 4, 128, 256), BF),
-            pltpu.VMEM((8, 2, 2, 64, 256), BF),
-            pltpu.VMEM((4, 2, 2, 128, 256), BF),
+            pltpu.VMEM((6, 2, 2, 64, 256), BF),
+            pltpu.VMEM((6, 2, 2, 128, 256), BF),
+            pltpu.VMEM((2, 128, 256), BF),
             pltpu.VMEM((4, 128, 256), BF),
-            pltpu.VMEM((4, 128, 256), BF),
-            pltpu.VMEM((4, 128, 256), F32),
+            pltpu.VMEM((2, 128, 256), F32),
             pltpu.SemaphoreType.DMA((5, 8)),
             pltpu.SemaphoreType.DMA((5, 8)),
         ]
@@ -304,17 +303,17 @@
 
     def first(self, c):
         s, at = c % 4, self.at
-        return [self.copy(0, c, self.part.at[s, :, at["xo"], pl.ds(0, 64)], self.r1.at[c % 8, 0], at["dev_xr"]),
-                self.copy(1, c, self.part.at[s, :, at["xo"], pl.ds(64, 64)], self.r1.at[c % 8, 1], at["dev_xl"])]
+        return [self.copy(0, c, self.part.at[s, :, at["xo"], pl.ds(0, 64)], self.r1.at[c % 6, 0], at["dev_xr"]),
+                self.copy(1, c, self.part.at[s, :, at["xo"], pl.ds(64, 64)], self.r1.at[c % 6, 1], at["dev_xl"])]
 
     def second(self, c):
         s, at = c % 4, self.at
-        return [self.copy(2, c, self.part.at[s, :, at["xr"]], self.r2.at[s, 0], at["dev_xr"]),
-                self.copy(3, c, self.part.at[s, :, at["xl"]], self.r2.at[s, 1], at["dev_xl"])]
+        return [self.copy(2, c, self.part.at[s, :, at["xr"]], self.r2.at[c % 6, 0], at["dev_xr"]),
+                self.copy(3, c, self.part.at[s, :, at["xl"]], self.r2.at[c % 6, 1], at["dev_xl"])]
 
     def third(self, c):
         s = c % 4
-        return [self.copy(4, c, self.zs.at[s], self.zr.at[s], self.at["dev_zl"])]
+        return [self.copy(4, c, self.zs.at[c % 2], self.zr.at[s], self.at["dev_zl"])]
 
     def store(self, c, value):
         for k in range(8):
@@ -329,9 +328,9 @@
         for copy in self.first(c):
             copy.wait()
         for z in range(2):
-            top = self.part[s, z, at["xr"], 0:64].astype(F32) + self.r1[c % 8, 0, z].astype(F32)
+            top = self.part[s, z, at["xr"], 0:64].astype(F32) + self.r1[c % 6, 0, z].astype(F32)
             self.part[s, z, at["xr"], 0:64] = top.astype(BF)
-            low = self.part[s, z, at["xl"], 64:128].astype(F32) + self.r1[c % 8, 1, z].astype(F32)
+            low = self.part[s, z, at["xl"], 64:128].astype(F32) + self.r1[c % 6, 1, z].astype(F32)
             self.part[s, z, at["xl"], 64:128] = low.astype(BF)
         for copy in self.second(c):
             copy.start()
@@ -343,23 +342,24 @@
 
         def total(z):
             own = self.part[s, z, at["x"]].astype(F32)
-            return own + self.r2[s, 0, z].astype(F32) + self.r2[s, 1, z].astype(F32)
-
-        self.zs[s] = total(1 - at["zl"]).astype(BF)
+            return own + self.r2[c % 6, 0, z].astype(F32) + self.r2[c % 6, 1, z].astype(F32)
+
+        self.zs[c % 2] = total(1 - at["zl"]).astype(BF)
         for copy in self.third(c):
             copy.start()
-        self.mine[s] = total(at["zl"])
+        self.mine[c % 2] = total(at["zl"])
 
     def add_third(self, c):
         s = c % 4
         for copy in self.third(c):
             copy.wait()
-        self.result(c, self.mine[s] + self.zr[s].astype(F32))
+        self.result(c, self.mine[c % 2] + self.zr[s].astype(F32))
 
     def steps(self, t):
-        for lag, step in ((2, self.add_first), (3, self.add_second), (4, self.add_third)):
+        for lag, step in ((2, self.add_first), (4, self.add_second), (5, self.add_third)):
             c = t - lag
-            pl.when((c >= 0) & (c < 16))(lambda step=step, c=c: step(c))
+            pl.when((c >= 0) & (c < 14))(lambda step=step, c=c: step(c))
+            pl.when((c >= 16) & (c < 18))(lambda step=step, c=c - 2: step(c))
 
 
 class SmallSum:
@@ -454,18 +454,27 @@
     pieces, output, input_grad, sums,
     w_in, w_mid, w_sem,
     gain, shift, b_sum,
-    normed_t, pre, grad_mid, rows, turned, mid, heads_t, outs_g, outs_gt, grad_feat,
-    cos_t, sin_t, seg_c, seg_r, lse, bias, p_f, q_m, g_m, ds_b, mean_row, rstd,
+    normed_t, pre, grad_mid, rows, turned, mid, heads_t, outs_gt, grad_feat,
+    cos_t, sin_t, seg_c, seg_r, lse, out_f, q_m, g_m, ds_b, q_2, g_2, mean_row, rstd,
     *scratch,
 ):
     at = neighbours()
-    grad_n = p_f
-    dp_f = grad_mid.at[:, pl.ds(1024, 256)]
+    bias, p_b = grad_feat.at[:, pl.ds(1024, 256)], grad_feat.at[:, pl.ds(1280, 512)]
+    s_f, d_f, grad_n = (grad_mid.at[:, pl.ds(a, n)] for a, n in ((0, 512), (512, 512), (1024, 256)))
     act_t = grad_feat
     n1, n2, n3 = len(GradSum.scratch()), len(Gather.scratch()), len(RowSum.scratch())
     small = SmallSum(scratch[n1 + n2 + n3:])
+
+    def unit(cols):
+        return (tokens[:, cols].astype(F32) - mean_row[:, 0:1]) * rstd[:, 0:1]
+
+    def own_chunk(c):
+        cols = at_rows(c % 8)
+        normed = (unit(cols) * gain[0:1, cols] + shift[0:1, cols]).astype(BF)
+        return jnp.where(c < 8, normed, cotangent[:, cols])
+
     grads = GradSum(at, pieces, scratch[:n1])
-    gather = Gather(at, scratch[n1:n1 + n2])
+    gather = Gather(at, own_chunk, scratch[n1:n1 + n2])
 
     def keep_rows(c, value):
         branch = (c < 6) | (c >= 14)
@@ -503,14 +512,6 @@
     scale = lax.rsqrt(jnp.mean(centered * centered, axis=1, keepdims=True) + EPSILON)
     rstd[...] = jnp.broadcast_to(scale, (128, 128))
     mean_row[...] = jnp.broadcast_to(mean, (128, 128))
-
-    def unit(cols):
-        return (tokens[:, cols].astype(F32) - mean_row[:, 0:1]) * rstd[:, 0:1]
-
-    for c in range(8):
-        cols = slice(c * 256, c * 256 + 256)
-        gather.own[c] = (unit(cols) * gain[0:1, cols] + shift[0:1, cols]).astype(BF)
-        gather.own[8 + c] = cotangent[:, cols]
 
     pl.semaphore_wait(barrier, len(greeted))
     for c in range(Gather.AHEAD):
@@ -557,8 +558,7 @@
                 pre[r, :] += dot(a, w_in[at_rows(c), :])
             normed_t[at_rows(c), :] = gather.all[c % 8].T
 
-    @pl.loop(0, 4)
-    def _(b):
+    def gelu(b):
         r = at_rows(b)
         for k in range(4):
             cols = slice(k * 256, k * 256 + 256)
@@ -567,9 +567,11 @@
             mid[r, cols] = a
             act_t[cols, r] = a.T
 
+    pl.loop(0, 2)(gelu)
+    gather.steps(10)
+    pl.loop(2, 4)(gelu)
     for copy in weights[4:]:
         copy.wait()
-    gather.steps(10)
 
     def make_rows(b):
         r = at_rows(b)
@@ -582,7 +584,8 @@
                     v = v * HEAD_DIM ** -0.5
                 v = v.astype(BF)
                 cols = slice(half * 128, half * 128 + 128)
-                rows[k, r, cols] = v
+                if k > 0:
+                    rows[k - 1, r, cols] = v
                 turned[k, cols, r] = v.T
 
     def attend_bias(qb):
@@ -596,33 +599,55 @@
                 keep = keep & (i <= j)
             bias[r, :] = jnp.where(keep, 0.0, -1e30).astype(BF)
 
-    def one_head(ref, source, h, cols):
+    def head_rows(h, count=64):
+        return pl.ds(pl.multiple_of(h * 64, 64), count)
+
+    def two_heads(ref, source, pair, cols):
         ref[...] = jnp.zeros_like(ref)
-        ref[head_rows(h), :] = source[head_rows(h), cols]
-
-    def head_rows(h):
-        return pl.ds(pl.multiple_of(h * 64, 64), 64)
+        for k in range(2):
+            hr = head_rows(pair * 2 + k)
+            ref[hr, k * 256:k * 256 + 256] = source[hr, cols]
+
+    def both(value):
+        return jnp.concatenate([value, value], axis=1)
+
+    def blocks(n):
+        return [slice(b, b + 64) for b in range(0, n, 64)]
+
+    def over_rows(op, value):
+        return op(value.reshape(8, 8, 512), axis=0)
 
     def attend(qb, heads):
         cols = slice(qb * 256, qb * 256 + 256)
         n = (qb + 1) * 256
         if heads[0] == 0:
             attend_bias(qb)
-
-        @pl.loop(*heads)
-        def _(h):
-            hr = head_rows(h)
-            one_head(q_m, turned.at[0], h, cols)
-            s = dot(rows[1, 0:n, :], q_m[...]) + bias[0:n, :].astype(F32)
-            p_f[0:n, :] = s
-            most = jnp.max(s, axis=0, keepdims=True)
-            e = jnp.exp(p_f[0:n, :] - most)
-            p_f[0:n, :] = e
-            total = jnp.sum(e, axis=0, keepdims=True)
-            ds_b[0:n, :] = (p_f[0:n, :] * (1.0 / total)).astype(BF)
-            heads_t[hr, cols] = dot(
-                turned[2, hr, 0:n], ds_b[0:n, :]).astype(BF)
-            lse[pl.ds(h, 1), cols] = most + jnp.log(total)
+        s_f = pre.at[:, pl.ds(1024, 512)]
+
+        @pl.loop(heads[0] // 2, heads[1] // 2)
+        def _(pair):
+            two_heads(q_m, turned.at[0], pair, cols)
+            s_f[0:n, :] = dot(rows[0, 0:n, :], q_m[...])
+            most = jnp.full((8, 512), -jnp.inf, F32)
+            for r in blocks(n):
+                s = s_f[r, :] + both(bias[r, :].astype(F32))
+                s_f[r, :] = s
+                most = jnp.maximum(most, over_rows(jnp.max, s))
+            most = jnp.max(most, axis=0, keepdims=True)
+            total = jnp.zeros((8, 512), F32)
+            for r in blocks(n):
+                e = jnp.exp(s_f[r, :] - most)
+                total = total + over_rows(jnp.sum, e)
+                ds_b[r, :] = e.astype(BF)
+            total = jnp.sum(total, axis=0, keepdims=True)
+            share, log_total = 1.0 / total, most + jnp.log(total)
+            out = dot(turned[2, head_rows(pair * 2, 128), 0:n], ds_b[0:n, :])
+            for k in range(2):
+                h, side = pair * 2 + k, slice(k * 256, k * 256 + 256)
+                value = out[k * 64:k * 64 + 64, side] * share[:, side]
+                out_f[head_rows(h), cols] = value
+                heads_t[head_rows(h), cols] = value.astype(BF)
+                lse[pl.ds(h, 1), cols] = log_total[:, side]
 
     def attend_back(qb, heads):
         cols = slice(qb * 256, qb * 256 + 256)
@@ -630,24 +655,29 @@
         if heads[0] == 0:
             attend_bias(qb)
 
-        @pl.loop(*heads)
-        def _(h):
-            hr = head_rows(h)
-            one_head(q_m, turned.at[0], h, cols)
-            one_head(g_m, outs_gt, h, cols)
-            p = jnp.exp(dot(rows[1, 0:n, :], q_m[...]) + bias[0:n, :].astype(F32) - lse[pl.ds(h, 1), cols])
-            p_f[0:n, :] = p
-            d = dot(rows[2, 0:n, :], g_m[...])
-            dp_f[0:n, :] = d
-            delta = jnp.sum(p_f[0:n, :] * d, axis=0, keepdims=True)
-            lane = lax.broadcasted_iota(jnp.int32, (256, 256), 1) // 64
-            q_h = jnp.where(lane == h, rows[0, cols, :].astype(F32), 0.0).astype(BF)
-            g_h = jnp.where(lane == h, outs_g[cols, :].astype(F32), 0.0).astype(BF)
-            pre[0:n, 1536:1792] += dot(p_f[0:n, :].astype(BF), g_h)
-            ds_b[0:n, :] = (p_f[0:n, :] * (dp_f[0:n, :] - delta)).astype(BF)
-            pre[0:n, 1280:1536] += dot(ds_b[0:n, :], q_h)
-            pre[pl.ds(pl.multiple_of(qb * 256 + h * 64, 64), 64), 1024:1280] = dot(
-                turned[1, hr, 0:n], ds_b[0:n, :])
+        @pl.loop(heads[0] // 2, heads[1] // 2)
+        def _(pair):
+            pair_rows = head_rows(pair * 2, 128)
+            two_heads(q_m, turned.at[0], pair, cols)
+            two_heads(g_m, outs_gt, pair, cols)
+            s_f[0:n, :] = dot(rows[0, 0:n, :], q_m[...])
+            d_f[0:n, :] = dot(rows[1, 0:n, :], g_m[...])
+            log_total = jnp.concatenate([lse[pl.ds(pair * 2 + k, 1), cols] for k in range(2)], axis=1)
+            product = outs_gt[pair_rows, cols].astype(F32) * out_f[pair_rows, cols]
+            delta = jnp.concatenate([jnp.sum(product[k * 64:k * 64 + 64], axis=0, keepdims=True)
+                                     for k in range(2)], axis=1)
+            for r in blocks(n):
+                p = jnp.exp(s_f[r, :] + both(bias[r, :].astype(F32)) - log_total)
+                p_b[r, :] = p.astype(BF)
+                ds_b[r, :] = (p * (d_f[r, :] - delta)).astype(BF)
+            q_2[...] = q_m[...].T
+            g_2[...] = g_m[...].T
+            grad_q = dot(turned[1, pair_rows, 0:n], ds_b[0:n, :])
+            for k in range(2):
+                pre[pl.ds(pl.multiple_of(qb * 256 + pair * 128 + k * 64, 64), 64), 1024:1280] = grad_q[
+                    k * 64:k * 64 + 64, k * 256:k * 256 + 256]
+            pre[0:n, 1536:1792] += dot(p_b[0:n, :], g_2[...])
+            pre[0:n, 1280:1536] += dot(ds_b[0:n, :], q_2[...])
 
     @pl.loop(0, 8)
     def _(t):
@@ -693,18 +723,19 @@
             grad_feat[r, cols] = (slope * grad_mid[r, cols]).astype(BF)
 
     def feature_piece(t):
-        q = t - 10
-        grads.own[t % 2] = dot(
-            normed_t[at_rows(q % 2, 1024), :], grad_feat[:, at_rows(q // 2)]).astype(BF)
+        @pl.when(t % 2 == 0)
+        def _():
+            value = dot(normed_t[...], grad_feat[:, at_rows((t - 10) // 2)])
+            for k in range(2):
+                grads.own[k] = value[k * 1024:k * 1024 + 1024].astype(BF)
+
         grads.send_piece(t)
 
     @pl.loop(0, 4)
     def _(b):
         r = at_rows(b)
         mid[r, 1024:1280] = heads_t[:, r].T
-        g = grad_mid[r, 1024:1280].astype(BF)
-        outs_g[r, :] = g
-        outs_gt[:, r] = g.T
+        outs_gt[:, r] = grad_mid[r, 1024:1280].astype(BF).T
         pre[r, 1024:1792] = jnp.zeros((256, 768), F32)
 
     @pl.loop(8, 10)
@@ -716,9 +747,13 @@
             grads.own[t % 2, r, :] = dot(heads_t[...], gather.all[4 * (t - 8) + j]).astype(BF)
         grads.send_piece(t)
         branch_chunk(t, t - RS)
-        pl.when(t == 9)(lambda: gelu_back(0))
-        for i, (qb, heads) in enumerate(UNITS[:2]):
-            pl.when(t == 8 + i)(lambda qb=qb, heads=heads: attend_back(qb, heads))
+
+        @pl.when(t == 8)
+        def _():
+            for k in range(4):
+                gelu_back(k)
+
+        pl.when(t == 9)(lambda: attend_back(*UNITS[0]))
 
     @pl.loop(10, 14)
     def _(t):
@@ -726,8 +761,7 @@
         row_sum.steps(t - RS)
         feature_piece(t)
         branch_chunk(t, t - RS)
-        pl.when(t >= 11)(lambda: gelu_back(t - 10))
-        for i, (qb, heads) in enumerate(UNITS[2:]):
+        for i, (qb, heads) in enumerate((UNITS[1], (2, (0, 4)), *UNITS[4:])):
             pl.when(t == 10 + i)(lambda qb=qb, heads=heads: attend_back(qb, heads))
 
     for b in range(4):
@@ -746,14 +780,15 @@
         row_sum.steps(t - RS)
         feature_piece(t)
         pl.when(t < 22)(lambda: normed_chunk(t, t - 14))
-        pl.when(t >= 22)(lambda: branch_chunk(t, t - 16))
 
     def late_steps(t):
         grads.steps(t)
         row_sum.steps(t - RS)
 
-    late_steps(24)
-    late_steps(25)
+    @pl.loop(24, 27)
+    def _(t):
+        late_steps(t)
+        pl.when(t < 26)(lambda: branch_chunk(t - 2, t - 18))
 
     def column_sum(value):
         return jnp.sum(value.astype(F32), axis=0, keepdims=True)
@@ -777,7 +812,7 @@
         row, lanes = 6 + k // 4, slice((k % 4) * 256, (k % 4) * 256 + 256)
         small.b1[mine, row:row + 1, lanes] = column_sum(grad_feat[:, k * 256:k * 256 + 256])
     small.start(0)
-    late_steps(26)
+    late_steps(27)
     mean_plain = mean_plain / 2048.0
     mean_unit = mean_unit / 2048.0
     for c in range(8):
@@ -785,15 +820,15 @@
         inner = grad_n[c * 128:c * 128 + 128, :] * gain[0:1, cols] - mean_plain - unit(cols) * mean_unit
         input_grad[:, cols] = (cotangent[:, cols].astype(F32) + rstd[:, 0:1] * inner).astype(BF)
 
-    late_steps(27)
+    late_steps(28)
     small.second()
-    late_steps(28)
     late_steps(29)
+    late_steps(30)
     small.third()
-    late_steps(30)
     late_steps(31)
+    late_steps(32)
     sums[...] = small.result()
-    late_steps(32)
+    late_steps(33)
 
 
 def run_block(tokens, segment, ln_gain, ln_bias, w_qkv, b_qkv, w_out, b_out, w_up, b_up, w_down,
@@ -806,15 +841,16 @@
         V((1, 2048), F32), V((1, 2048), F32), V((1, 2048), F32),
         V((2048, 1024), BF),
         V((1024, FEAT), F32), V((1024, MID), F32),
-        V((3, 1024, 256), BF), V((3, 256, 1024), BF),
+        V((2, 1024, 256), BF), V((3, 256, 1024), BF),
         V((1024, MID), BF), V((256, 1024), BF),
-        V((1024, 256), BF), V((256, 1024), BF),
+        V((256, 1024), BF),
         V((1024, FEAT), BF),
         V((1024, 128), F32), V((1024, 128), F32),
         V((1024, 128), F32), V((8, 1024), F32),
         V((8, 1024), F32),
-        V((1024, 256), BF), V((1024, 256), F32),
-        V((256, 256), BF), V((256, 256), BF), V((1024, 256), BF),
+        V((256, 1024), F32),
+        V((256, 512), BF), V((256, 512), BF), V((1024, 512), BF),
+        V((512, 256), BF), V((512, 256), BF),
         V((128, 128), F32), V((128, 128), F32),
     ] + GradSum.scratch() + Gather.scratch() + RowSum.scratch() + SmallSum.scratch()
     return pl.pallas_call(

time: 212 us -> 199 us (0.939)
  Pallas kernels: 211 us -> 198 us
    pallas_call x1, Pallas kernels: 196 us -> 183 us  [run_block(): pl.pallas_call(block_kernel, out_shape=(jax.ShapeDtypeStruct((NP, 1024, 2...]
where the time goes in v5:
time: 199 us; the launch traced here: 198 us
  Pallas kernels  198 us (99%)
    pallas_call x1, Pallas kernels, run_block(): pl.pallas_call(block_kernel, out_shape=(jax.ShapeDtypeStruct((NP, 1024, 2...  183 us
    pallas_call x1, Pallas kernels, widen(): pl.pallas_call(widen_kernel, grid=(8,), out_shape=(shape(1024, 2048), sha...  15 us

profile of v5, /device:TPU:1, one launch (start us, length us, event | category | flops | bytes accessed | tf_op | source)
XLA Modules:
  0.0 198.4 jit_solution(3328406950067081496)
XLA Ops:
  0.6 182.5 %shard_map.220 = (bf16[24,1024,256]{2,1,0:T(8,128)(2,1)}, bf16[128,2048]{1,0:T(8,128)(2,1)}, bf16[128,2048]{1,0:T(8,128)(2,1)}, f32[8,1024]{1,0:T(8,128)}) custom-call(bf16[128,2048]{1,0:T(8,128)(2,1)} %tokens.1, bf16[128,2048]{1,0:T(8,128)(2,1)} %cotangent.1, s32[1,1024]{1,0:T(1,128)} %bitcast.13, bf16[2048]{0:T(1024)(128)(2,1)} %gain_h.1, ...), custom_call_target="tpu_custom_call" | custom-call | flops 49999998976 | bytes 31457280 | tf_op jit(solution)/shard_map/pallas_call | solution.py:856
  183.2 15.0 %shard_map.221 = (f32[1024,2048]{1,0:T(8,128)}, f32[256,2048]{1,0:T(8,128)}, f32[2048,1024]{1,0:T(8,128)}, f32[6144,256]{1,0:T(8,128)}, bf16[128,2048]{1,0:T(8,1...) custom-call(bf16[24576,256]{1,0:T(8,128)(2,1)} %bitcast.8, ...), custom_call_target="tpu_custom_call" | custom-call | tf_op jit(solution)/shard_map/pallas_call | solution.py:909

commit v6 on v5

--- a/solution.py
+++ b/solution.py
@@ -358,8 +358,7 @@
     def steps(self, t):
         for lag, step in ((2, self.add_first), (4, self.add_second), (5, self.add_third)):
             c = t - lag
-            pl.when((c >= 0) & (c < 14))(lambda step=step, c=c: step(c))
-            pl.when((c >= 16) & (c < 18))(lambda step=step, c=c - 2: step(c))
+            pl.when((c >= 0) & (c < 16))(lambda step=step, c=c: step(c))
 
 
 class SmallSum:
@@ -444,7 +443,7 @@
 
 WIDE = 14
 UNITS = ((3, (0, 2)), (3, (2, 4)), (2, (0, 2)), (2, (2, 4)), (1, (0, 4)), (0, (0, 4)))
-RS = 8
+RS = 10
 FEAT, MID = 1792, 1280
 
 
@@ -477,17 +476,17 @@
     gather = Gather(at, own_chunk, scratch[n1:n1 + n2])
 
     def keep_rows(c, value):
-        branch = (c < 6) | (c >= 14)
+        branch = (c < 4) | (c >= 12)
 
         @pl.when(branch)
         def _():
-            cols = at_rows(jnp.where(c < 6, c, c - 8))
+            cols = at_rows(jnp.where(c < 4, c, c - 8))
             own = tokens[:, cols].astype(F32) + value + b_sum[0:1, cols]
             output[:, cols] = own.astype(BF)
 
         @pl.when(jnp.logical_not(branch))
         def _():
-            grad_n[at_rows(c - 6, 128), :] = value
+            grad_n[at_rows(c - 4, 128), :] = value
 
     row_sum = RowSum(at, scratch[n1 + n2:n1 + n2 + n3], keep_rows)
 
@@ -741,12 +740,10 @@
     @pl.loop(8, 10)
     def _(t):
         grads.steps(t)
-        row_sum.steps(t - RS)
         for j in range(4):
             r = slice(j * 256, j * 256 + 256)
             grads.own[t % 2, r, :] = dot(heads_t[...], gather.all[4 * (t - 8) + j]).astype(BF)
         grads.send_piece(t)
-        branch_chunk(t, t - RS)
 
         @pl.when(t == 8)
         def _():
@@ -780,6 +777,7 @@
         row_sum.steps(t - RS)
         feature_piece(t)
         pl.when(t < 22)(lambda: normed_chunk(t, t - 14))
+        pl.when(t >= 22)(lambda: branch_chunk(t, t - 18))
 
     def late_steps(t):
         grads.steps(t)
@@ -788,7 +786,7 @@
     @pl.loop(24, 27)
     def _(t):
         late_steps(t)
-        pl.when(t < 26)(lambda: branch_chunk(t - 2, t - 18))
+        pl.when(t < 26)(lambda: branch_chunk(t, t - 18))
 
     def column_sum(value):
         return jnp.sum(value.astype(F32), axis=0, keepdims=True)
@@ -908,22 +906,22 @@
 
     down, out, up, qkv, *rest = pl.pallas_call(
         widen_kernel,
-        grid=(8,),
+        grid=(4,),
         out_shape=(
             shape(1024, 2048), shape(256, 2048), shape(2048, 1024), shape(6144, 256),
             shape(128, 2048, kind=BF), shape(128, 2048, kind=BF),
             shape(2048), shape(2048), shape(2048), shape(2048), shape(1024), shape(3, 256),
         ),
         in_specs=[
-            rows(768, 256),
-            pl.BlockSpec((8, 32, 256), lambda i: (3, i, 0)),
-            pl.BlockSpec((8, 128, 256), lambda i: (1, i, 0)),
-            pl.BlockSpec((4, 1, 256, 256), lambda i: (2, i // 4, i % 4, 0)),
-            rows(16, 2048), rows(16, 2048), whole(8, 1024),
+            rows(1536, 256),
+            pl.BlockSpec((8, 64, 256), lambda i: (3, i, 0)),
+            pl.BlockSpec((8, 256, 256), lambda i: (1, i, 0)),
+            pl.BlockSpec((4, 1, 512, 256), lambda i: (2, i // 2, i % 2, 0)),
+            rows(32, 2048), rows(32, 2048), whole(8, 1024),
         ],
         out_specs=(
-            rows(128, 2048), rows(32, 2048), rows(256, 1024), rows(768, 256),
-            rows(16, 2048), rows(16, 2048),
+            rows(256, 2048), rows(64, 2048), rows(512, 1024), rows(1536, 256),
+            rows(32, 2048), rows(32, 2048),
             whole(2048), whole(2048), whole(2048), whole(2048), whole(1024), whole(3, 256),
         ),
         compiler_params=pltpu.CompilerParams(vmem_limit_bytes=VMEM_LIMIT),

time: 199 us -> 196 us (0.985)
  Pallas kernels: 198 us -> 195 us
where the time goes in v6:
time: 196 us; the launch traced here: 195 us
  Pallas kernels  195 us (99%)
    pallas_call x1, Pallas kernels, run_block(): pl.pallas_call(block_kernel, out_shape=(jax.ShapeDtypeStruct((NP, 1024, 2...  181 us
    pallas_call x1, Pallas kernels, widen(): pl.pallas_call(widen_kernel, grid=(4,), out_shape=(shape(1024, 2048), sha...  13.3 us

profile of v6, /device:TPU:1, one launch (start us, length us, event | category | flops | bytes accessed | tf_op | source)
XLA Modules:
  0.0 195.5 jit_solution(9983072728100345205)
XLA Ops:
  0.6 181.3 %shard_map.220 = (bf16[24,1024,256]{2,1,0:T(8,128)(2,1)}, bf16[128,2048]{1,0:T(8,128)(2,1)}, bf16[128,2048]{1,0:T(8,128)(2,1)}, f32[8,1024]{1,0:T(8,128)}) custom-call(bf16[128,2048]{1,0:T(8,128)(2,1)} %tokens.1, bf16[128,2048]{1,0:T(8,128)(2,1)} %cotangent.1, s32[1,1024]{1,0:T(1,128)} %bitcast.13, bf16[2048]{0:T(1024)(128)(2,1)} %gain_h.1, ...), custom_call_target="tpu_custom_call" | custom-call | flops 49999998976 | bytes 31457280 | tf_op jit(solution)/shard_map/pallas_call | solution.py:854
  182.0 13.3 %shard_map.221 = (f32[1024,2048]{1,0:T(8,128)}, f32[256,2048]{1,0:T(8,128)}, f32[2048,1024]{1,0:T(8,128)}, f32[6144,256]{1,0:T(8,128)}, bf16[128,2048]{1,0:T(8,1...) custom-call(bf16[24576,256]{1,0:T(8,128)(2,1)} %bitcast.8, ...), custom_call_target="tpu_custom_call" | custom-call | tf_op jit(solution)/shard_map/pallas_call | solution.py:907

commit v7 on v6

--- a/solution.py
+++ b/solution.py
@@ -448,10 +448,10 @@
 
 
 def block_kernel(
-    tokens, cotangent, seg_row, gain_h, shift_h, b_qkv, b_out_h, b_up_h, b_down_h,
-    w_qkv_h, w_out_h, w_up_h, w_down_h,
-    pieces, output, input_grad, sums,
-    w_in, w_mid, w_sem,
+    seg_row, gain_h, shift_h, b_qkv, b_out_h, b_up_h, b_down_h,
+    tokens_h, cotangent_h, w_qkv_h, w_out_h, w_up_h, w_down_h,
+    pieces, output_h, input_grad_h, sums,
+    tokens, cotangent, output, input_grad, row_sem, w_in, w_mid, w_sem,
     gain, shift, b_sum,
     normed_t, pre, grad_mid, rows, turned, mid, heads_t, outs_gt, grad_feat,
     cos_t, sin_t, seg_c, seg_r, lse, out_f, q_m, g_m, ds_b, q_2, g_2, mean_row, rstd,
@@ -495,6 +495,13 @@
     moves += [(w_down_h, w_mid.at[pl.ds(0, 1024)]), (w_out_h, w_mid.at[pl.ds(1024, 256)])]
     weights = [pltpu.make_async_copy(src, dst, w_sem.at[i]) for i, (src, dst) in enumerate(moves)]
 
+    rows_in = [pltpu.make_async_copy(tokens_h, tokens, row_sem.at[0]),
+               pltpu.make_async_copy(cotangent_h, cotangent, row_sem.at[1])]
+    rows_out = [pltpu.make_async_copy(output, output_h, row_sem.at[2]),
+                pltpu.make_async_copy(input_grad, input_grad_h, row_sem.at[3])]
+    for copy in rows_in:
+        copy.start()
+
     barrier = pltpu.get_barrier_semaphore()
     greeted = small.devices()
     for device in greeted:
@@ -505,6 +512,7 @@
     gain[...] = gain_h[...].astype(F32).reshape(1, 2048)
     shift[...] = shift_h[...].astype(F32).reshape(1, 2048)
     b_sum[...] = (b_out_h[...].astype(F32) + b_down_h[...].astype(F32)).reshape(1, 2048)
+    rows_in[0].wait()
     x = tokens[...].astype(F32)
     mean = jnp.mean(x, axis=1, keepdims=True)
     centered = x - mean
@@ -512,6 +520,7 @@
     rstd[...] = jnp.broadcast_to(scale, (128, 128))
     mean_row[...] = jnp.broadcast_to(mean, (128, 128))
 
+    rows_in[1].wait()
     pl.semaphore_wait(barrier, len(greeted))
     for c in range(Gather.AHEAD):
         gather.begin(c)
@@ -532,6 +541,7 @@
         sine = jnp.sin(angle)
         cos_t[r, :] = jnp.where(lane < ROT, jnp.cos(angle), 1.0)
         sin_t[r, :] = jnp.where(lane < ROT // 2, -sine, jnp.where(lane < ROT, sine, 0.0))
+        grad_mid[r, :] = jnp.zeros((256, MID), F32)
         pre[r, 0:1024] = jnp.broadcast_to(b_up_h[...].astype(F32).reshape(1, 1024), (256, 1024))
         for k in range(3):
             cols = slice(1024 + k * 256, 1280 + k * 256)
@@ -686,10 +696,6 @@
         grads.send_piece(t)
         gather.steps(11 + t)
 
-        @pl.when(t == 0)
-        def _():
-            grad_mid[...] = jnp.zeros_like(grad_mid)
-
         @pl.loop(0, 2)
         def _(b):
             r = at_rows(b, 512)
@@ -733,7 +739,6 @@
     @pl.loop(0, 4)
     def _(b):
         r = at_rows(b)
-        mid[r, 1024:1280] = heads_t[:, r].T
         outs_gt[:, r] = grad_mid[r, 1024:1280].astype(BF).T
         pre[r, 1024:1792] = jnp.zeros((256, 768), F32)
 
@@ -750,7 +755,13 @@
             for k in range(4):
                 gelu_back(k)
 
-        pl.when(t == 9)(lambda: attend_back(*UNITS[0]))
+        @pl.when(t == 9)
+        def _():
+            attend_back(*UNITS[0])
+            for b in range(4):
+                r = slice(b * 256, b * 256 + 256)
+                mid[r, 1024:1280] = heads_t[:, r].T
+
 
     @pl.loop(10, 14)
     def _(t):
@@ -818,14 +829,18 @@
         inner = grad_n[c * 128:c * 128 + 128, :] * gain[0:1, cols] - mean_plain - unit(cols) * mean_unit
         input_grad[:, cols] = (cotangent[:, cols].astype(F32) + rstd[:, 0:1] * inner).astype(BF)
 
+    rows_out[1].start()
     late_steps(28)
     small.second()
     late_steps(29)
     late_steps(30)
+    rows_out[0].start()
     small.third()
     late_steps(31)
     late_steps(32)
     sums[...] = small.result()
+    for copy in rows_out:
+        copy.wait()
     late_steps(33)
 
 
@@ -835,6 +850,8 @@
     hbm = pl.BlockSpec(memory_space=pl.ANY)
     V = pltpu.VMEM
     scratch = [
+        V((128, 2048), BF), V((128, 2048), BF),
+        V((128, 2048), BF), V((128, 2048), BF), pltpu.SemaphoreType.DMA((4,)),
         V((2048, FEAT), BF), V((MID, 2048), BF), pltpu.SemaphoreType.DMA((6,)),
         V((1, 2048), F32), V((1, 2048), F32), V((1, 2048), F32),
         V((2048, 1024), BF),
@@ -859,15 +876,15 @@
             jax.ShapeDtypeStruct((128, 2048), BF),
             jax.ShapeDtypeStruct((8, 1024), F32),
         ),
-        in_specs=[vmem] * 9 + [hbm] * 4,
-        out_specs=(hbm, vmem, vmem, vmem),
+        in_specs=[vmem] * 7 + [hbm] * 6,
+        out_specs=(hbm, hbm, hbm, vmem),
         scratch_shapes=scratch,
         compiler_params=pltpu.CompilerParams(
             collective_id=0, has_side_effects=True, vmem_limit_bytes=VMEM_LIMIT),
         cost_estimate=pl.CostEstimate(flops=50 * 10**9, bytes_accessed=30 << 20, transcendentals=10**7),
     )(
-        tokens, cotangent, segment.reshape(1, 1024), ln_gain, ln_bias, b_qkv, b_out, b_up, b_down,
-        w_qkv.transpose(1, 0, 2), w_out, w_up, w_down,
+        segment.reshape(1, 1024), ln_gain, ln_bias, b_qkv, b_out, b_up, b_down,
+        tokens, cotangent, w_qkv.transpose(1, 0, 2), w_out, w_up, w_down,
     )
 
 

time: 196 us -> 194 us (0.990)
  Pallas kernels: 195 us -> 193 us
where the time goes in v7:
time: 194 us
  Pallas kernels  193 us (99%)
    pallas_call x1, Pallas kernels, run_block(): pl.pallas_call(block_kernel, out_shape=(jax.ShapeDtypeStruct((NP, 1024, 2...  180 us
    pallas_call x1, Pallas kernels, widen(): pl.pallas_call(widen_kernel, grid=(4,), out_shape=(shape(1024, 2048), sha...  13.3 us

profile of v7, /device:TPU:1, one launch (start us, length us, event | category | flops | bytes accessed | tf_op | source)
XLA Modules:
  0.0 194.0 jit_solution(10178567647866943815)
XLA Ops:
  0.6 179.9 %shard_map.220 = (bf16[24,1024,256]{2,1,0:T(8,128)(2,1)}, bf16[128,2048]{1,0:T(8,128)(2,1)}, bf16[128,2048]{1,0:T(8,128)(2,1)}, f32[8,1024]{1,0:T(8,128)}) custom-call(s32[1,1024]{1,0:T(1,128)} %bitcast.13, bf16[2048]{0:T(1024)(128)(2,1)} %gain_h.1, bf16[2048]{0:T(1024)(128)(2,1)} %shift_h.1, bf16[3,256]{1,0:T(4,128)(2,1)} %b_qkv.1, ...), custom_call_target="tpu_custom_call" | custom-call | flops 49999998976 | bytes 31457280 | tf_op jit(solution)/shard_map/pallas_call | solution.py:871
  180.6 13.3 %shard_map.221 = (f32[1024,2048]{1,0:T(8,128)}, f32[256,2048]{1,0:T(8,128)}, f32[2048,1024]{1,0:T(8,128)}, f32[6144,256]{1,0:T(8,128)}, bf16[128,2048]{1,0:T(8,1...) custom-call(bf16[24576,256]{1,0:T(8,128)(2,1)} %bitcast.8, ...), custom_call_target="tpu_custom_call" | custom-call | tf_op jit(solution)/shard_map/pallas_call | solution.py:924

commit v8 on v7

--- a/solution.py
+++ b/solution.py
@@ -685,8 +685,12 @@
             for k in range(2):
                 pre[pl.ds(pl.multiple_of(qb * 256 + pair * 128 + k * 64, 64), 64), 1024:1280] = grad_q[
                     k * 64:k * 64 + 64, k * 256:k * 256 + 256]
-            pre[0:n, 1536:1792] += dot(p_b[0:n, :], g_2[...])
-            pre[0:n, 1280:1536] += dot(ds_b[0:n, :], q_2[...])
+            grad_v, grad_k = dot(p_b[0:n, :], g_2[...]), dot(ds_b[0:n, :], q_2[...])
+            if (qb, heads) == UNITS[0]:
+                pre[:, 1536:1792], pre[:, 1280:1536] = grad_v, grad_k
+            else:
+                pre[0:n, 1536:1792] += grad_v
+                pre[0:n, 1280:1536] += grad_k
 
     @pl.loop(0, 8)
     def _(t):
@@ -740,7 +744,6 @@
     def _(b):
         r = at_rows(b)
         outs_gt[:, r] = grad_mid[r, 1024:1280].astype(BF).T
-        pre[r, 1024:1792] = jnp.zeros((256, 768), F32)
 
     @pl.loop(8, 10)
     def _(t):

time: 194 us -> 194 us (level)
  no operation moved by 1% of the time
where the time goes in v8:
time: 194 us
  Pallas kernels  193 us (99%)
    pallas_call x1, Pallas kernels, run_block(): pl.pallas_call(block_kernel, out_shape=(jax.ShapeDtypeStruct((NP, 1024, 2...  180 us
    pallas_call x1, Pallas kernels, widen(): pl.pallas_call(widen_kernel, grid=(4,), out_shape=(shape(1024, 2048), sha...  13.3 us

profile of v8, /device:TPU:1, one launch (start us, length us, event | category | flops | bytes accessed | tf_op | source)
XLA Modules:
  0.0 194.0 jit_solution(13034589150460521964)
XLA Ops:
  0.6 179.8 %shard_map.220 = (bf16[24,1024,256]{2,1,0:T(8,128)(2,1)}, bf16[128,2048]{1,0:T(8,128)(2,1)}, bf16[128,2048]{1,0:T(8,128)(2,1)}, f32[8,1024]{1,0:T(8,128)}) custom-call(s32[1,1024]{1,0:T(1,128)} %bitcast.13, bf16[2048]{0:T(1024)(128)(2,1)} %gain_h.1, bf16[2048]{0:T(1024)(128)(2,1)} %shift_h.1, bf16[3,256]{1,0:T(4,128)(2,1)} %b_qkv.1, ...), custom_call_target="tpu_custom_call" | custom-call | flops 49999998976 | bytes 31457280 | tf_op jit(solution)/shard_map/pallas_call | solution.py:874
  180.5 13.3 %shard_map.221 = (f32[1024,2048]{1,0:T(8,128)}, f32[256,2048]{1,0:T(8,128)}, f32[2048,1024]{1,0:T(8,128)}, f32[6144,256]{1,0:T(8,128)}, bf16[128,2048]{1,0:T(8,1...) custom-call(bf16[24576,256]{1,0:T(8,128)(2,1)} %bitcast.8, ...), custom_call_target="tpu_custom_call" | custom-call | tf_op jit(solution)/shard_map/pallas_call | solution.py:927
